TPU v7x, 32 devices: a whole 2x2x4 slice. The times are simulated.
32 devices in a mesh: seq: 8 (over z, y), ch: 4 (over x, core).
Axes of the slice: x: 2, y: 2, z: 4, core: 2. Of those that a mesh axis runs over, the one named last changes fastest.
Arguments:
- hidden_in: bfloat16 [2, 1024, 2048], P(None, 'seq'), may hold values from -6 to 6
- segments: int32 [2, 1024], P(None, 'seq'), may hold values from 1 to 2048, as said below
- cotangent: bfloat16 [2, 1024, 2048], P(None, 'seq'), may hold values from -6 to 6
- norm_gain: float32 [2, 2048], replicated, may hold values from 0.5 to 1.5
- input_projection_weight: bfloat16 [2, 2048, 2, 4096], P(None, None, None, 'ch'), may hold values from -0.125 to 0.125
- conv_weight: float32 [2, 4, 4096], P(None, None, 'ch'), may hold values from -3 to 3
- conv_bias: float32 [2, 4096], P(None, 'ch'), may hold values from -3 to 3
- proj_weight: bfloat16 [2, 4096, 160], P(None, 'ch'), may hold values from -0.1875 to 0.1875
- step_weight: bfloat16 [2, 128, 4096], P(None, None, 'ch'), may hold values from -0.5 to 0.5
- step_bias: float32 [2, 4096], P(None, 'ch'), may hold values from -4 to -1
- decay_log: float32 [2, 16, 4096], P(None, None, 'ch'), may hold values from -7 to 1.5
- skip_gain: float32 [2, 4096], P(None, 'ch'), may hold values from 0.5 to 1.5
- output_projection_weight: bfloat16 [2, 4096, 2048], P(None, 'ch'), may hold values from -0.09375 to 0.09375
Outputs:
- activations: bfloat16 [2, 1024, 2048], P(None, 'seq', 'ch')
- grad_input: float32 [2, 1024, 2048], P(None, 'seq', 'ch')
- grad_norm_gain: float32 [2, 2048], P(None, 'ch')
- grad_in_weight: float32 [2, 2048, 2, 4096], P(None, 'seq', None, 'ch')
- grad_conv_weight: float32 [2, 4, 4096], P(None, None, 'ch')
- grad_conv_bias: float32 [2, 4096], P(None, 'ch')
- grad_proj_weight: float32 [2, 4096, 160], P(None, 'ch')
- grad_step_weight: float32 [2, 128, 4096], P(None, None, 'ch')
- grad_step_bias: float32 [2, 4096], P(None, 'ch')
- grad_decay_log: float32 [2, 16, 4096], P(None, None, 'ch')
- grad_skip_gain: float32 [2, 4096], P(None, 'ch')
- grad_out_weight: float32 [2, 4096, 2048], P(None, 'ch', 'seq')
Inputs may be any that keep to these rules, and one draw needn't show every extreme that they name: `segments`: A token's document id is 1024 times its sequence's number, plus one, plus the position at which its document begins; so ids never fall along a sequence and every id of a later sequence exceeds those of earlier ones. The last token of the last sequence is a document of its own. In one of the sequences a single document begins within its first 128 tokens and lasts into its last 128 tokens.
All inputs are finite; a program needn't handle non-finite values.
Results may differ from a plain program's by a relative error of at most 0.025.
Values may be sent and summed in bfloat16 or wider, within the bound.
A program may use at most 256 MiB of HBM per device.

v0:
```python
from functools import partial

import jax
import jax.numpy as jnp
from jax import lax
from jax.sharding import PartitionSpec as P

STATE = 16
RANK = 128
KERN = 4
LAYERS = 2
SPAN = 32


epsilon = 1e-05
masked_log = -1e30


def passed_along(block, axis, distance):
    devices = range(lax.axis_size(axis))
    route = [(i - distance, i) for i in devices if i - distance in devices]
    return lax.ppermute(block, axis, route)


def prefix(shard, axis, combine, identity):
    count, here = (lax.axis_size(axis), lax.axis_index(axis))
    everything = jax.tree.map(lambda part: lax.all_gather(part, axis), shard)
    start = jax.tree.map(
        lambda part, zero: jnp.broadcast_to(jnp.asarray(zero, part.dtype), part.shape),
        shard,
        identity,
    )

    def prefix_hop(k, before):
        reached = k < here
        new = combine(before, jax.tree.map(lambda part: part[k], everything))
        return jax.tree.map(lambda a, b: jnp.where(reached, a, b), new, before)

    return lax.fori_loop(0, count, prefix_hop, start)


def entering(shard, axis, combine, identity):
    count, here = (lax.axis_size(axis), lax.axis_index(axis))
    everything = jax.tree.map(
        lambda part, kind: lax.all_gather(part.astype(kind), axis),
        shard,
        (jnp.bfloat16, jnp.bfloat16),
    )
    start = jax.tree.map(
        lambda part, zero: jnp.broadcast_to(jnp.asarray(zero, part.dtype), part.shape),
        shard,
        identity,
    )

    def entering_hop(k, before):
        at = count - 1 - k
        reached = at > here
        new = combine(
            before, jax.tree.map(lambda part, own: part[at].astype(own.dtype), everything, shard)
        )
        return jax.tree.map(lambda a, b: jnp.where(reached, a, b), new, before)

    return lax.fori_loop(0, count, entering_hop, start)


def silu_slope(argument):
    logistic = jax.nn.sigmoid(argument)
    return logistic * (1.0 + argument * (1.0 - logistic))


def conv_local(extended, weights, biases, seg_ext):
    length_now = extended.shape[1] - (KERN - 1)
    seg_now = seg_ext[:, KERN - 1 :]
    summed = biases + jnp.zeros((extended.shape[0], length_now, extended.shape[2]), jnp.float32)
    for lag_index in range(KERN):
        same_doc = (seg_ext[:, lag_index : lag_index + length_now] == seg_now).astype(jnp.float32)
        summed = (
            summed
            + weights[lag_index]
            * extended[:, lag_index : lag_index + length_now]
            * same_doc[:, :, None]
        )
    return summed


def span_update(carry, piece):
    carried, total, last_seg, first_seg, a_mat = carry
    step_size, values, input_mat, output_mat, seg_rows = piece
    span_len = step_size.shape[1]
    log_rate = step_size[:, :, :, None] * a_mat
    cumulative = jnp.cumsum(log_rate, axis=1)
    order = jnp.arange(span_len)
    lower = order[:, None] >= order[None, :]
    same_doc = (seg_rows[:, :, None] == seg_rows[:, None, :]) & lower[None]
    source = step_size * values

    def per_state(items):
        cum_slice, input_slice = items
        differ = cum_slice[:, :, None, :] - cum_slice[:, None, :, :]
        weights = jnp.exp(jnp.where(same_doc[:, :, :, None], differ, masked_log))
        weighted = source * input_slice[:, :, None]
        inner = jnp.einsum("stjc,sjc->stc", weights, weighted)
        return (inner, jnp.sum(weights[:, -1] * weighted, axis=1))

    inner_all, end_parts = lax.map(
        jax.checkpoint(per_state), (jnp.moveaxis(cumulative, 3, 0), jnp.moveaxis(input_mat, 2, 0))
    )
    outputs = jnp.sum(inner_all * jnp.moveaxis(output_mat, 2, 0)[:, :, :, None], axis=0)
    alive = seg_rows == last_seg[:, None]
    from_start = jnp.where(alive[:, :, None, None], jnp.exp(cumulative), 0.0)
    outputs = outputs + jnp.einsum("stcn,stn,scn->stc", from_start, output_mat, carried)
    carried = jnp.moveaxis(end_parts, 0, 2) + from_start[:, -1] * carried
    first_alive = seg_rows == first_seg[:, None]
    decay_rows = jnp.where(first_alive[:, :, None, None], jnp.exp(total[:, None] + cumulative), 0.0)
    total = total + cumulative[:, -1]
    return ((carried, total, seg_rows[:, -1], first_seg, a_mat), (outputs, decay_rows))


def local_states(step_size, values, input_mat, output_mat, a_mat, seg_rows, seg_prev):
    seq_count, length, channels = step_size.shape
    span_count = length // SPAN

    def arrange(array):
        return jnp.swapaxes(array.reshape((seq_count, span_count, SPAN) + array.shape[2:]), 0, 1)

    def restore(array):
        return jnp.swapaxes(array, 0, 1).reshape((seq_count, length) + array.shape[3:])

    pieces = tuple(
        (arrange(array) for array in (step_size, values, input_mat, output_mat, seg_rows))
    )
    zeros_state = jnp.zeros((seq_count, channels, STATE), jnp.float32)
    initial = (zeros_state, zeros_state, seg_prev, seg_prev, a_mat)
    final_carry, (outputs, decay_rows) = lax.scan(jax.checkpoint(span_update), initial, pieces)
    decay_map = restore(decay_rows)
    return (restore(outputs), decay_map, final_carry[0], decay_map[:, -1])


def compose(earlier, later):
    return (earlier[0] * later[0], later[0] * earlier[1] + later[1])


def local(
    hidden_in,
    segments,
    cotangent,
    norm_gain,
    input_projection_weight,
    conv_weight,
    conv_bias,
    proj_weight,
    step_weight,
    step_bias,
    decay_log,
    skip_gain,
    output_projection_weight,
):
    width = hidden_in.shape[-1]
    share_size = width // lax.axis_size("ch")
    share_start = lax.axis_index("ch") * share_size
    seg_own = segments.astype(jnp.float32)
    hidden_rows = hidden_in.astype(jnp.float32)
    stored = []
    for layer_number in range(LAYERS):
        scale_now = norm_gain[layer_number]
        inv_rms = lax.rsqrt(jnp.mean(hidden_rows * hidden_rows, axis=-1, keepdims=True) + epsilon)
        normalized_rows = (hidden_rows * inv_rms * scale_now).astype(jnp.bfloat16)
        projected_rows = jnp.einsum(
            "uaz,zfe->uafe",
            normalized_rows,
            input_projection_weight[layer_number],
            preferred_element_type=jnp.float32,
        )
        values = projected_rows[:, :, 0]
        gate_pre = projected_rows[:, :, 1]
        edge_rows, seg_edge = passed_along(
            (values[:, -(KERN - 1) :], seg_own[:, -(KERN - 1) :]), "seq", 1
        )
        extended = jnp.concatenate([edge_rows, values], axis=1)
        seg_ext = jnp.concatenate([seg_edge, seg_own], axis=1)
        conv_out, conv_pull = jax.vjp(
            partial(conv_local, seg_ext=seg_ext),
            extended,
            conv_weight[layer_number],
            conv_bias[layer_number],
        )
        activated = jax.nn.silu(conv_out)
        act_low = activated.astype(jnp.bfloat16)
        proj_part = jnp.einsum(
            "slc,cj->slj", act_low, proj_weight[layer_number], preferred_element_type=jnp.float32
        )
        proj_out = lax.psum(proj_part, "ch")
        rank_low = proj_out[:, :, :RANK].astype(jnp.bfloat16)
        input_mat = proj_out[:, :, RANK : RANK + STATE]
        output_mat = proj_out[:, :, RANK + STATE :]
        step_pre = (
            jnp.einsum(
                "slr,rc->slc",
                rank_low,
                step_weight[layer_number],
                preferred_element_type=jnp.float32,
            )
            + step_bias[layer_number]
        )
        step_size = jax.nn.softplus(step_pre)
        a_mat = -jnp.exp(decay_log[layer_number]).T
        seg_prev = seg_edge[:, -1]
        (y_zero, decay_map, end_state, end_gain), scan_pull = jax.vjp(
            partial(local_states, seg_rows=seg_own, seg_prev=seg_prev),
            step_size,
            activated,
            input_mat,
            output_mat,
            a_mat,
        )
        identity = (jnp.ones_like(end_gain), jnp.zeros_like(end_state))
        state_in = prefix((end_gain, end_state), "seq", compose, identity)[1]
        scanned = (
            y_zero
            + jnp.einsum("slcn,sln,scn->slc", decay_map, output_mat, state_in)
            + skip_gain[layer_number] * activated
        )
        gate_act = jax.nn.silu(gate_pre)
        mixer_output_reduced = (scanned * gate_act).astype(jnp.bfloat16)
        out_part = jnp.einsum(
            "uhk,kw->uhw",
            mixer_output_reduced,
            output_projection_weight[layer_number],
            preferred_element_type=jnp.float32,
        )
        branch = lax.psum(out_part, "ch")
        stored.append(
            (
                hidden_rows,
                inv_rms,
                normalized_rows,
                gate_pre,
                conv_out,
                activated,
                act_low,
                conv_pull,
                rank_low,
                step_pre,
                output_mat,
                a_mat,
                scan_pull,
                decay_map,
                state_in,
                end_gain,
                scanned,
                gate_act,
                mixer_output_reduced,
            )
        )
        hidden_rows = hidden_rows + branch
    result = lax.dynamic_slice_in_dim(hidden_rows, share_start, share_size, 2).astype(jnp.bfloat16)
    grad_rows = cotangent.astype(jnp.float32)
    collected = [None] * LAYERS
    for layer_number in reversed(range(LAYERS)):
        (
            hidden_rows,
            inv_rms,
            normalized_rows,
            gate_pre,
            conv_out,
            activated,
            act_low,
            conv_pull,
            rank_low,
            step_pre,
            output_mat,
            a_mat,
            scan_pull,
            decay_map,
            state_in,
            end_gain,
            scanned,
            gate_act,
            mixer_output_reduced,
        ) = stored[layer_number]
        output_reduced = grad_rows.astype(jnp.bfloat16)
        grad_out_weight = jnp.einsum(
            "okg,okv->gv", output_reduced, mixer_output_reduced, preferred_element_type=jnp.float32
        )
        grad_mixed = jnp.einsum(
            "urp,yp->ury",
            output_reduced,
            output_projection_weight[layer_number],
            preferred_element_type=jnp.float32,
        )
        grad_scan = grad_mixed * gate_act
        grad_gate = grad_mixed * scanned * silu_slope(gate_pre)
        grad_skip = jnp.sum(grad_scan * activated, axis=(0, 1))
        local_gain = jnp.einsum("slcn,sln,slc->scn", decay_map, output_mat, grad_scan)
        identity = (jnp.ones_like(end_gain), jnp.zeros_like(local_gain))
        grad_end = entering((end_gain, local_gain), "seq", compose, identity)[1]
        grad_decay = grad_scan[:, :, :, None] * output_mat[:, :, None, :] * state_in[:, None]
        grad_step, grad_act, grad_input_mat, grad_output_mat, grad_amat = scan_pull(
            (grad_scan, grad_decay, grad_end, grad_end * state_in)
        )
        grad_act = grad_act + grad_scan * skip_gain[layer_number]
        grad_output_mat = grad_output_mat + jnp.einsum(
            "slcn,slc,scn->sln", decay_map, grad_scan, state_in
        )
        grad_decay_log = (grad_amat * a_mat).T
        grad_pre = grad_step * jax.nn.sigmoid(step_pre)
        grad_step_bias = jnp.sum(grad_pre, axis=(0, 1))
        pre_low = grad_pre.astype(jnp.bfloat16)
        grad_step_weight = jnp.einsum(
            "slr,slc->rc", rank_low, pre_low, preferred_element_type=jnp.float32
        )
        rank_part = jnp.einsum(
            "slc,rc->slr", pre_low, step_weight[layer_number], preferred_element_type=jnp.float32
        )
        grad_rank, grad_in_sum, grad_out_sum = (
            lax.psum(rank_part.astype(jnp.bfloat16), "ch").astype(jnp.float32),
            lax.psum(grad_input_mat.astype(jnp.bfloat16), "ch").astype(jnp.float32),
            lax.psum(grad_output_mat.astype(jnp.bfloat16), "ch").astype(jnp.float32),
        )
        grad_proj = jnp.concatenate([grad_rank, grad_in_sum, grad_out_sum], axis=-1).astype(
            jnp.bfloat16
        )
        grad_proj_weight = jnp.einsum(
            "slc,slj->cj", act_low, grad_proj, preferred_element_type=jnp.float32
        )
        grad_act = grad_act + jnp.einsum(
            "slj,cj->slc", grad_proj, proj_weight[layer_number], preferred_element_type=jnp.float32
        )
        grad_conv_in, grad_conv_weight, grad_conv_bias = conv_pull(grad_act * silu_slope(conv_out))
        returned = passed_along(grad_conv_in[:, : KERN - 1], "seq", -1)
        grad_values = grad_conv_in[:, KERN - 1 :]
        grad_values = jnp.concatenate(
            [grad_values[:, : -(KERN - 1)], grad_values[:, -(KERN - 1) :] + returned], axis=1
        )
        grad_value_gate = jnp.stack([grad_values, grad_gate], axis=2).astype(jnp.bfloat16)
        grad_in_weight = jnp.einsum(
            "xpj,xpze->jze", normalized_rows, grad_value_gate, preferred_element_type=jnp.float32
        )
        grad_part = jnp.einsum(
            "fuva,jva->fuj",
            grad_value_gate,
            input_projection_weight[layer_number],
            preferred_element_type=jnp.float32,
        )
        scale_now = norm_gain[layer_number]
        inv_cubed = inv_rms * inv_rms * inv_rms
        grad_normed = lax.psum(grad_part.astype(jnp.bfloat16), "ch").astype(jnp.float32)
        inner_dot = jnp.sum(grad_normed * scale_now * hidden_rows, axis=-1, keepdims=True)
        grad_hidden = (
            inv_rms * scale_now * grad_normed - hidden_rows * inv_cubed * inner_dot / width
        )
        grad_norm_full = jnp.sum(grad_normed * hidden_rows * inv_rms, axis=(0, 1))
        grad_norm = lax.dynamic_slice_in_dim(grad_norm_full, share_start, share_size, 0)
        grad_rows = grad_rows + grad_hidden
        summed_in, summed_out = (
            lax.psum_scatter(
                grad_in_weight.astype(jnp.bfloat16), "seq", scatter_dimension=0, tiled=True
            ).astype(jnp.float32),
            lax.psum_scatter(
                grad_out_weight.astype(jnp.bfloat16), "seq", scatter_dimension=0, tiled=True
            ).astype(jnp.float32),
        )
        small_grads = (
            lax.psum(grad_norm.astype(jnp.bfloat16), "seq").astype(jnp.float32),
            lax.psum(grad_conv_weight.astype(jnp.bfloat16), "seq").astype(jnp.float32),
            lax.psum(grad_conv_bias.astype(jnp.bfloat16), "seq").astype(jnp.float32),
            lax.psum(grad_proj_weight.astype(jnp.bfloat16), "seq").astype(jnp.float32),
            lax.psum(grad_step_weight.astype(jnp.bfloat16), "seq").astype(jnp.float32),
            lax.psum(grad_step_bias.astype(jnp.bfloat16), "seq").astype(jnp.float32),
            lax.psum(grad_decay_log.astype(jnp.bfloat16), "seq").astype(jnp.float32),
            lax.psum(grad_skip.astype(jnp.bfloat16), "seq").astype(jnp.float32),
        )
        collected[layer_number] = (
            small_grads[0],
            summed_in,
            small_grads[1],
            small_grads[2],
            small_grads[3],
            small_grads[4],
            small_grads[5],
            small_grads[6],
            small_grads[7],
            summed_out.T,
        )
    grad_input = lax.dynamic_slice_in_dim(grad_rows, share_start, share_size, 2)
    stacked = [
        jnp.stack([collected[layer_number][member] for layer_number in range(LAYERS)], axis=0)
        for member in range(10)
    ]
    return (
        result,
        grad_input,
        stacked[0],
        stacked[1],
        stacked[2],
        stacked[3],
        stacked[4],
        stacked[5],
        stacked[6],
        stacked[7],
        stacked[8],
        stacked[9],
    )


def solution(mesh):
    in_specs = (
        P(None, "seq", None),
        P(None, "seq"),
        P(None, "seq", None),
        P(),
        P(None, None, None, "ch"),
        P(None, None, "ch"),
        P(None, "ch"),
        P(None, "ch", None),
        P(None, None, "ch"),
        P(None, "ch"),
        P(None, None, "ch"),
        P(None, "ch"),
        P(None, "ch", None),
    )
    out_specs = (
        P(None, "seq", "ch"),
        P(None, "seq", "ch"),
        P(None, "ch"),
        P(None, "seq", None, "ch"),
        P(None, None, "ch"),
        P(None, "ch"),
        P(None, "ch", None),
        P(None, None, "ch"),
        P(None, "ch"),
        P(None, None, "ch"),
        P(None, "ch"),
        P(None, "ch", "seq"),
    )
    return jax.shard_map(local, mesh=mesh, in_specs=in_specs, out_specs=out_specs, check_vma=False)
```

profile of v0, /device:TPU:10, one launch (start us, length us, event | category | flops | bytes accessed | tf_op | source)
XLA Modules:
  0.0 5620.2 jit_solution(3949519843686862410)
XLA Ops:
  94.9 580.6 %while.381 = (s32[]{:T(128)}, f32[2,1024,16]{1,2,0:T(8,128)S(1)}, f32[2,1024,16]{1,2,0:T(8,128)S(1)}, f32[2]{0:T(128)S(1)}, f32[4,2,32,1024]{3,2,1,0:T(8,128)}, ...) while((s32[]{:T(128)}, f32[2,1024,16]{1,2,0:T(8,128)S(1)}, ...), condition=%wide.region_8.9_spmd.clone, body=%wide.region_2.8_spmd.clone.sunk | while | flops 54824064 | bytes 56254248 | solution.py:134
  106.6 125.2 %while.394 = (s32[]{:T(128)}, f32[16,2,32,1024]{3,2,1,0:T(8,128)}, f32[16,2,1024]{2,0,1:T(8,128)S(1)}, f32[16,2,32,1024]{3,0,2,1:T(8,128)}, f32[16,2,32]{2,1,0:T...) while((s32[]{:T(128)}, f32[16,2,32,1024]{3,2,1,0:T(8,128)}, ...), condition=%wide.region_6.6_spmd.clone, body=%wide.region_4.5_spmd.clone.sunk | while | flops 12716034 | bytes 12895101 | solution.py:105
  251.7 125.2 %while.394 = (s32[]{:T(128)}, f32[16,2,32,1024]{3,2,1,0:T(8,128)}, f32[16,2,1024]{2,0,1:T(8,128)S(1)}, f32[16,2,32,1024]{3,0,2,1:T(8,128)}, f32[16,2,32]{2,1,0:T...) while((s32[]{:T(128)}, f32[16,2,32,1024]{3,2,1,0:T(8,128)}, ...), condition=%wide.region_6.6_spmd.clone, body=%wide.region_4.5_spmd.clone.sunk | while | flops 12716034 | bytes 12895101 | solution.py:105
  396.9 125.2 %while.394 = (s32[]{:T(128)}, f32[16,2,32,1024]{3,2,1,0:T(8,128)}, f32[16,2,1024]{2,0,1:T(8,128)S(1)}, f32[16,2,32,1024]{3,0,2,1:T(8,128)}, f32[16,2,32]{2,1,0:T...) while((s32[]{:T(128)}, f32[16,2,32,1024]{3,2,1,0:T(8,128)}, ...), condition=%wide.region_6.6_spmd.clone, body=%wide.region_4.5_spmd.clone.sunk | while | flops 12716034 | bytes 12895101 | solution.py:105
  542.2 125.2 %while.394 = (s32[]{:T(128)}, f32[16,2,32,1024]{3,2,1,0:T(8,128)}, f32[16,2,1024]{2,0,1:T(8,128)S(1)}, f32[16,2,32,1024]{3,0,2,1:T(8,128)}, f32[16,2,32]{2,1,0:T...) while((s32[]{:T(128)}, f32[16,2,32,1024]{3,2,1,0:T(8,128)}, ...), condition=%wide.region_6.6_spmd.clone, body=%wide.region_4.5_spmd.clone.sunk | while | flops 12716034 | bytes 12895101 | solution.py:105
  902.2 571.3 %while.384 = (s32[]{:T(128)}, f32[2,1024,16]{1,2,0:T(8,128)S(1)}, f32[2,1024,16]{1,2,0:T(8,128)S(1)}, f32[2]{0:T(128)S(1)}, f32[4,2,32,1024]{3,2,1,0:T(8,128)S(1...) while((s32[]{:T(128)}, f32[2,1024,16]{1,2,0:T(8,128)S(1)}, ...), condition=%wide.region_20.21_spmd.clone, body=%wide.region_14.20_spmd.clone.sunk | while | flops 54824064 | bytes 55729468 | solution.py:134
  912.4 125.1 %while.395 = (s32[]{:T(128)}, f32[16,2,32,1024]{3,2,1,0:T(8,128)}, f32[16,2,1024]{2,0,1:T(8,128)S(1)}, f32[16,2,32,1024]{3,0,2,1:T(8,128)}, f32[16,2,32]{2,1,0:T...) while((s32[]{:T(128)}, f32[16,2,32,1024]{3,2,1,0:T(8,128)}, ...), condition=%wide.region_18.18_spmd.clone, body=%wide.region_16.17_spmd.clone.sunk | while | flops 12716034 | bytes 12895101 | solution.py:105
  1055.3 125.1 %while.395 = (s32[]{:T(128)}, f32[16,2,32,1024]{3,2,1,0:T(8,128)}, f32[16,2,1024]{2,0,1:T(8,128)S(1)}, f32[16,2,32,1024]{3,0,2,1:T(8,128)}, f32[16,2,32]{2,1,0:T...) while((s32[]{:T(128)}, f32[16,2,32,1024]{3,2,1,0:T(8,128)}, ...), condition=%wide.region_18.18_spmd.clone, body=%wide.region_16.17_spmd.clone.sunk | while | flops 12716034 | bytes 12895101 | solution.py:105
  1198.1 125.1 %while.395 = (s32[]{:T(128)}, f32[16,2,32,1024]{3,2,1,0:T(8,128)}, f32[16,2,1024]{2,0,1:T(8,128)S(1)}, f32[16,2,32,1024]{3,0,2,1:T(8,128)}, f32[16,2,32]{2,1,0:T...) while((s32[]{:T(128)}, f32[16,2,32,1024]{3,2,1,0:T(8,128)}, ...), condition=%wide.region_18.18_spmd.clone, body=%wide.region_16.17_spmd.clone.sunk | while | flops 12716034 | bytes 12895101 | solution.py:105
  1341.0 125.1 %while.395 = (s32[]{:T(128)}, f32[16,2,32,1024]{3,2,1,0:T(8,128)}, f32[16,2,1024]{2,0,1:T(8,128)S(1)}, f32[16,2,32,1024]{3,0,2,1:T(8,128)}, f32[16,2,32]{2,1,0:T...) while((s32[]{:T(128)}, f32[16,2,32,1024]{3,2,1,0:T(8,128)}, ...), condition=%wide.region_18.18_spmd.clone, body=%wide.region_16.17_spmd.clone.sunk | while | flops 12716034 | bytes 12895101 | solution.py:105
  1641.7 1494.4 %while.389 = (s32[]{:T(128)}, f32[2,1024,16]{1,2,0:T(8,128)S(1)}, f32[2,1024,16]{1,2,0:T(8,128)}, f32[1024,16]{0,1:T(8,128)S(1)}, f32[4,2,32,1024]{3,2,1,0:T(8,1...) while((s32[]{:T(128)}, f32[2,1024,16]{1,2,0:T(8,128)S(1)}, ...), condition=%wide.region_40.41_spmd.clone, body=%wide.region_26.40_spmd.clone.sunk | while | flops 130867264 | bytes 126217648 | solution.py:134
  1752.4 251.8 %while.397 = (s32[]{:T(128)}, f32[2,32,1024]{2,1,0:T(8,128)S(1)}, f32[16,2,32,1024]{3,0,2,1:T(8,128)}, bf16[16,2,32]{2,1,0:T(2,128)(2,1)S(1)}, f32[16,2,32,1024]...) while((s32[]{:T(128)}, f32[2,32,1024]{2,1,0:T(8,128)S(1)}, ...), condition=%wide.region_33.33_spmd.clone, body=%wide.region_29.32_spmd.clone.sunk | while | flops 25694148 | bytes 16820540 | solution.py:105
  2126.0 251.8 %while.397 = (s32[]{:T(128)}, f32[2,32,1024]{2,1,0:T(8,128)S(1)}, f32[16,2,32,1024]{3,0,2,1:T(8,128)}, bf16[16,2,32]{2,1,0:T(2,128)(2,1)S(1)}, f32[16,2,32,1024]...) while((s32[]{:T(128)}, f32[2,32,1024]{2,1,0:T(8,128)S(1)}, ...), condition=%wide.region_33.33_spmd.clone, body=%wide.region_29.32_spmd.clone.sunk | while | flops 25694148 | bytes 16820540 | solution.py:105
  2499.7 251.8 %while.397 = (s32[]{:T(128)}, f32[2,32,1024]{2,1,0:T(8,128)S(1)}, f32[16,2,32,1024]{3,0,2,1:T(8,128)}, bf16[16,2,32]{2,1,0:T(2,128)(2,1)S(1)}, f32[16,2,32,1024]...) while((s32[]{:T(128)}, f32[2,32,1024]{2,1,0:T(8,128)S(1)}, ...), condition=%wide.region_33.33_spmd.clone, body=%wide.region_29.32_spmd.clone.sunk | while | flops 25694148 | bytes 16820540 | solution.py:105
  2873.4 251.8 %while.397 = (s32[]{:T(128)}, f32[2,32,1024]{2,1,0:T(8,128)S(1)}, f32[16,2,32,1024]{3,0,2,1:T(8,128)}, bf16[16,2,32]{2,1,0:T(2,128)(2,1)S(1)}, f32[16,2,32,1024]...) while((s32[]{:T(128)}, f32[2,32,1024]{2,1,0:T(8,128)S(1)}, ...), condition=%wide.region_33.33_spmd.clone, body=%wide.region_29.32_spmd.clone.sunk | while | flops 25694148 | bytes 16820540 | solution.py:105
  3300.2 1503.8 %while.393 = (s32[]{:T(128)}, f32[2,1024,16]{1,2,0:T(8,128)S(1)}, f32[2,1024,16]{1,2,0:T(8,128)}, f32[1024,16]{0,1:T(8,128)S(1)}, f32[4,2,32,1024]{3,2,1,0:T(8,1...) while((s32[]{:T(128)}, f32[2,1024,16]{1,2,0:T(8,128)S(1)}, ...), condition=%wide.region_62.63_spmd.clone, body=%wide.region_48.62_spmd.clone.sunk | while | flops 130867264 | bytes 127036952 | solution.py:134
  3414.0 251.1 %while.399 = (s32[]{:T(128)}, f32[2,32,1024]{2,1,0:T(8,128)S(1)}, f32[16,2,32,1024]{3,0,2,1:T(8,128)}, bf16[16,2,32]{2,1,0:T(2,128)(2,1)S(1)}, f32[16,2,32,1024]...) while((s32[]{:T(128)}, f32[2,32,1024]{2,1,0:T(8,128)S(1)}, ...), condition=%wide.region_55.55_spmd.clone, body=%wide.region_51.54_spmd.clone.sunk | while | flops 25694148 | bytes 16820540 | solution.py:105
  3790.0 251.1 %while.399 = (s32[]{:T(128)}, f32[2,32,1024]{2,1,0:T(8,128)S(1)}, f32[16,2,32,1024]{3,0,2,1:T(8,128)}, bf16[16,2,32]{2,1,0:T(2,128)(2,1)S(1)}, f32[16,2,32,1024]...) while((s32[]{:T(128)}, f32[2,32,1024]{2,1,0:T(8,128)S(1)}, ...), condition=%wide.region_55.55_spmd.clone, body=%wide.region_51.54_spmd.clone.sunk | while | flops 25694148 | bytes 16820540 | solution.py:105
  4166.0 251.1 %while.399 = (s32[]{:T(128)}, f32[2,32,1024]{2,1,0:T(8,128)S(1)}, f32[16,2,32,1024]{3,0,2,1:T(8,128)}, bf16[16,2,32]{2,1,0:T(2,128)(2,1)S(1)}, f32[16,2,32,1024]...) while((s32[]{:T(128)}, f32[2,32,1024]{2,1,0:T(8,128)S(1)}, ...), condition=%wide.region_55.55_spmd.clone, body=%wide.region_51.54_spmd.clone.sunk | while | flops 25694148 | bytes 16820540 | solution.py:105
  4542.1 251.1 %while.399 = (s32[]{:T(128)}, f32[2,32,1024]{2,1,0:T(8,128)S(1)}, f32[16,2,32,1024]{3,0,2,1:T(8,128)}, bf16[16,2,32]{2,1,0:T(2,128)(2,1)S(1)}, f32[16,2,32,1024]...) while((s32[]{:T(128)}, f32[2,32,1024]{2,1,0:T(8,128)S(1)}, ...), condition=%wide.region_55.55_spmd.clone, body=%wide.region_51.54_spmd.clone.sunk | while | flops 25694148 | bytes 16820540 | solution.py:105
  5124.2 87.5 %reduce-scatter.11.cloned.1.call-done = bf16[256,1024]{1,0:T(8,128)(2,1)} async-done(((bf16[2048,1024]{1,0:T(8,128)(2,1)}), bf16[256,1024]{1,0:T(8,128)(2,1)}) %reduce-scatter.11.cloned.1.call-update) | async-done | bytes 524304 | tf_op jit(solution)/shard_map/reduce_scatter | solution.py:359
  5211.7 91.8 %reduce-scatter.9.cloned.1.call-done = bf16[256,1024]{1,0:T(8,128)(2,1)} async-done(((bf16[2048,1024]{1,0:T(8,128)(2,1)}), bf16[256,1024]{1,0:T(8,128)(2,1)}) %reduce-scatter.9.cloned.1.call-update) | async-done | bytes 524304 | tf_op jit(solution)/shard_map/reduce_scatter | solution.py:359
  5306.6 147.5 %reduce-scatter.7.cloned.1.call-done = bf16[256,2,1024]{2,0,1:T(8,128)(2,1)} async-done(((bf16[2048,2,1024]{2,0,1:T(8,128)(2,1)}), bf16[256,2,1024]{2,0,1:T(8,128)(2,1)}) %reduce-scatter.7.cloned.1.call-update) | async-done | bytes 1048592 | tf_op jit(solution)/shard_map/reduce_scatter | solution.py:356
  5454.1 152.0 %reduce-scatter.5.cloned.1.call-done = bf16[256,2,1024]{2,0,1:T(8,128)(2,1)} async-done(((bf16[2048,2,1024]{2,0,1:T(8,128)(2,1)}), bf16[256,2,1024]{2,0,1:T(8,128)(2,1)}) %reduce-scatter.5.cloned.1.call-update) | async-done | bytes 1048592 | tf_op jit(solution)/shard_map/reduce_scatter | solution.py:356
  (5303 shorter events, 5725.0 us)
Async XLA Ops:
  7.2 67.0 %all-reduce.39.cloned.1.call-start = ((), (), s32[]{:S(2)}) async-start(), calls=%async_computation.4 | async-start | bytes 327680 | tf_op jit(solution)/shard_map/psum | solution.py:192
  8.0 32.3 collective-permute-start
  33.6 6.8 collective-permute-start.1
  43.2 673.3 %all-gather.15.cloned.1.call-start = ((), (), s32[]{:S(2)}) async-start(), calls=%async_computation.17 | async-start | bytes 1179648 | tf_op jit(solution)/shard_map/all_gather | solution.py:27
  676.3 82.2 %all-gather.13.cloned.1.call-start = ((), (), s32[]{:S(2)}) async-start(), calls=%async_computation.16 | async-start | bytes 1179648 | tf_op jit(solution)/shard_map/all_gather | solution.py:27
  689.5 142.8 %all-reduce.41.cloned.1.call-start = ((), (), s32[]{:S(2)}) async-start(), calls=%async_computation.5 | async-start | bytes 4194304 | tf_op jit(solution)/shard_map/psum | solution.py:231
  781.9 103.7 %all-reduce.43.cloned.1.call-start = ((), (), s32[]{:S(2)}) async-start(), calls=%async_computation.6 | async-start | bytes 327680 | tf_op jit(solution)/shard_map/psum | solution.py:192
  842.4 6.7 collective-permute-start.2
  854.8 705.2 %all-gather.19.cloned.1.call-start = ((), (), s32[]{:S(2)}) async-start(), calls=%async_computation.19 | async-start | bytes 1179648 | tf_op jit(solution)/shard_map/all_gather | solution.py:27
  1474.2 127.6 %all-gather.17.cloned.1.call-start = ((), (), s32[]{:S(2)}) async-start(), calls=%async_computation.18 | async-start | bytes 1179648 | tf_op jit(solution)/shard_map/all_gather | solution.py:27
  1558.7 1616.7 %all-reduce.47.cloned.1.call-start = ((), (), s32[]{:S(2)}) async-start(), calls=%async_computation.8 | async-start | bytes 131072 | tf_op jit(solution)/shard_map/psum | solution.py:316
  3145.4 84.6 %all-reduce.49.cloned.1.call-start = ((), (), s32[]{:S(2)}) async-start(), calls=%async_computation.9 | async-start | bytes 2097152 | tf_op jit(solution)/shard_map/psum | solution.py:347
  3182.3 6.2 collective-permute-start.3
  3193.5 1655.2 %all-reduce.51.cloned.1.call-start = ((), (), s32[]{:S(2)}) async-start(), calls=%async_computation.10 | async-start | bytes 131072 | tf_op jit(solution)/shard_map/psum | solution.py:316
  3300.2 1505.2 %copy-start.13 = (f32[2,128,1024]{2,1,0:T(8,128)S(1)}, f32[2,128,1024]{2,1,0:T(8,128)}, u32[]{:S(2)}) copy-start(f32[2,128,1024]{2,1,0:T(8,128)} %copy-done.12) | copy-start | bytes 3145732
  4814.7 85.4 %all-reduce.53.cloned.1.call-start = ((), (), s32[]{:S(2)}) async-start(), calls=%async_computation.11 | async-start | bytes 2097152 | tf_op jit(solution)/shard_map/psum | solution.py:347
  4852.6 6.2 collective-permute-start.4
  4863.6 90.9 %all-reduce.45.cloned.1.call-start = ((), (), s32[]{:S(2)}) async-start(), calls=%async_computation.7 | async-start | bytes 4194304 | tf_op jit(solution)/shard_map/psum | solution.py:231
  4869.6 165.1 %all-reduce.55.cloned.1.call-start = ((), (), s32[]{:S(2)}) async-start(), calls=%async_computation.20 | async-start | bytes 221184 | tf_op jit(solution)/shard_map/psum | solution.py:364
  4902.7 217.2 %all-reduce.57.cloned.1.call-start = ((), (), s32[]{:S(2)}) async-start(), calls=%async_computation.21 | async-start | bytes 2359296 | tf_op jit(solution)/shard_map/psum | solution.py:367
  4904.7 306.9 %reduce-scatter.11.cloned.1.call-start = ((), (), s32[]{:S(2)}) async-start(), calls=%async_computation.15 | async-start | bytes 4718592 | tf_op jit(solution)/shard_map/reduce_scatter | solution.py:359
  4909.2 394.2 %reduce-scatter.9.cloned.1.call-start = ((), (), s32[]{:S(2)}) async-start(), calls=%async_computation.14 | async-start | bytes 4718592 | tf_op jit(solution)/shard_map/reduce_scatter | solution.py:359
  4914.5 539.6 %reduce-scatter.7.cloned.1.call-start = ((), (), s32[]{:S(2)}) async-start(), calls=%async_computation.13 | async-start | bytes 9437184 | tf_op jit(solution)/shard_map/reduce_scatter | solution.py:356
  4923.2 682.9 %reduce-scatter.5.cloned.1.call-start = ((), (), s32[]{:S(2)}) async-start(), calls=%async_computation.12 | async-start | bytes 9437184 | tf_op jit(solution)/shard_map/reduce_scatter | solution.py:356
  (229 other events, 3966.2 us)
Sparse Core Ops, SparseCore 0:
  43.4 30.7 all-reduce.38
  676.4 40.1 all-gather.14
  719.5 38.8 all-gather.12
  782.0 50.2 all-reduce.40
  854.9 30.6 all-reduce.42
  1474.3 44.0 all-gather.18
  1558.8 42.9 all-gather.16
  3145.5 29.8 all-reduce.46
  3193.6 36.3 all-reduce.48
  4814.8 33.8 all-reduce.50
  4863.8 36.3 all-reduce.52
  4903.1 51.4 all-reduce.44
  4960.7 73.9 all-reduce.54
  5039.5 80.3 all-reduce.56
  5124.0 87.6 reduce-scatter.10
  5215.6 87.8 reduce-scatter.8
  5306.9 147.1 reduce-scatter.6
  5458.0 148.0 reduce-scatter.4
where the time goes:
time: 5670 us; the launch traced here: 5620 us
  local copies, waits for them, and re-layouts  2220 us (39%)
  other arithmetic  2170 us (38%)
  waiting for transfers between devices  937 us (17%)
  blocking collectives  142 us (3%)
  matrix products  94.5 us (2%)
    dynamic_update_slice x896, local copies, waits for them, and re-layouts, span_update(): lax.map(jax.checkpoint(per_state), (jnp.moveaxis(cumulative, 3, 0), jnp.m...  1060 us
    dot_general x256, other arithmetic, per_state(): inner = jnp.einsum('stjc,sjc->stc', weights, weighted)  598 us
    reduce_sum x128, other arithmetic, per_state(): differ = cum_slice[:, :, None, :] - cum_slice[:, None, :, :]  491 us
    while x264, other arithmetic  383 us
    squeeze x640, local copies, waits for them, and re-layouts, span_update(): lax.map(jax.checkpoint(per_state), (jnp.moveaxis(cumulative, 3, 0), jnp.m...  339 us
    reduce_scatter x2, waiting for transfers between devices, local(): lax.psum_scatter(grad_in_weight.astype(jnp.bfloat16), 'seq', scatter_dime...  299 us
    dynamic_slice x256, local copies, waits for them, and re-layouts, span_update(): lax.map(jax.checkpoint(per_state), (jnp.moveaxis(cumulative, 3, 0), jnp.m...  239 us
    exp x128, other arithmetic, per_state(): weights = jnp.exp(jnp.where(same_doc[:, :, :, None], differ, masked_log))  198 us

commit v1 on v0

--- a/solution.py
+++ b/solution.py
@@ -1,19 +1,315 @@
+import functools
 from functools import partial
 
 import jax
 import jax.numpy as jnp
 from jax import lax
+from jax.experimental import pallas as pl
+from jax.experimental.pallas import tpu as pltpu
 from jax.sharding import PartitionSpec as P
 
 STATE = 16
 RANK = 128
 KERN = 4
 LAYERS = 2
-SPAN = 32
 
 
 epsilon = 1e-05
-masked_log = -1e30
+LANES = 128
+BIG = 1e30
+LOG2E = 1.4426950408889634
+
+def softplus(v):
+    return jnp.maximum(v, 0.0) + jnp.log(1.0 + jnp.exp(-jnp.abs(v)))
+
+def spread_states(bc_ref, wide_ref, pick_ref, rows, unroll=8):
+    lane = lax.broadcasted_iota(jnp.int32, (STATE, 2 * STATE), 1)
+    row = lax.broadcasted_iota(jnp.int32, (STATE, 2 * STATE), 0)
+    mask = (lane % STATE == row).astype(jnp.float32)
+    src = lax.broadcasted_iota(jnp.int32, (2 * STATE, 2 * LANES), 0)
+    dst = lax.broadcasted_iota(jnp.int32, (2 * STATE, 2 * LANES), 1)
+    route = ((src // STATE) == (dst // LANES)).astype(jnp.bfloat16)
+    chunk = 32
+    def step(i, _):
+        t0 = pl.multiple_of(i * chunk, chunk)
+        bcv = bc_ref[pl.ds(t0, chunk), :]
+        for j in range(chunk):
+            pick_ref[pl.ds(j * STATE, STATE), :] = (bcv[j:j + 1] * mask).astype(jnp.bfloat16)
+        wide_ref[pl.ds(pl.multiple_of(t0 * STATE, chunk * STATE), chunk * STATE), :] = jnp.dot(pick_ref[...], route, preferred_element_type=jnp.float32)
+        return 0
+    lax.fori_loop(0, rows // chunk, step, 0)
+
+def prep(step_ref_pre, act_ref, keep_ref, dstep_ref, dx_ref, rows):
+    def body(i, _):
+        sl = pl.ds(pl.multiple_of(i * 32, 32), 32)
+        for g in range(dstep_ref.shape[0]):
+            st = softplus(step_ref_pre[sl, lanes(g)])
+            dstep_ref[g, sl, :] = jnp.where(keep_ref[sl, :] > 0.0, st, BIG)
+            dx_ref[g, sl, :] = st * act_ref[sl, lanes(g)]
+        return 0
+    lax.fori_loop(0, rows // 32, body, 0)
+
+def lanes(g):
+    return pl.ds(g * LANES, LANES)
+
+def group_sets(channels, width):
+    n = channels // LANES
+    return [list(range(i, min(i + width, n))) for i in range(0, n, width)]
+
+def local_kernel(seqs, pre_ref, act_ref, bc_ref, keep_ref, dl_ref, end_ref, gain_ref, wide, pick, dstep, dx):
+    rows, channels = pre_ref.shape
+    length = rows // seqs
+    spread_states(bc_ref, wide, pick, rows)
+    prep(pre_ref, act_ref, keep_ref, dstep, dx, rows)
+    for gs in group_sets(channels, 8):
+        a2 = [-jnp.exp(dl_ref[:, lanes(g)]) * LOG2E for g in gs]
+        for s in range(seqs):
+            for k, g in enumerate(gs):
+                tot = jnp.sum(dstep[g, pl.ds(s * length, length), :], axis=0, keepdims=True)
+                gain_ref[s, :, lanes(g)] = jnp.exp2(a2[k] * tot)
+            def blk(i, st):
+                st = list(st)
+                t0 = pl.multiple_of(s * length + i * 8, 8)
+                for j in range(8):
+                    b = wide[pl.ds(pl.multiple_of((t0 + j) * STATE, STATE), STATE), pl.ds(0, LANES)]
+                    for k, g in enumerate(gs):
+                        d = jnp.exp2(a2[k] * dstep[g, pl.ds(t0 + j, 1), :])
+                        st[k] = d * st[k] + b * dx[g, pl.ds(t0 + j, 1), :]
+                return tuple(st)
+            st = lax.fori_loop(0, length // 8, blk, tuple(jnp.zeros((STATE, LANES), jnp.float32) for _ in gs))
+            for k, g in enumerate(gs):
+                end_ref[s, :, lanes(g)] = st[k]
+
+VM = pl.BlockSpec(memory_space=pltpu.VMEM)
+
+def scan_local(pre, act, bc, keep, dl, seqs):
+    rows, channels = pre.shape
+    f = jnp.float32
+    return pl.pallas_call(
+        functools.partial(local_kernel, seqs),
+        out_shape=[jax.ShapeDtypeStruct((seqs, STATE, channels), f)] * 2,
+        in_specs=[VM] * 5, out_specs=[VM] * 2,
+        scratch_shapes=[pltpu.VMEM((rows * STATE, 2 * LANES), f), pltpu.VMEM((32 * STATE, 2 * STATE), jnp.bfloat16),
+                        pltpu.VMEM((channels // LANES, rows, LANES), f), pltpu.VMEM((channels // LANES, rows, LANES), f)],
+        compiler_params=pltpu.CompilerParams(vmem_limit_bytes=60 * 2**20),
+        name="scan_local",
+    )(pre, act, bc, keep, dl)
+
+def forward_kernel(seqs, pre_ref, act_ref, bc_ref, keep_ref, dl_ref, in_ref, y_ref, wide, pick, dstep, dx, part):
+    rows, channels = pre_ref.shape
+    length = rows // seqs
+    spread_states(bc_ref, wide, pick, rows)
+    prep(pre_ref, act_ref, keep_ref, dstep, dx, rows)
+    for gs in group_sets(channels, 4):
+        a2 = [-jnp.exp(dl_ref[:, lanes(g)]) * LOG2E for g in gs]
+        for s in range(seqs):
+            def blk(i, st):
+                st = list(st)
+                t0 = pl.multiple_of(s * length + i * 8, 8)
+                for j in range(8):
+                    at = pl.ds(pl.multiple_of((t0 + j) * STATE, STATE), STATE)
+                    b = wide[at, pl.ds(0, LANES)]
+                    c = wide[at, pl.ds(LANES, LANES)]
+                    for k, g in enumerate(gs):
+                        d = jnp.exp2(a2[k] * dstep[g, pl.ds(t0 + j, 1), :])
+                        st[k] = d * st[k] + b * dx[g, pl.ds(t0 + j, 1), :]
+                        v = st[k] * c
+                        part[k, pl.ds(pl.multiple_of(i * 64 + j * 8, 8), 8), :] = v[:8] + v[8:]
+                return tuple(st)
+            lax.fori_loop(0, length // 8, blk, tuple(in_ref[s, :, lanes(g)] for g in gs))
+            def red(i, _):
+                t0 = pl.multiple_of(s * length + i * 8, 8)
+                for k, g in enumerate(gs):
+                    acc = part[k, pl.ds(i * 64, 8, stride=8), :]
+                    for m in range(1, 8):
+                        acc = acc + part[k, pl.ds(i * 64 + m, 8, stride=8), :]
+                    y_ref[pl.ds(t0, 8), lanes(g)] = acc
+                return 0
+            lax.fori_loop(0, length // 8, red, 0)
+
+def scan_forward(pre, act, bc, keep, dl, state_in, seqs):
+    rows, channels = pre.shape
+    f = jnp.float32
+    return pl.pallas_call(
+        functools.partial(forward_kernel, seqs),
+        out_shape=jax.ShapeDtypeStruct((rows, channels), f),
+        in_specs=[VM] * 6, out_specs=VM,
+        scratch_shapes=[pltpu.VMEM((rows * STATE, 2 * LANES), f), pltpu.VMEM((32 * STATE, 2 * STATE), jnp.bfloat16),
+                        pltpu.VMEM((channels // LANES, rows, LANES), f), pltpu.VMEM((channels // LANES, rows, LANES), f),
+                        pltpu.VMEM((4, rows // seqs * 8, LANES), f)],
+        compiler_params=pltpu.CompilerParams(vmem_limit_bytes=60 * 2**20),
+        name="scan_forward",
+    )(pre, act, bc, keep, dl, state_in)
+
+LN2 = 0.6931471805599453
+
+def back_local_kernel(seqs, pre_ref, gs_ref, bc_ref, keep_ref, dl_ref, out_ref, wide, pick, dstep, gsc):
+    rows, channels = pre_ref.shape
+    length = rows // seqs
+    spread_states(bc_ref, wide, pick, rows)
+    def body(i, _):
+        sl = pl.ds(pl.multiple_of(i * 32, 32), 32)
+        for g in range(channels // LANES):
+            st = softplus(pre_ref[sl, lanes(g)])
+            dstep[g, sl, :] = jnp.where(keep_ref[sl, :] > 0.0, st, BIG)
+            gsc[g, sl, :] = gs_ref[sl, lanes(g)]
+        return 0
+    lax.fori_loop(0, rows // 32, body, 0)
+    for gs in group_sets(channels, 8):
+        a2 = [-jnp.exp(dl_ref[:, lanes(g)]) * LOG2E for g in gs]
+        for s in range(seqs):
+            def blk(i, st):
+                st = list(st)
+                t0 = pl.multiple_of(s * length + (length // 8 - 1 - i) * 8, 8)
+                for j in reversed(range(8)):
+                    c = wide[pl.ds(pl.multiple_of((t0 + j) * STATE, STATE), STATE), pl.ds(LANES, LANES)]
+                    for k, g in enumerate(gs):
+                        d = jnp.exp2(a2[k] * dstep[g, pl.ds(t0 + j, 1), :])
+                        st[k] = d * (st[k] + c * gsc[g, pl.ds(t0 + j, 1), :])
+                return tuple(st)
+            st = lax.fori_loop(0, length // 8, blk, tuple(jnp.zeros((STATE, LANES), jnp.float32) for _ in gs))
+            for k, g in enumerate(gs):
+                out_ref[s, :, lanes(g)] = st[k]
+
+def scan_back_local(pre, gs, bc, keep, dl, seqs):
+    rows, channels = pre.shape
+    f = jnp.float32
+    return pl.pallas_call(
+        functools.partial(back_local_kernel, seqs),
+        out_shape=jax.ShapeDtypeStruct((seqs, STATE, channels), f),
+        in_specs=[VM] * 5, out_specs=VM,
+        scratch_shapes=[pltpu.VMEM((rows * STATE, 2 * LANES), f), pltpu.VMEM((32 * STATE, 2 * STATE), jnp.bfloat16),
+                        pltpu.VMEM((channels // LANES, rows, LANES), f), pltpu.VMEM((channels // LANES, rows, LANES), f)],
+        compiler_params=pltpu.CompilerParams(vmem_limit_bytes=60 * 2**20),
+        name="scan_back_local",
+    )(pre, gs, bc, keep, dl)
+
+def back_kernel(seqs, pre_ref, act_ref, gs_ref, bc_ref, keep_ref, dl_ref, skip_ref, in_ref, lam_ref,
+                gpre_ref, gact_ref, gbc_ref, gdl_ref,
+                wide, pick, dstep, dx, stepc, gsc, states, partq, partr, accb, accc, rowsum):
+    rows, channels = pre_ref.shape
+    length = rows // seqs
+    f = jnp.float32
+    spread_states(bc_ref, wide, pick, rows)
+    def body(i, _):
+        sl = pl.ds(pl.multiple_of(i * 32, 32), 32)
+        for g in range(channels // LANES):
+            st = softplus(pre_ref[sl, lanes(g)])
+            stepc[g, sl, :] = st
+            dstep[g, sl, :] = jnp.where(keep_ref[sl, :] > 0.0, st, BIG)
+            dx[g, sl, :] = st * act_ref[sl, lanes(g)]
+            gsc[g, sl, :] = gs_ref[sl, lanes(g)]
+        return 0
+    lax.fori_loop(0, rows // 32, body, 0)
+    sets = group_sets(channels, 4)
+    for index, gs in enumerate(sets):
+        a2 = [-jnp.exp(dl_ref[:, lanes(g)]) * LOG2E for g in gs]
+        gdl = [jnp.zeros((STATE, LANES), f) for _ in gs]
+        for s in range(seqs):
+            for k, g in enumerate(gs):
+                states[k, pl.ds(0, STATE), :] = in_ref[s, :, lanes(g)]
+            def fwd(i, st):
+                st = list(st)
+                t0 = pl.multiple_of(s * length + i * 8, 8)
+                for j in range(8):
+                    b = wide[pl.ds(pl.multiple_of((t0 + j) * STATE, STATE), STATE), pl.ds(0, LANES)]
+                    for k, g in enumerate(gs):
+                        d = jnp.exp2(a2[k] * dstep[g, pl.ds(t0 + j, 1), :])
+                        st[k] = d * st[k] + b * dx[g, pl.ds(t0 + j, 1), :]
+                        states[k, pl.ds(pl.multiple_of((i * 8 + j + 1) * STATE, STATE), STATE), :] = st[k]
+                return tuple(st)
+            lax.fori_loop(0, length // 8, fwd, tuple(in_ref[s, :, lanes(g)] for g in gs))
+            def bwd(i, carry):
+                st = list(carry[:len(gs)])
+                am = list(carry[len(gs):])
+                l0 = (length // 8 - 1 - i) * 8
+                t0 = pl.multiple_of(s * length + l0, 8)
+                for j in reversed(range(8)):
+                    at = pl.ds(pl.multiple_of((t0 + j) * STATE, STATE), STATE)
+                    b = wide[at, pl.ds(0, LANES)]
+                    c = wide[at, pl.ds(LANES, LANES)]
+                    tb = tc = None
+                    here = pl.ds(pl.multiple_of((l0 + j) * 8, 8), 8)
+                    for k, g in enumerate(gs):
+                        row = pl.ds(t0 + j, 1)
+                        grow = gsc[g, row, :]
+                        d = jnp.exp2(a2[k] * dstep[g, row, :])
+                        lam = st[k] + c * grow
+                        old = states[k, pl.ds(pl.multiple_of((l0 + j) * STATE, STATE), STATE), :]
+                        new = states[k, pl.ds(pl.multiple_of((l0 + j + 1) * STATE, STATE), STATE), :]
+                        st[k] = d * lam
+                        lp = st[k] * old
+                        q = lam * b
+                        partq[k, here, :] = q[:8] + q[8:]
+                        r = lp * a2[k]
+                        partr[k, here, :] = r[:8] + r[8:]
+                        am[k] = am[k] + lp * stepc[g, row, :]
+                        u = lam * dx[g, row, :]
+                        v = new * grow
+                        tb = u if tb is None else tb + u
+                        tc = v if tc is None else tc + v
+                    if index > 0:
+                        tb = tb + accb[at, :]
+                        tc = tc + accc[at, :]
+                    accb[at, :] = tb
+                    accc[at, :] = tc
+                return tuple(st) + tuple(am)
+            out = lax.fori_loop(0, length // 8, bwd, tuple(lam_ref[s, :, lanes(g)] for g in gs) + tuple(gdl))
+            gdl = list(out[len(gs):])
+            def red(i, _):
+                t0 = pl.multiple_of(s * length + i * 8, 8)
+                for k, g in enumerate(gs):
+                    q = partq[k, pl.ds(i * 64, 8, stride=8), :]
+                    r = partr[k, pl.ds(i * 64, 8, stride=8), :]
+                    for m in range(1, 8):
+                        q = q + partq[k, pl.ds(i * 64 + m, 8, stride=8), :]
+                        r = r + partr[k, pl.ds(i * 64 + m, 8, stride=8), :]
+                    here = pl.ds(t0, 8)
+                    p = pre_ref[here, lanes(g)]
+                    gstep = r * LN2 + act_ref[here, lanes(g)] * q
+                    gpre_ref[here, lanes(g)] = gstep * (1.0 / (1.0 + jnp.exp(-p)))
+                    gact_ref[here, lanes(g)] = stepc[g, here, :] * q + gsc[g, here, :] * skip_ref[:, lanes(g)]
+                return 0
+            lax.fori_loop(0, length // 8, red, 0)
+        for k, g in enumerate(gs):
+            gdl_ref[:, lanes(g)] = gdl[k] * (a2[k] * LN2)
+    ones = jnp.ones((LANES, LANES), jnp.bfloat16)
+    lane = lax.broadcasted_iota(jnp.int32, (32 * STATE, LANES), 1)
+    row = lax.broadcasted_iota(jnp.int32, (32 * STATE, LANES), 0) % STATE
+    mb = lane == row
+    mc = lane == row + STATE
+    def fin(i, _):
+        sl = pl.ds(pl.multiple_of(i * 32 * STATE, 32 * STATE), 32 * STATE)
+        sb = jnp.dot(accb[sl, :].astype(jnp.bfloat16), ones, preferred_element_type=f)
+        sc = jnp.dot(accc[sl, :].astype(jnp.bfloat16), ones, preferred_element_type=f)
+        rowsum[...] = jnp.where(mb, sb, jnp.where(mc, sc, 0.0))
+        acc = rowsum[pl.ds(0, 32, stride=STATE), :]
+        for m in range(1, STATE):
+            acc = acc + rowsum[pl.ds(m, 32, stride=STATE), :]
+        gbc_ref[pl.ds(pl.multiple_of(i * 32, 32), 32), :] = acc
+        return 0
+    lax.fori_loop(0, rows // 32, fin, 0)
+
+def scan_back(pre, act, gs, bc, keep, dl, skip, state_in, lam_in, seqs):
+    rows, channels = pre.shape
+    f = jnp.float32
+    groups = channels // LANES
+    length = rows // seqs
+    big = pltpu.VMEM((groups, rows, LANES), f)
+    return pl.pallas_call(
+        functools.partial(back_kernel, seqs),
+        out_shape=[jax.ShapeDtypeStruct((rows, channels), f), jax.ShapeDtypeStruct((rows, channels), f),
+                   jax.ShapeDtypeStruct((rows, LANES), f), jax.ShapeDtypeStruct((STATE, channels), f)],
+        in_specs=[VM] * 9, out_specs=[VM] * 4,
+        scratch_shapes=[pltpu.VMEM((rows * STATE, 2 * LANES), f), pltpu.VMEM((32 * STATE, 2 * STATE), jnp.bfloat16),
+                        big, big, big, big,
+                        pltpu.VMEM((4, (length + 1) * STATE, LANES), f),
+                        pltpu.VMEM((4, length * 8, LANES), f), pltpu.VMEM((4, length * 8, LANES), f),
+                        pltpu.VMEM((rows * STATE, LANES), f), pltpu.VMEM((rows * STATE, LANES), f),
+                        pltpu.VMEM((32 * STATE, LANES), f)],
+        compiler_params=pltpu.CompilerParams(vmem_limit_bytes=60 * 2**20),
+        name="scan_back",
+    )(pre, act, gs, bc, keep, dl, skip, state_in, lam_in)
 
 
 def passed_along(block, axis, distance):
@@ -24,7 +320,9 @@
 
 def prefix(shard, axis, combine, identity):
     count, here = (lax.axis_size(axis), lax.axis_index(axis))
-    everything = jax.tree.map(lambda part: lax.all_gather(part, axis), shard)
+    everything = jax.tree.map(
+        lambda part: lax.all_gather(part.astype(jnp.bfloat16), axis).astype(part.dtype), shard
+    )
     start = jax.tree.map(
         lambda part, zero: jnp.broadcast_to(jnp.asarray(zero, part.dtype), part.shape),
         shard,
@@ -81,59 +379,6 @@
             * same_doc[:, :, None]
         )
     return summed
-
-
-def span_update(carry, piece):
-    carried, total, last_seg, first_seg, a_mat = carry
-    step_size, values, input_mat, output_mat, seg_rows = piece
-    span_len = step_size.shape[1]
-    log_rate = step_size[:, :, :, None] * a_mat
-    cumulative = jnp.cumsum(log_rate, axis=1)
-    order = jnp.arange(span_len)
-    lower = order[:, None] >= order[None, :]
-    same_doc = (seg_rows[:, :, None] == seg_rows[:, None, :]) & lower[None]
-    source = step_size * values
-
-    def per_state(items):
-        cum_slice, input_slice = items
-        differ = cum_slice[:, :, None, :] - cum_slice[:, None, :, :]
-        weights = jnp.exp(jnp.where(same_doc[:, :, :, None], differ, masked_log))
-        weighted = source * input_slice[:, :, None]
-        inner = jnp.einsum("stjc,sjc->stc", weights, weighted)
-        return (inner, jnp.sum(weights[:, -1] * weighted, axis=1))
-
-    inner_all, end_parts = lax.map(
-        jax.checkpoint(per_state), (jnp.moveaxis(cumulative, 3, 0), jnp.moveaxis(input_mat, 2, 0))
-    )
-    outputs = jnp.sum(inner_all * jnp.moveaxis(output_mat, 2, 0)[:, :, :, None], axis=0)
-    alive = seg_rows == last_seg[:, None]
-    from_start = jnp.where(alive[:, :, None, None], jnp.exp(cumulative), 0.0)
-    outputs = outputs + jnp.einsum("stcn,stn,scn->stc", from_start, output_mat, carried)
-    carried = jnp.moveaxis(end_parts, 0, 2) + from_start[:, -1] * carried
-    first_alive = seg_rows == first_seg[:, None]
-    decay_rows = jnp.where(first_alive[:, :, None, None], jnp.exp(total[:, None] + cumulative), 0.0)
-    total = total + cumulative[:, -1]
-    return ((carried, total, seg_rows[:, -1], first_seg, a_mat), (outputs, decay_rows))
-
-
-def local_states(step_size, values, input_mat, output_mat, a_mat, seg_rows, seg_prev):
-    seq_count, length, channels = step_size.shape
-    span_count = length // SPAN
-
-    def arrange(array):
-        return jnp.swapaxes(array.reshape((seq_count, span_count, SPAN) + array.shape[2:]), 0, 1)
-
-    def restore(array):
-        return jnp.swapaxes(array, 0, 1).reshape((seq_count, length) + array.shape[3:])
-
-    pieces = tuple(
-        (arrange(array) for array in (step_size, values, input_mat, output_mat, seg_rows))
-    )
-    zeros_state = jnp.zeros((seq_count, channels, STATE), jnp.float32)
-    initial = (zeros_state, zeros_state, seg_prev, seg_prev, a_mat)
-    final_carry, (outputs, decay_rows) = lax.scan(jax.checkpoint(span_update), initial, pieces)
-    decay_map = restore(decay_rows)
-    return (restore(outputs), decay_map, final_carry[0], decay_map[:, -1])
 
 
 def compose(earlier, later):
@@ -191,8 +436,6 @@
         )
         proj_out = lax.psum(proj_part, "ch")
         rank_low = proj_out[:, :, :RANK].astype(jnp.bfloat16)
-        input_mat = proj_out[:, :, RANK : RANK + STATE]
-        output_mat = proj_out[:, :, RANK + STATE :]
         step_pre = (
             jnp.einsum(
                 "slr,rc->slc",
@@ -202,24 +445,21 @@
             )
             + step_bias[layer_number]
         )
-        step_size = jax.nn.softplus(step_pre)
-        a_mat = -jnp.exp(decay_log[layer_number]).T
-        seg_prev = seg_edge[:, -1]
-        (y_zero, decay_map, end_state, end_gain), scan_pull = jax.vjp(
-            partial(local_states, seg_rows=seg_own, seg_prev=seg_prev),
-            step_size,
-            activated,
-            input_mat,
-            output_mat,
-            a_mat,
+        shape = step_pre.shape
+        seqs, channels = shape[0], shape[-1]
+        flat = lambda v: v.reshape(-1, v.shape[-1])
+        rates = decay_log[layer_number]
+        mats = flat(proj_out[:, :, RANK:])
+        keep = (seg_ext[:, KERN - 2 : -1] == seg_own).astype(jnp.float32).reshape(-1, 1)
+        end_state, end_gain = scan_local(
+            flat(step_pre), flat(activated), mats, keep, rates, seqs
         )
         identity = (jnp.ones_like(end_gain), jnp.zeros_like(end_state))
         state_in = prefix((end_gain, end_state), "seq", compose, identity)[1]
-        scanned = (
-            y_zero
-            + jnp.einsum("slcn,sln,scn->slc", decay_map, output_mat, state_in)
-            + skip_gain[layer_number] * activated
-        )
+        y = scan_forward(
+            flat(step_pre), flat(activated), mats, keep, rates, state_in, seqs
+        ).reshape(shape)
+        scanned = y + skip_gain[layer_number] * activated
         gate_act = jax.nn.silu(gate_pre)
         mixer_output_reduced = (scanned * gate_act).astype(jnp.bfloat16)
         out_part = jnp.einsum(
@@ -241,10 +481,8 @@
                 conv_pull,
                 rank_low,
                 step_pre,
-                output_mat,
-                a_mat,
-                scan_pull,
-                decay_map,
+                mats,
+                keep,
                 state_in,
                 end_gain,
                 scanned,
@@ -268,10 +506,8 @@
             conv_pull,
             rank_low,
             step_pre,
-            output_mat,
-            a_mat,
-            scan_pull,
-            decay_map,
+            mats,
+            keep,
             state_in,
             end_gain,
             scanned,
@@ -291,19 +527,25 @@
         grad_scan = grad_mixed * gate_act
         grad_gate = grad_mixed * scanned * silu_slope(gate_pre)
         grad_skip = jnp.sum(grad_scan * activated, axis=(0, 1))
-        local_gain = jnp.einsum("slcn,sln,slc->scn", decay_map, output_mat, grad_scan)
+        rates = decay_log[layer_number]
+        local_gain = scan_back_local(flat(step_pre), flat(grad_scan), mats, keep, rates, seqs)
         identity = (jnp.ones_like(end_gain), jnp.zeros_like(local_gain))
         grad_end = entering((end_gain, local_gain), "seq", compose, identity)[1]
-        grad_decay = grad_scan[:, :, :, None] * output_mat[:, :, None, :] * state_in[:, None]
-        grad_step, grad_act, grad_input_mat, grad_output_mat, grad_amat = scan_pull(
-            (grad_scan, grad_decay, grad_end, grad_end * state_in)
-        )
-        grad_act = grad_act + grad_scan * skip_gain[layer_number]
-        grad_output_mat = grad_output_mat + jnp.einsum(
-            "slcn,slc,scn->sln", decay_map, grad_scan, state_in
-        )
-        grad_decay_log = (grad_amat * a_mat).T
-        grad_pre = grad_step * jax.nn.sigmoid(step_pre)
+        grad_pre, grad_act, grad_mats, grad_decay_log = scan_back(
+            flat(step_pre),
+            flat(activated),
+            flat(grad_scan),
+            mats,
+            keep,
+            rates,
+            skip_gain[layer_number][None],
+            state_in,
+            grad_end,
+            seqs,
+        )
+        grad_pre = grad_pre.reshape(shape)
+        grad_act = grad_act.reshape(shape)
+        grad_mats = grad_mats[:, : 2 * STATE].reshape(shape[:2] + (2 * STATE,))
         grad_step_bias = jnp.sum(grad_pre, axis=(0, 1))
         pre_low = grad_pre.astype(jnp.bfloat16)
         grad_step_weight = jnp.einsum(
@@ -312,14 +554,9 @@
         rank_part = jnp.einsum(
             "slc,rc->slr", pre_low, step_weight[layer_number], preferred_element_type=jnp.float32
         )
-        grad_rank, grad_in_sum, grad_out_sum = (
-            lax.psum(rank_part.astype(jnp.bfloat16), "ch").astype(jnp.float32),
-            lax.psum(grad_input_mat.astype(jnp.bfloat16), "ch").astype(jnp.float32),
-            lax.psum(grad_output_mat.astype(jnp.bfloat16), "ch").astype(jnp.float32),
-        )
-        grad_proj = jnp.concatenate([grad_rank, grad_in_sum, grad_out_sum], axis=-1).astype(
-            jnp.bfloat16
-        )
+        grad_proj = lax.psum(
+            jnp.concatenate([rank_part, grad_mats], axis=-1).astype(jnp.bfloat16), "ch"
+        ).astype(jnp.bfloat16)
         grad_proj_weight = jnp.einsum(
             "slc,slj->cj", act_low, grad_proj, preferred_element_type=jnp.float32
         )

time: 5670 us -> 1410 us (0.25)
  local copies, waits for them, and re-layouts: 2220 us -> 46.3 us
  other arithmetic: 2170 us -> 73.4 us
  Pallas kernels: 0 us -> 99.5 us
    dynamic_update_slice x928 -> x0, local copies, waits for them, and re-layouts: 1080 us -> none  [the longest x896 1060 us: span_update(): lax.map(jax.checkpoint(per_state), (jnp.moveaxis(cumulative, 3, 0), jnp.m...]
    dot_general x270 -> x0, other arithmetic: 645 us -> none  [the longest x256 598 us: per_state(): inner = jnp.einsum('stjc,sjc->stc', weights, weighted)]
    reduce_sum x409 -> x1, other arithmetic: 615 us -> 2.81 us  [conv_local(): biases + jnp.zeros((extended.shape[0], length_now, extended.shape[2]), jn...]
    squeeze x712 -> x1, local copies, waits for them, and re-layouts: 423 us -> 0.65 us  [local(): rates = decay_log[layer_number]]
    while x264 -> x0, other arithmetic: 383 us -> none
    dynamic_slice x256 -> x0, local copies, waits for them, and re-layouts: 239 us -> none  [span_update(): lax.map(jax.checkpoint(per_state), (jnp.moveaxis(cumulative, 3, 0), jnp.m...]
    exp x128 -> x0, other arithmetic: 198 us -> none  [per_state(): weights = jnp.exp(jnp.where(same_doc[:, :, :, None], differ, masked_log))]
    sub x128 -> x0, local copies, waits for them, and re-layouts: 125 us -> none  [per_state(): differ = cum_slice[:, :, None, :] - cum_slice[:, None, :, :]]
where the time goes in v1:
time: 1410 us; the launch traced here: 1400 us
  waiting for transfers between devices  885 us (63%)
  blocking collectives  180 us (13%)
  Pallas kernels  99.5 us (7%)
  matrix products  79.1 us (6%)
  other arithmetic  73.4 us (5%)
  local copies, waits for them, and re-layouts  46.3 us (3%)
  starting transfers between devices  19.7 us (1%)
  between operations  15.9 us (1%)
    reduce_scatter x2, waiting for transfers between devices, local(): lax.psum_scatter(grad_in_weight.astype(jnp.bfloat16), 'seq', scatter_dime...  300 us
    reduce_scatter x2, waiting for transfers between devices, local(): lax.psum_scatter(grad_out_weight.astype(jnp.bfloat16), 'seq', scatter_dim...  179 us
    all_gather x4, blocking collectives, prefix(): lax.all_gather(part.astype(jnp.bfloat16), axis).astype(part.dtype)  122 us
    psum x1, waiting for transfers between devices, local(): lax.psum(grad_proj_weight.astype(jnp.bfloat16), 'seq').astype(jnp.float32)  78.5 us
    psum x2, waiting for transfers between devices, local(): branch = lax.psum(out_part, 'ch')  76.6 us
    psum x1, waiting for transfers between devices, local(): lax.psum(grad_norm.astype(jnp.bfloat16), 'seq').astype(jnp.float32)  74.7 us
    psum x2, waiting for transfers between devices, local(): proj_out = lax.psum(proj_part, 'ch')  60.2 us
    all_gather x2, blocking collectives, entering(): lax.all_gather(part.astype(kind), axis)  57.3 us
  transfers between devices with their start and end apart: 19, of which 17 were waited for; matrix products, arithmetic and copies ran while one was open for 5% of the time, Pallas kernels for 1%

profile of v1, /device:TPU:10, one launch (start us, length us, event | category | flops | bytes accessed | tf_op | source)
XLA Modules:
  0.0 1399.0 jit_solution(9104430926339071805)
XLA Ops:
  10.2 14.0 %fusion.122 = (bf16[1,2048,2,1024]{3,2,1,0:T(2,128)(2,1)S(1)}, bf16[1,2048,2,1024]{3,2,1,0:T(2,128)(2,1)}) fusion(bf16[2,2048,2,1024]{3,2,1,0:T(2,128)(2,1)} %param.25), kind=kLoop, calls=%fused_computation.240 | loop fusion | bytes 33554432 | tf_op jit(solution)/shard_map/slice | solution.py:416
  42.4 29.5 %all-reduce.29.cloned.1.call-done = f32[2,128,160]{1,2,0:T(8,128)} async-done(((f32[2,128,160]{1,2,0:T(8,128)}), f32[2,128,160]{1,2,0:T(8,128)}) %all-reduce.29.cloned.1.call-update) | async-done | bytes 163856 | tf_op jit(solution)/shard_map/psum | solution.py:437
  84.4 28.8 %all-gather = bf16[16,16,1024]{2,1,0:T(8,128)(2,1)S(1)} all-gather(bf16[2,16,1024]{2,1,0:T(8,128)(2,1)S(1)} %convert_element_type.259), channel_id=2, replica_groups=mesh['seq'=8,'ch'=4] {'seq'}, dimensions={0}, use_global_device_ids=true | all-gather | bytes 589824 | tf_op jit(solution)/shard_map/all_gather | solution.py:324
  114.2 31.2 %all-gather.1 = bf16[16,16,1024]{2,1,0:T(8,128)(2,1)S(1)} all-gather(bf16[2,16,1024]{2,1,0:T(8,128)(2,1)S(1)} %convert_element_type.261), channel_id=3, replica_groups=mesh['seq'=8,'ch'=4] {'seq'}, dimensions={0}, use_global_device_ids=true | all-gather | bytes 589824 | tf_op jit(solution)/shard_map/all_gather | solution.py:324
  146.3 11.2 scan_forward.2
  165.5 53.9 %all-reduce.31.cloned.1.call-done = f32[2,128,2048]{2,1,0:T(8,128)} async-done(((f32[2,128,2048]{2,1,0:T(8,128)}), f32[2,128,2048]{2,1,0:T(8,128)}) %all-reduce.31.cloned.1.call-update) | async-done | bytes 2097168 | tf_op jit(solution)/shard_map/psum | solution.py:471
  241.5 30.7 %all-reduce.33.cloned.1.call-done = f32[2,128,160]{1,2,0:T(8,128)} async-done(((f32[2,128,160]{1,2,0:T(8,128)}), f32[2,128,160]{1,2,0:T(8,128)}) %all-reduce.33.cloned.1.call-update) | async-done | bytes 163856 | tf_op jit(solution)/shard_map/psum | solution.py:437
  286.1 28.6 %all-gather.4 = bf16[16,16,1024]{2,1,0:T(8,128)(2,1)S(1)} all-gather(bf16[2,16,1024]{2,1,0:T(8,128)(2,1)S(1)} %convert_element_type.273), channel_id=6, replica_groups=mesh['seq'=8,'ch'=4] {'seq'}, dimensions={0}, use_global_device_ids=true | all-gather | bytes 589824 | tf_op jit(solution)/shard_map/all_gather | solution.py:343
  323.5 31.5 %all-gather.2 = bf16[16,16,1024]{2,1,0:T(8,128)(2,1)S(1)} all-gather(bf16[2,16,1024]{2,1,0:T(8,128)(2,1)S(1)} %convert_element_type.266), channel_id=4, replica_groups=mesh['seq'=8,'ch'=4] {'seq'}, dimensions={0}, use_global_device_ids=true | all-gather | bytes 589824 | tf_op jit(solution)/shard_map/all_gather | solution.py:324
  357.8 31.0 %all-gather.3 = bf16[16,16,1024]{2,1,0:T(8,128)(2,1)S(1)} all-gather(bf16[2,16,1024]{2,1,0:T(8,128)(2,1)S(1)} %convert_element_type.268), channel_id=5, replica_groups=mesh['seq'=8,'ch'=4] {'seq'}, dimensions={0}, use_global_device_ids=true | all-gather | bytes 589824 | tf_op jit(solution)/shard_map/all_gather | solution.py:324
  397.1 23.0 %scan_back.2 = (f32[256,1024]{1,0:T(8,128)}, f32[256,1024]{1,0:T(8,128)}, f32[256,128]{1,0:T(8,128)}, f32[16,1024]{1,0:T(8,128)}) custom-call(f32[256,1024]{1,0:T(8,128)} %bitcast.319, f32[256,1024]{1,0:T(8,128)} %bitcast.311, f32[256,1024]{1,0:T(8,128)} %bitcast.326, f32[256,32]{1,0:T(8,128)} %bitcast.340, f32[256,1]{1,0:T(8,128)} %copy.78.keep_ref, ...), custom_call_target="tpu_custom_call" | custom-call | tf_op jit(solution)/shard_map/scan_back/pallas_call | solution.py:299
  435.5 23.2 %all-reduce.37.cloned.1.call-done = bf16[2,128,160]{1,2,0:T(8,128)(2,1)} async-done(((bf16[2,128,160]{1,2,0:T(8,128)(2,1)}), bf16[2,128,160]{1,2,0:T(8,128)(2,1)}) %all-reduce.37.cloned.1.call-update) | async-done | bytes 81936 | tf_op jit(solution)/shard_map/psum | solution.py:557
  475.3 35.0 %all-reduce.39.cloned.1.call-done = bf16[2,128,2048]{2,1,0:T(8,128)(2,1)} async-done(((bf16[2,128,2048]{2,1,0:T(8,128)(2,1)}), bf16[2,128,2048]{2,1,0:T(8,128)(2,1)}) %all-reduce.39.cloned.1.call-update) | async-done | bytes 1048592 | tf_op jit(solution)/shard_map/psum | solution.py:584
  529.6 28.7 %all-gather.5 = bf16[16,16,1024]{2,1,0:T(8,128)(2,1)S(1)} all-gather(bf16[2,16,1024]{2,1,0:T(8,128)(2,1)S(1)} %convert_element_type.279), channel_id=7, replica_groups=mesh['seq'=8,'ch'=4] {'seq'}, dimensions={0}, use_global_device_ids=true | all-gather | bytes 589824 | tf_op jit(solution)/shard_map/all_gather | solution.py:343
  566.0 23.0 %scan_back.3 = (f32[256,1024]{1,0:T(8,128)}, f32[256,1024]{1,0:T(8,128)}, f32[256,128]{1,0:T(8,128)}, f32[16,1024]{1,0:T(8,128)}) custom-call(f32[256,1024]{1,0:T(8,128)} %bitcast.316, f32[256,1024]{1,0:T(8,128)} %bitcast.309, f32[256,1024]{1,0:T(8,128)} %bitcast.328, f32[256,32]{1,0:T(8,128)} %bitcast.337, f32[256,1]{1,0:T(8,128)} %copy.78.keep_ref, ...), custom_call_target="tpu_custom_call" | custom-call | tf_op jit(solution)/shard_map/scan_back/pallas_call | solution.py:299
  595.4 32.2 %all-reduce.41.cloned.1.call-done = bf16[2,128,160]{1,2,0:T(8,128)(2,1)} async-done(((bf16[2,128,160]{1,2,0:T(8,128)(2,1)}), bf16[2,128,160]{1,2,0:T(8,128)(2,1)}) %all-reduce.41.cloned.1.call-update) | async-done | bytes 81936 | tf_op jit(solution)/shard_map/psum | solution.py:557
  658.9 19.6 %all-reduce.43.cloned.1.call-done = bf16[2,128,2048]{2,1,0:T(8,128)(2,1)} async-done(((bf16[2,128,2048]{2,1,0:T(8,128)(2,1)}), bf16[2,128,2048]{2,1,0:T(8,128)(2,1)}) %all-reduce.43.cloned.1.call-update) | async-done | bytes 1048592 | tf_op jit(solution)/shard_map/psum | solution.py:584
  710.5 22.6 %all-reduce.35.cloned.1.call-done = f32[2,128,2048]{2,1,0:T(8,128)} async-done(((f32[2,128,2048]{2,1,0:T(8,128)}), f32[2,128,2048]{2,1,0:T(8,128)}) %all-reduce.35.cloned.1.call-update) | async-done | bytes 2097168 | tf_op jit(solution)/shard_map/psum | solution.py:471
  738.6 74.7 %all-reduce.45.cloned.1.call-done = (bf16[1,512]{1,0:T(2,128)(2,1)}, bf16[1,512]{1,0:T(2,128)(2,1)}, bf16[1,4,1024]{2,1,0:T(4,128)(2,1)}, bf16[1,4,1024]{2,1,0:T...) async-done(((bf16[1,512]{1,0:T(2,128)(2,1)}, ...) | async-done | bytes 96272 | tf_op jit(solution)/shard_map/psum | solution.py:601
  820.0 78.5 %all-reduce.47.cloned.1.call-done = (bf16[1,1024,160]{1,2,0:T(8,128)(2,1)}, bf16[1,1024,160]{1,2,0:T(8,128)(2,1)}, bf16[1,128,1024]{2,1,0:T(8,128)(2,1)}, bf16[1,128,1024]{2,1,0:T(8,128)(2,1)}) async-done(((bf16[1,1024,160]{1,2,0:T(8,128)(2,1)}, bf16[1,1024,160]{1,2,0:T(8,128)(2,1)}, bf16[1,128,1024]{2,1,0:T(8,128)(2,1)}, bf16[1,128,1024]{2,1,0:T(8,128)(2,1)}), (bf16[1,1024,160]{1,2,0:T(8,128)(2,1)}, ...) | async-done | bytes 1179664 | tf_op jit(solution)/shard_map/psum | solution.py:604
  902.7 87.7 %reduce-scatter.11.cloned.1.call-done = bf16[256,1024]{1,0:T(8,128)(2,1)} async-done(((bf16[2048,1024]{1,0:T(8,128)(2,1)}), bf16[256,1024]{1,0:T(8,128)(2,1)}) %reduce-scatter.11.cloned.1.call-update) | async-done | bytes 524304 | tf_op jit(solution)/shard_map/reduce_scatter | solution.py:596
  990.4 91.8 %reduce-scatter.9.cloned.1.call-done = bf16[256,1024]{1,0:T(8,128)(2,1)} async-done(((bf16[2048,1024]{1,0:T(8,128)(2,1)}), bf16[256,1024]{1,0:T(8,128)(2,1)}) %reduce-scatter.9.cloned.1.call-update) | async-done | bytes 524304 | tf_op jit(solution)/shard_map/reduce_scatter | solution.py:596
  1085.3 147.6 %reduce-scatter.7.cloned.1.call-done = bf16[256,2,1024]{2,0,1:T(8,128)(2,1)} async-done(((bf16[2048,2,1024]{2,0,1:T(8,128)(2,1)}), bf16[256,2,1024]{2,0,1:T(8,128)(2,1)}) %reduce-scatter.7.cloned.1.call-update) | async-done | bytes 1048592 | tf_op jit(solution)/shard_map/reduce_scatter | solution.py:593
  1233.0 152.0 %reduce-scatter.5.cloned.1.call-done = bf16[256,2,1024]{2,0,1:T(8,128)(2,1)} async-done(((bf16[2048,2,1024]{2,0,1:T(8,128)(2,1)}), bf16[256,2,1024]{2,0,1:T(8,128)(2,1)}) %reduce-scatter.5.cloned.1.call-update) | async-done | bytes 1048592 | tf_op jit(solution)/shard_map/reduce_scatter | solution.py:593
  (433 shorter events, 269.8 us)
Async XLA Ops:
  7.2 64.7 %all-reduce.29.cloned.1.call-start = ((), (), s32[]{:S(2)}) async-start(), calls=%async_computation.4 | async-start | bytes 327680 | tf_op jit(solution)/shard_map/psum | solution.py:437
  8.0 214.1 %copy-start.57 = (f32[1,2048]{1,0:T(1,128)}, f32[1,2048]{1,0:T(1,128)S(1)}, u32[]{:S(2)}) copy-start(f32[1,2048]{1,0:T(1,128)S(1)} %get-tuple-element.713) | copy-start | bytes 24580
  27.7 10.2 collective-permute-start
  31.4 6.3 collective-permute-start.1
  40.9 178.5 %all-reduce.31.cloned.1.call-start = ((), (), s32[]{:S(2)}) async-start(), calls=%async_computation.5 | async-start | bytes 4194304 | tf_op jit(solution)/shard_map/psum | solution.py:471
  41.6 473.0 %copy-start.49 = (f32[1,1024]{1,0:T(1,128)}, f32[1,1024]{1,0:T(1,128)S(1)}, u32[]{:S(2)}) copy-start(f32[1,1024]{1,0:T(1,128)S(1)} %get-tuple-element.716.skip_ref) | copy-start | bytes 12292
  165.0 107.2 %all-reduce.33.cloned.1.call-start = ((), (), s32[]{:S(2)}) async-start(), calls=%async_computation.6 | async-start | bytes 327680 | tf_op jit(solution)/shard_map/psum | solution.py:437
  228.9 7.0 collective-permute-start.2
  240.3 44.9 %copy-start.3 = (f32[2,128,1024]{2,1,0:T(8,128)}, f32[2,128,1024]{2,1,0:T(8,128)S(1)}, u32[]{:S(2)}) copy-start(f32[2,128,1024]{2,1,0:T(8,128)S(1)} %get-tuple-element.678) | copy-start | bytes 3145732
  241.4 217.3 %all-reduce.37.cloned.1.call-start = ((), (), s32[]{:S(2)}) async-start(), calls=%async_computation.8 | async-start | bytes 163840 | tf_op jit(solution)/shard_map/psum | solution.py:557
  424.5 85.8 %all-reduce.39.cloned.1.call-start = ((), (), s32[]{:S(2)}) async-start(), calls=%async_computation.9 | async-start | bytes 2097152 | tf_op jit(solution)/shard_map/psum | solution.py:584
  461.4 7.4 collective-permute-start.3
  470.7 39.7 %copy-start.77 = (f32[2,128]{1,0:T(2,128)S(1)}, f32[2,128]{1,0:T(2,128)}, u32[]{:S(2)}) copy-start(f32[2,128]{1,0:T(2,128)} %copy-done.76) | copy-start | bytes 3076
  470.7 39.7 %copy-start.111 = (f32[2,128]{1,0:T(2,128)S(1)}, f32[2,128]{1,0:T(2,128)}, u32[]{:S(2)}) copy-start(f32[2,128]{1,0:T(2,128)} %get-tuple-element.726) | copy-start | bytes 3076
  474.6 153.0 %all-reduce.41.cloned.1.call-start = ((), (), s32[]{:S(2)}) async-start(), calls=%async_computation.10 | async-start | bytes 163840 | tf_op jit(solution)/shard_map/psum | solution.py:557
  593.4 85.2 %all-reduce.43.cloned.1.call-start = ((), (), s32[]{:S(2)}) async-start(), calls=%async_computation.11 | async-start | bytes 2097152 | tf_op jit(solution)/shard_map/psum | solution.py:584
  631.7 6.2 collective-permute-start.4
  642.1 91.1 %all-reduce.35.cloned.1.call-start = ((), (), s32[]{:S(2)}) async-start(), calls=%async_computation.7 | async-start | bytes 4194304 | tf_op jit(solution)/shard_map/psum | solution.py:471
  649.5 163.7 %all-reduce.45.cloned.1.call-start = ((), (), s32[]{:S(2)}) async-start(), calls=%async_computation.16 | async-start | bytes 221184 | tf_op jit(solution)/shard_map/psum | solution.py:601
  681.1 217.3 %all-reduce.47.cloned.1.call-start = ((), (), s32[]{:S(2)}) async-start(), calls=%async_computation.17 | async-start | bytes 2359296 | tf_op jit(solution)/shard_map/psum | solution.py:604
  682.2 308.2 %reduce-scatter.11.cloned.1.call-start = ((), (), s32[]{:S(2)}) async-start(), calls=%async_computation.15 | async-start | bytes 4718592 | tf_op jit(solution)/shard_map/reduce_scatter | solution.py:596
  686.8 395.3 %reduce-scatter.9.cloned.1.call-start = ((), (), s32[]{:S(2)}) async-start(), calls=%async_computation.14 | async-start | bytes 4718592 | tf_op jit(solution)/shard_map/reduce_scatter | solution.py:596
  692.9 540.1 %reduce-scatter.7.cloned.1.call-start = ((), (), s32[]{:S(2)}) async-start(), calls=%async_computation.13 | async-start | bytes 9437184 | tf_op jit(solution)/shard_map/reduce_scatter | solution.py:593
  701.5 683.4 %reduce-scatter.5.cloned.1.call-start = ((), (), s32[]{:S(2)}) async-start(), calls=%async_computation.12 | async-start | bytes 9437184 | tf_op jit(solution)/shard_map/reduce_scatter | solution.py:593
  (113 other events, 1358.9 us)
Sparse Core Ops, SparseCore 0:
  41.0 30.8 all-reduce.28
  165.1 54.2 all-reduce.30
  241.6 30.5 all-reduce.32
  424.6 34.0 all-reduce.36
  474.8 35.5 all-reduce.38
  593.5 34.0 all-reduce.40
  642.2 36.3 all-reduce.42
  681.6 51.4 all-reduce.34
  739.3 73.9 all-reduce.44
  818.0 80.3 all-reduce.46
  902.7 87.6 reduce-scatter.10
  994.3 87.8 reduce-scatter.8
  1085.8 147.1 reduce-scatter.6
  1236.9 148.0 reduce-scatter.4

commit v2 on v1

v2 whole, which is shorter than its diff:
```python
import functools

import jax
import jax.numpy as jnp
from jax import lax
from jax.experimental import pallas as pl
from jax.experimental.pallas import tpu as pltpu
from jax.sharding import PartitionSpec as P

STATE = 16
RANK = 128
KERN = 4
LAYERS = 2
MESH = pl.DeviceIdType.MESH
ANY = pl.BlockSpec(memory_space=pl.ANY)
f32, bf16 = jnp.float32, jnp.bfloat16
epsilon = 1e-05


def after(kernel, count, pins):
    def run(*refs):
        return kernel(*refs[:count], *refs[count + len(pins) :])
    return run


def cost(us):
    return pl.CostEstimate(flops=int(us * 1.0e9), bytes_accessed=0, transcendentals=0)


LANES = 128
BIG = 1e30
LOG2E = 1.4426950408889634

def softplus(v):
    return jnp.maximum(v, 0.0) + jnp.log(1.0 + jnp.exp(-jnp.abs(v)))

def spread_states(bc_ref, wide_ref, pick_ref, rows, unroll=8):
    lane = lax.broadcasted_iota(jnp.int32, (STATE, 2 * STATE), 1)
    row = lax.broadcasted_iota(jnp.int32, (STATE, 2 * STATE), 0)
    mask = (lane % STATE == row).astype(jnp.float32)
    src = lax.broadcasted_iota(jnp.int32, (2 * STATE, 2 * LANES), 0)
    dst = lax.broadcasted_iota(jnp.int32, (2 * STATE, 2 * LANES), 1)
    route = ((src // STATE) == (dst // LANES)).astype(jnp.bfloat16)
    chunk = 32
    def step(i, _):
        t0 = pl.multiple_of(i * chunk, chunk)
        bcv = bc_ref[pl.ds(t0, chunk), :]
        for j in range(chunk):
            pick_ref[pl.ds(j * STATE, STATE), :] = (bcv[j:j + 1] * mask).astype(jnp.bfloat16)
        wide_ref[pl.ds(pl.multiple_of(t0 * STATE, chunk * STATE), chunk * STATE), :] = jnp.dot(pick_ref[...], route, preferred_element_type=jnp.float32)
        return 0
    lax.fori_loop(0, rows // chunk, step, 0)

def prep(step_ref_pre, act_ref, keep_ref, dstep_ref, dx_ref, rows):
    def body(i, _):
        sl = pl.ds(pl.multiple_of(i * 32, 32), 32)
        for g in range(dstep_ref.shape[0]):
            st = softplus(step_ref_pre[sl, lanes(g)])
            dstep_ref[g, sl, :] = jnp.where(keep_ref[sl, :] > 0.0, st, BIG)
            dx_ref[g, sl, :] = st * act_ref[sl, lanes(g)]
        return 0
    lax.fori_loop(0, rows // 32, body, 0)

def lanes(g):
    return pl.ds(g * LANES, LANES)

def group_sets(channels, width):
    n = channels // LANES
    return [list(range(i, min(i + width, n))) for i in range(0, n, width)]

def local_kernel(seqs, pre_ref, act_ref, bc_ref, keep_ref, dl_ref, end_ref, gain_ref, wide, pick, dstep, dx):
    rows, channels = pre_ref.shape
    length = rows // seqs
    spread_states(bc_ref, wide, pick, rows)
    prep(pre_ref, act_ref, keep_ref, dstep, dx, rows)
    for gs in group_sets(channels, 8):
        a2 = [-jnp.exp(dl_ref[:, lanes(g)]) * LOG2E for g in gs]
        for s in range(seqs):
            for k, g in enumerate(gs):
                tot = jnp.sum(dstep[g, pl.ds(s * length, length), :], axis=0, keepdims=True)
                gain_ref[pl.ds(s, 1), lanes(g)] = tot
            def blk(i, st):
                st = list(st)
                t0 = pl.multiple_of(s * length + i * 8, 8)
                for j in range(8):
                    b = wide[pl.ds(pl.multiple_of((t0 + j) * STATE, STATE), STATE), pl.ds(0, LANES)]
                    for k, g in enumerate(gs):
                        d = jnp.exp2(a2[k] * dstep[g, pl.ds(t0 + j, 1), :])
                        st[k] = d * st[k] + b * dx[g, pl.ds(t0 + j, 1), :]
                return tuple(st)
            st = lax.fori_loop(0, length // 8, blk, tuple(jnp.zeros((STATE, LANES), jnp.float32) for _ in gs))
            for k, g in enumerate(gs):
                end_ref[s, :, lanes(g)] = st[k]

VM = pl.BlockSpec(memory_space=pltpu.VMEM)

def scan_local(pre, act, bc, keep, dl, seqs, pins=()):
    rows, channels = pre.shape
    f = jnp.float32
    return pl.pallas_call(
        after(functools.partial(local_kernel, seqs), 5, pins),
        out_shape=[
            jax.ShapeDtypeStruct((seqs, STATE, channels), f),
            jax.ShapeDtypeStruct((seqs, channels), f),
        ],
        in_specs=[VM] * 5 + [ANY] * len(pins), out_specs=[VM] * 2,
        scratch_shapes=[pltpu.VMEM((rows * STATE, 2 * LANES), f), pltpu.VMEM((32 * STATE, 2 * STATE), jnp.bfloat16),
                        pltpu.VMEM((channels // LANES, rows, LANES), f), pltpu.VMEM((channels // LANES, rows, LANES), f)],
        compiler_params=pltpu.CompilerParams(vmem_limit_bytes=60 * 2**20),
        cost_estimate=cost(8),
        name="scan_local",
    )(pre, act, bc, keep, dl, *pins)

def forward_kernel(seqs, pre_ref, act_ref, bc_ref, keep_ref, dl_ref, in_ref, y_ref, wide, pick, dstep, dx, part):
    rows, channels = pre_ref.shape
    length = rows // seqs
    spread_states(bc_ref, wide, pick, rows)
    prep(pre_ref, act_ref, keep_ref, dstep, dx, rows)
    for gs in group_sets(channels, 4):
        a2 = [-jnp.exp(dl_ref[:, lanes(g)]) * LOG2E for g in gs]
        for s in range(seqs):
            def blk(i, st):
                st = list(st)
                t0 = pl.multiple_of(s * length + i * 8, 8)
                for j in range(8):
                    at = pl.ds(pl.multiple_of((t0 + j) * STATE, STATE), STATE)
                    b = wide[at, pl.ds(0, LANES)]
                    c = wide[at, pl.ds(LANES, LANES)]
                    for k, g in enumerate(gs):
                        d = jnp.exp2(a2[k] * dstep[g, pl.ds(t0 + j, 1), :])
                        st[k] = d * st[k] + b * dx[g, pl.ds(t0 + j, 1), :]
                        v = st[k] * c
                        part[k, pl.ds(pl.multiple_of(i * 64 + j * 8, 8), 8), :] = v[:8] + v[8:]
                return tuple(st)
            lax.fori_loop(0, length // 8, blk, tuple(in_ref[s, :, lanes(g)] for g in gs))
            def red(i, _):
                t0 = pl.multiple_of(s * length + i * 8, 8)
                for k, g in enumerate(gs):
                    acc = part[k, pl.ds(i * 64, 8, stride=8), :]
                    for m in range(1, 8):
                        acc = acc + part[k, pl.ds(i * 64 + m, 8, stride=8), :]
                    y_ref[pl.ds(t0, 8), lanes(g)] = acc
                return 0
            lax.fori_loop(0, length // 8, red, 0)

def scan_forward(pre, act, bc, keep, dl, state_in, seqs, pins=()):
    rows, channels = pre.shape
    f = jnp.float32
    return pl.pallas_call(
        after(functools.partial(forward_kernel, seqs), 6, pins),
        out_shape=jax.ShapeDtypeStruct((rows, channels), f),
        in_specs=[VM] * 6 + [ANY] * len(pins), out_specs=VM,
        scratch_shapes=[pltpu.VMEM((rows * STATE, 2 * LANES), f), pltpu.VMEM((32 * STATE, 2 * STATE), jnp.bfloat16),
                        pltpu.VMEM((channels // LANES, rows, LANES), f), pltpu.VMEM((channels // LANES, rows, LANES), f),
                        pltpu.VMEM((4, rows // seqs * 8, LANES), f)],
        compiler_params=pltpu.CompilerParams(vmem_limit_bytes=60 * 2**20),
        cost_estimate=cost(11),
        name="scan_forward",
    )(pre, act, bc, keep, dl, state_in, *pins)

LN2 = 0.6931471805599453

def back_local_kernel(seqs, pre_ref, gs_ref, bc_ref, keep_ref, dl_ref, out_ref, wide, pick, dstep, gsc):
    rows, channels = pre_ref.shape
    length = rows // seqs
    spread_states(bc_ref, wide, pick, rows)
    def body(i, _):
        sl = pl.ds(pl.multiple_of(i * 32, 32), 32)
        for g in range(channels // LANES):
            st = softplus(pre_ref[sl, lanes(g)])
            dstep[g, sl, :] = jnp.where(keep_ref[sl, :] > 0.0, st, BIG)
            gsc[g, sl, :] = gs_ref[sl, lanes(g)]
        return 0
    lax.fori_loop(0, rows // 32, body, 0)
    for gs in group_sets(channels, 8):
        a2 = [-jnp.exp(dl_ref[:, lanes(g)]) * LOG2E for g in gs]
        for s in range(seqs):
            def blk(i, st):
                st = list(st)
                t0 = pl.multiple_of(s * length + (length // 8 - 1 - i) * 8, 8)
                for j in reversed(range(8)):
                    c = wide[pl.ds(pl.multiple_of((t0 + j) * STATE, STATE), STATE), pl.ds(LANES, LANES)]
                    for k, g in enumerate(gs):
                        d = jnp.exp2(a2[k] * dstep[g, pl.ds(t0 + j, 1), :])
                        st[k] = d * (st[k] + c * gsc[g, pl.ds(t0 + j, 1), :])
                return tuple(st)
            st = lax.fori_loop(0, length // 8, blk, tuple(jnp.zeros((STATE, LANES), jnp.float32) for _ in gs))
            for k, g in enumerate(gs):
                out_ref[s, :, lanes(g)] = st[k]

def scan_back_local(pre, gs, bc, keep, dl, seqs, pins=()):
    rows, channels = pre.shape
    f = jnp.float32
    return pl.pallas_call(
        after(functools.partial(back_local_kernel, seqs), 5, pins),
        out_shape=jax.ShapeDtypeStruct((seqs, STATE, channels), f),
        in_specs=[VM] * 5 + [ANY] * len(pins), out_specs=VM,
        scratch_shapes=[pltpu.VMEM((rows * STATE, 2 * LANES), f), pltpu.VMEM((32 * STATE, 2 * STATE), jnp.bfloat16),
                        pltpu.VMEM((channels // LANES, rows, LANES), f), pltpu.VMEM((channels // LANES, rows, LANES), f)],
        compiler_params=pltpu.CompilerParams(vmem_limit_bytes=60 * 2**20),
        cost_estimate=cost(8),
        name="scan_back_local",
    )(pre, gs, bc, keep, dl, *pins)

def back_kernel(seqs, pre_ref, act_ref, gs_ref, bc_ref, keep_ref, dl_ref, skip_ref, in_ref, lam_ref,
                gpre_ref, gact_ref, gbc_ref, gdl_ref,
                wide, pick, dstep, dx, stepc, gsc, states, partq, partr, accb, accc, rowsum):
    rows, channels = pre_ref.shape
    length = rows // seqs
    f = jnp.float32
    spread_states(bc_ref, wide, pick, rows)
    def body(i, _):
        sl = pl.ds(pl.multiple_of(i * 32, 32), 32)
        for g in range(channels // LANES):
            st = softplus(pre_ref[sl, lanes(g)])
            stepc[g, sl, :] = st
            dstep[g, sl, :] = jnp.where(keep_ref[sl, :] > 0.0, st, BIG)
            dx[g, sl, :] = st * act_ref[sl, lanes(g)]
            gsc[g, sl, :] = gs_ref[sl, lanes(g)]
        return 0
    lax.fori_loop(0, rows // 32, body, 0)
    sets = group_sets(channels, 4)
    for index, gs in enumerate(sets):
        a2 = [-jnp.exp(dl_ref[:, lanes(g)]) * LOG2E for g in gs]
        gdl = [jnp.zeros((STATE, LANES), f) for _ in gs]
        for s in range(seqs):
            for k, g in enumerate(gs):
                states[k, pl.ds(0, STATE), :] = in_ref[s, :, lanes(g)]
            def fwd(i, st):
                st = list(st)
                t0 = pl.multiple_of(s * length + i * 8, 8)
                for j in range(8):
                    b = wide[pl.ds(pl.multiple_of((t0 + j) * STATE, STATE), STATE), pl.ds(0, LANES)]
                    for k, g in enumerate(gs):
                        d = jnp.exp2(a2[k] * dstep[g, pl.ds(t0 + j, 1), :])
                        st[k] = d * st[k] + b * dx[g, pl.ds(t0 + j, 1), :]
                        states[k, pl.ds(pl.multiple_of((i * 8 + j + 1) * STATE, STATE), STATE), :] = st[k]
                return tuple(st)
            lax.fori_loop(0, length // 8, fwd, tuple(in_ref[s, :, lanes(g)] for g in gs))
            def bwd(i, carry):
                st = list(carry[:len(gs)])
                am = list(carry[len(gs):])
                l0 = (length // 8 - 1 - i) * 8
                t0 = pl.multiple_of(s * length + l0, 8)
                for j in reversed(range(8)):
                    at = pl.ds(pl.multiple_of((t0 + j) * STATE, STATE), STATE)
                    b = wide[at, pl.ds(0, LANES)]
                    c = wide[at, pl.ds(LANES, LANES)]
                    tb = tc = None
                    here = pl.ds(pl.multiple_of((l0 + j) * 8, 8), 8)
                    for k, g in enumerate(gs):
                        row = pl.ds(t0 + j, 1)
                        grow = gsc[g, row, :]
                        d = jnp.exp2(a2[k] * dstep[g, row, :])
                        lam = st[k] + c * grow
                        old = states[k, pl.ds(pl.multiple_of((l0 + j) * STATE, STATE), STATE), :]
                        new = states[k, pl.ds(pl.multiple_of((l0 + j + 1) * STATE, STATE), STATE), :]
                        st[k] = d * lam
                        lp = st[k] * old
                        q = lam * b
                        partq[k, here, :] = q[:8] + q[8:]
                        r = lp * a2[k]
                        partr[k, here, :] = r[:8] + r[8:]
                        am[k] = am[k] + lp * stepc[g, row, :]
                        u = lam * dx[g, row, :]
                        v = new * grow
                        tb = u if tb is None else tb + u
                        tc = v if tc is None else tc + v
                    if index > 0:
                        tb = tb + accb[at, :]
                        tc = tc + accc[at, :]
                    accb[at, :] = tb
                    accc[at, :] = tc
                return tuple(st) + tuple(am)
            out = lax.fori_loop(0, length // 8, bwd, tuple(lam_ref[s, :, lanes(g)] for g in gs) + tuple(gdl))
            gdl = list(out[len(gs):])
            def red(i, _):
                t0 = pl.multiple_of(s * length + i * 8, 8)
                for k, g in enumerate(gs):
                    q = partq[k, pl.ds(i * 64, 8, stride=8), :]
                    r = partr[k, pl.ds(i * 64, 8, stride=8), :]
                    for m in range(1, 8):
                        q = q + partq[k, pl.ds(i * 64 + m, 8, stride=8), :]
                        r = r + partr[k, pl.ds(i * 64 + m, 8, stride=8), :]
                    here = pl.ds(t0, 8)
                    p = pre_ref[here, lanes(g)]
                    gstep = r * LN2 + act_ref[here, lanes(g)] * q
                    gpre_ref[here, lanes(g)] = gstep * (1.0 / (1.0 + jnp.exp(-p)))
                    gact_ref[here, lanes(g)] = stepc[g, here, :] * q + gsc[g, here, :] * skip_ref[:, lanes(g)]
                return 0
            lax.fori_loop(0, length // 8, red, 0)
        for k, g in enumerate(gs):
            gdl_ref[:, lanes(g)] = gdl[k] * (a2[k] * LN2)
    ones = jnp.ones((LANES, LANES), jnp.bfloat16)
    lane = lax.broadcasted_iota(jnp.int32, (32 * STATE, LANES), 1)
    row = lax.broadcasted_iota(jnp.int32, (32 * STATE, LANES), 0) % STATE
    mb = lane == row
    mc = lane == row + STATE
    def fin(i, _):
        sl = pl.ds(pl.multiple_of(i * 32 * STATE, 32 * STATE), 32 * STATE)
        sb = jnp.dot(accb[sl, :].astype(jnp.bfloat16), ones, preferred_element_type=f)
        sc = jnp.dot(accc[sl, :].astype(jnp.bfloat16), ones, preferred_element_type=f)
        rowsum[...] = jnp.where(mb, sb, jnp.where(mc, sc, 0.0))
        acc = rowsum[pl.ds(0, 32, stride=STATE), :]
        for m in range(1, STATE):
            acc = acc + rowsum[pl.ds(m, 32, stride=STATE), :]
        gbc_ref[pl.ds(pl.multiple_of(i * 32, 32), 32), :] = acc
        return 0
    lax.fori_loop(0, rows // 32, fin, 0)

def scan_back(pre, act, gs, bc, keep, dl, skip, state_in, lam_in, seqs, pins=()):
    rows, channels = pre.shape
    f = jnp.float32
    groups = channels // LANES
    length = rows // seqs
    big = pltpu.VMEM((groups, rows, LANES), f)
    return pl.pallas_call(
        after(functools.partial(back_kernel, seqs), 9, pins),
        out_shape=[jax.ShapeDtypeStruct((rows, channels), f), jax.ShapeDtypeStruct((rows, channels), f),
                   jax.ShapeDtypeStruct((rows, LANES), f), jax.ShapeDtypeStruct((STATE, channels), f)],
        in_specs=[VM] * 9 + [ANY] * len(pins), out_specs=[VM] * 4,
        scratch_shapes=[pltpu.VMEM((rows * STATE, 2 * LANES), f), pltpu.VMEM((32 * STATE, 2 * STATE), jnp.bfloat16),
                        big, big, big, big,
                        pltpu.VMEM((4, (length + 1) * STATE, LANES), f),
                        pltpu.VMEM((4, length * 8, LANES), f), pltpu.VMEM((4, length * 8, LANES), f),
                        pltpu.VMEM((rows * STATE, LANES), f), pltpu.VMEM((rows * STATE, LANES), f),
                        pltpu.VMEM((32 * STATE, LANES), f)],
        compiler_params=pltpu.CompilerParams(vmem_limit_bytes=60 * 2**20),
        cost_estimate=cost(23),
        name="scan_back",
    )(pre, act, gs, bc, keep, dl, skip, state_in, lam_in, *pins)


def greet(peers):
    barrier = pltpu.get_barrier_semaphore()
    for p in peers:
        pl.semaphore_signal(barrier, inc=1, device_id=p, device_id_type=MESH)
    pl.semaphore_wait(barrier, len(peers))

def ch_sum_kernel(n, x_ref, out_ref, mine, slots, send, recv):
    me = lax.axis_index("ch")
    peers = [{"ch": lax.rem(me + d, n)} for d in range(1, n)]
    greet(peers)
    mine[...] = x_ref[...].astype(bf16)
    copies = []
    for d in range(1, n):
        c = pltpu.make_async_remote_copy(src_ref=mine, dst_ref=slots.at[d - 1], send_sem=send.at[d - 1], recv_sem=recv.at[d - 1], device_id=peers[d - 1], device_id_type=MESH)
        c.start()
        copies.append(c)
    total = x_ref[...].astype(bf16).astype(f32)
    for d, c in zip(range(1, n), copies):
        c.wait()
        total = total + slots[d - 1].astype(f32)
    out_ref[...] = total

def ch_sum(x, n, cid):
    return pl.pallas_call(
        functools.partial(ch_sum_kernel, n),
        out_shape=jax.ShapeDtypeStruct(x.shape, f32), in_specs=[VM], out_specs=VM,
        scratch_shapes=[pltpu.VMEM(x.shape, bf16), pltpu.VMEM((n - 1,) + x.shape, bf16), pltpu.SemaphoreType.DMA((n - 1,)), pltpu.SemaphoreType.DMA((n - 1,))],
        compiler_params=pltpu.CompilerParams(collective_id=cid, has_side_effects=True, vmem_limit_bytes=32 * 2**20), cost_estimate=cost(10), name="ch_sum",
    )(x)

def reduce_kernel(n, parts, gather, x_ref, out_ref, s1, sum1, s2, mine, got, fin, sem1, rem1, sem2, rem2, sem3, rem3, sem4, rem4):
    xs = n // 2
    me = lax.axis_index("ch")
    x, core = me // 2, lax.rem(me, 2)
    peer = {"ch": x * 2 + 1 - core}
    others = [lax.rem(x + d, xs) for d in range(1, xs)]
    greet([peer] + [{"ch": o * 2 + core} for o in others])
    rows, width = x_ref.shape[0] // parts, x_ref.shape[1] // n
    def cols(block):
        return pl.ds(pl.multiple_of(block * width, width), width)
    def stage1(p, k):
        return pltpu.make_async_remote_copy(src_ref=x_ref.at[pl.ds(p * rows, rows), cols(k * 2 + 1 - core)], dst_ref=s1.at[p, k], send_sem=sem1.at[p, k], recv_sem=rem1.at[p, k], device_id=peer, device_id_type=MESH)
    def stage2(p, d):
        o = others[d]
        return pltpu.make_async_remote_copy(src_ref=sum1.at[p, o], dst_ref=s2.at[p, d], send_sem=sem2.at[p, d], recv_sem=rem2.at[p, d], device_id={"ch": o * 2 + core}, device_id_type=MESH)
    def stage3(p, d):
        o = others[d]
        return pltpu.make_async_remote_copy(src_ref=mine.at[p], dst_ref=got.at[p, d], send_sem=sem3.at[p, d], recv_sem=rem3.at[p, d], device_id={"ch": o * 2 + core}, device_id_type=MESH)
    for p in range(parts):
        for k in range(xs):
            stage1(p, k).start()
    for p in range(parts):
        for k in range(xs):
            stage1(p, k).wait_recv()
            sum1[p, k] = (x_ref[pl.ds(p * rows, rows), cols(k * 2 + core)].astype(f32) + s1[p, k].astype(f32)).astype(bf16)
        for d in range(xs - 1):
            stage2(p, d).start()
    for p in range(parts):
        total = sum1[p, x].astype(f32)
        for d in range(xs - 1):
            stage2(p, d).wait_recv()
            total = total + s2[p, d].astype(f32)
        if gather:
            mine[p] = total.astype(bf16)
            for d in range(xs - 1):
                stage3(p, d).start()
        else:
            out_ref[pl.ds(p * rows, rows), :] = total
    if gather:
        def stage4(p, d):
            src = mine.at[p] if d < 0 else got.at[p, d]
            return pltpu.make_async_remote_copy(src_ref=src, dst_ref=fin.at[p, d + 1], send_sem=sem4.at[p, d + 1], recv_sem=rem4.at[p, d + 1], device_id=peer, device_id_type=MESH)
        def chip(d):
            return lax.rem(x + xs - 1 - d, xs)
        for p in range(parts):
            stage4(p, -1).start()
            out_ref[pl.ds(p * rows, rows), cols(me)] = mine[p].astype(out_ref.dtype)
            for d in range(xs - 1):
                stage3(p, d).wait_recv()
                stage4(p, d).start()
                out_ref[pl.ds(p * rows, rows), cols(chip(d) * 2 + core)] = got[p, d].astype(out_ref.dtype)
        for p in range(parts):
            for d in range(-1, xs - 1):
                stage4(p, d).wait_recv()
                out_ref[pl.ds(p * rows, rows), cols(chip(d) * 2 + 1 - core)] = fin[p, d + 1].astype(out_ref.dtype)
    for p in range(parts):
        for k in range(xs):
            stage1(p, k).wait_send()
        for d in range(xs - 1):
            stage2(p, d).wait_send()
            if gather:
                stage3(p, d).wait_send()
        if gather:
            for d in range(-1, xs - 1):
                stage4(p, d).wait_send()

def ch_reduce(x, n, cid, gather, parts=2, out_dtype=f32):
    rows, width = x.shape
    xs, r, w = n // 2, rows // parts, width // n
    sem = pltpu.SemaphoreType.DMA
    return pl.pallas_call(
        functools.partial(reduce_kernel, n, parts, gather),
        out_shape=jax.ShapeDtypeStruct((rows, width if gather else w), out_dtype), in_specs=[VM], out_specs=VM,
        scratch_shapes=[pltpu.VMEM((parts, xs, r, w), bf16), pltpu.VMEM((parts, xs, r, w), bf16), pltpu.VMEM((parts, xs - 1, r, w), bf16),
                        pltpu.VMEM((parts, r, w), bf16), pltpu.VMEM((parts, xs - 1, r, w), bf16), pltpu.VMEM((parts, xs, r, w), bf16),
                        sem((parts, xs)), sem((parts, xs)), sem((parts, xs - 1)), sem((parts, xs - 1)), sem((parts, xs - 1)), sem((parts, xs - 1)), sem((parts, xs)), sem((parts, xs))],
        compiler_params=pltpu.CompilerParams(collective_id=cid, has_side_effects=True, vmem_limit_bytes=48 * 2**20), cost_estimate=cost(18), name="ch_reduce",
    )(x)


def carry_kernel(n, fwd, rev, *refs):
    refs = list(refs)
    tot_ref, dl_ref = refs.pop(0), refs.pop(0)
    k = fwd + rev
    ends = [refs.pop(0) for _ in range(k)]
    outs = [refs.pop(0) for _ in range(k)]
    mine, slots, tots, send, recv, tsend, trecv = refs
    me = lax.axis_index("seq")
    seqs = tot_ref.shape[0]
    greet([{"seq": lax.rem(me + d, n)} for d in range(1, n)])
    a2 = -jnp.exp(dl_ref[...]) * LOG2E
    directions = [False] * fwd + [True] * rev
    def copies(i, d):
        away = -d if directions[i] else d
        to = {"seq": lax.rem(me + away + n, n)}
        return (
            pltpu.make_async_remote_copy(src_ref=mine.at[i], dst_ref=slots.at[i, d - 1], send_sem=send.at[i, d - 1], recv_sem=recv.at[i, d - 1], device_id=to, device_id_type=MESH),
            pltpu.make_async_remote_copy(src_ref=tot_ref, dst_ref=tots.at[i, d - 1], send_sem=tsend.at[i, d - 1], recv_sem=trecv.at[i, d - 1], device_id=to, device_id_type=MESH),
        )
    for i in range(k):
        mine[i] = ends[i][...].astype(bf16)
        outs[i][...] = jnp.zeros_like(outs[i])
    for d in reversed(range(1, n)):
        for i in range(k):
            place = n - 1 - me if directions[i] else me
            @pl.when(place + d < n)
            def _():
                for c in copies(i, d):
                    c.start()
    for d in reversed(range(1, n)):
        for i in range(k):
            place = n - 1 - me if directions[i] else me
            @pl.when(place >= d)
            def _():
                for c in copies(i, d):
                    c.wait_recv()
                for s in range(seqs):
                    gain = jnp.exp2(a2 * tots[i, d - 1, pl.ds(s, 1), :])
                    outs[i][s] = gain * outs[i][s] + slots[i, d - 1, s].astype(f32)
    for d in reversed(range(1, n)):
        for i in range(k):
            place = n - 1 - me if directions[i] else me
            @pl.when(place + d < n)
            def _():
                for c in copies(i, d):
                    c.wait_send()

def carry_over(tot, dl, ends, n, cid, fwd, rev):
    k = len(ends)
    sem = pltpu.SemaphoreType.DMA
    return pl.pallas_call(
        functools.partial(carry_kernel, n, int(fwd), int(rev)),
        out_shape=[jax.ShapeDtypeStruct(ends[0].shape, f32)] * k, in_specs=[VM] * (k + 2), out_specs=[VM] * k,
        scratch_shapes=[pltpu.VMEM((k,) + ends[0].shape, bf16), pltpu.VMEM((k, n - 1) + ends[0].shape, bf16), pltpu.VMEM((k, n - 1) + tot.shape, f32),
                        sem((k, n - 1)), sem((k, n - 1)), sem((k, n - 1)), sem((k, n - 1))],
        compiler_params=pltpu.CompilerParams(collective_id=cid, has_side_effects=True, vmem_limit_bytes=32 * 2**20), cost_estimate=cost(19), name="carry_over",
    )(tot, dl, *ends)


def passed_along(block, axis, distance):
    devices = range(lax.axis_size(axis))
    route = [(i - distance, i) for i in devices if i - distance in devices]
    return lax.ppermute(block, axis, route)


def silu_slope(argument):
    logistic = jax.nn.sigmoid(argument)
    return logistic * (1.0 + argument * (1.0 - logistic))


def conv_local(extended, weights, biases, seg_ext):
    length_now = extended.shape[1] - (KERN - 1)
    seg_now = seg_ext[:, KERN - 1 :]
    summed = biases + jnp.zeros((extended.shape[0], length_now, extended.shape[2]), f32)
    for lag_index in range(KERN):
        same_doc = (seg_ext[:, lag_index : lag_index + length_now] == seg_now).astype(f32)
        summed = (
            summed
            + weights[lag_index]
            * extended[:, lag_index : lag_index + length_now]
            * same_doc[:, :, None]
        )
    return summed


def dot(a, b, contract):
    return lax.dot_general(a, b, ((contract[:1], contract[1:]), ((), ())), preferred_element_type=f32)


def tokens_of_all(rows):
    return lax.all_gather(rows, "seq", tiled=True)


def columns_of_all(rows):
    n = lax.axis_size("seq")
    return lax.all_to_all(rows, "seq", split_axis=1, concat_axis=0, tiled=True)


def local(
    hidden_in,
    segments,
    cotangent,
    norm_gain,
    input_projection_weight,
    conv_weight,
    conv_bias,
    proj_weight,
    step_weight,
    step_bias,
    decay_log,
    skip_gain,
    output_projection_weight,
):
    seqs, length, width = hidden_in.shape
    rows = seqs * length
    nch, nseq = lax.axis_size("ch"), lax.axis_size("seq")
    channels = conv_bias.shape[-1]
    share = width // nch
    share_start = lax.axis_index("ch") * share
    seg_own = segments.astype(f32)
    seg_edge = passed_along(seg_own[:, -(KERN - 1) :], "seq", 1)
    seg_ext = jnp.concatenate([seg_edge, seg_own], axis=1)
    keep = (seg_ext[:, KERN - 2 : -1] == seg_own).astype(f32).reshape(-1, 1)
    hidden = hidden_in.astype(f32).reshape(rows, width)
    grad_rows = cotangent.astype(f32).reshape(rows, width)
    ids = iter(range(100))

    out_cols = {LAYERS - 1: columns_of_all(grad_rows.astype(bf16))}
    stored = []
    result = None
    ready = {(0, "local"): (out_cols[LAYERS - 1],)}
    for layer in range(LAYERS):
        last = layer == LAYERS - 1
        inv_rms = lax.rsqrt(jnp.mean(hidden * hidden, axis=-1, keepdims=True) + epsilon)
        normed = (hidden * inv_rms * norm_gain[layer]).astype(bf16)
        w_in = lax.optimization_barrier(input_projection_weight)[layer]
        both = lax.dot_general(normed, w_in, (((1,), (0,)), ((), ())), preferred_element_type=f32)
        values, gate_pre = both[:, 0], both[:, 1]
        normed_cols = columns_of_all(normed)
        values3 = values.reshape(seqs, length, channels)
        edge = passed_along(values3[:, -(KERN - 1) :], "seq", 1)
        extended = jnp.concatenate([edge, values3], axis=1)
        conv_out, conv_pull = jax.vjp(
            functools.partial(conv_local, seg_ext=seg_ext), extended, conv_weight[layer], conv_bias[layer]
        )
        conv_out = conv_out.reshape(rows, channels)
        activated = jax.nn.silu(conv_out)
        act_low = activated.astype(bf16)
        proj_out = ch_sum(dot(act_low, proj_weight[layer], (1, 0)), nch, next(ids))
        rank_low = proj_out[:, :RANK].astype(bf16)
        mats = proj_out[:, RANK:]
        step_pre = dot(rank_low, step_weight[layer], (1, 0)) + step_bias[layer]
        rates = decay_log[layer]
        end_state, total = scan_local(
            step_pre, activated, mats, keep, rates, seqs, ready.get((layer, "local"), ())
        )
        gate_act = jax.nn.silu(gate_pre)
        if last:
            out_low = grad_rows.astype(bf16)
            grad_mixed = dot(out_low, output_projection_weight[layer], (1, 1))
            grad_scan = grad_mixed * gate_act
            start = scan_back_local(step_pre, grad_scan, mats, keep, rates, seqs)
            state_in, lam_in = carry_over(total, rates, [end_state, start], nseq, next(ids), True, True)
        else:
            (state_in,) = carry_over(total, rates, [end_state], nseq, next(ids), True, False)
        pins = (normed_cols,) if layer == 0 else (normed_cols, stored[0][-2])
        y = scan_forward(step_pre, activated, mats, keep, rates, state_in, seqs, pins)
        scanned = y + skip_gain[layer] * activated
        mixed = (scanned * gate_act).astype(bf16)
        out_part = dot(mixed, output_projection_weight[layer], (1, 0)).astype(bf16)
        mixed_all = tokens_of_all(mixed)
        stored.append(
            (hidden, inv_rms, normed, gate_pre, gate_act, conv_out, activated, act_low, conv_pull, rank_low,
             step_pre, mats, total, state_in, scanned, mixed_all, normed_cols)
        )
        if last:
            branch = ch_reduce(out_part, nch, next(ids), False)
            result = (lax.dynamic_slice_in_dim(hidden, share_start, share, 1) + branch).astype(bf16)
        else:
            hidden = hidden + ch_reduce(out_part, nch, next(ids), True)

    collected = [None] * LAYERS
    for layer in reversed(range(LAYERS)):
        last = layer == LAYERS - 1
        (hidden, inv_rms, normed, gate_pre, gate_act, conv_out, activated, act_low, conv_pull, rank_low,
         step_pre, mats, total, state_in, scanned, mixed_all, normed_cols) = stored[layer]
        rates = decay_log[layer]
        if not last:
            out_low = grad_rows.astype(bf16)
            grad_mixed = dot(out_low, output_projection_weight[layer], (1, 1))
            grad_scan = grad_mixed * gate_act
            start = scan_back_local(step_pre, grad_scan, mats, keep, rates, seqs, (stored[layer + 1][-2],))
            (lam_in,) = carry_over(total, rates, [start], nseq, next(ids), False, True)
            out_cols[layer] = columns_of_all(out_low)
        grad_gate = (grad_mixed * scanned * silu_slope(gate_pre)).astype(bf16)
        gate_all = tokens_of_all(grad_gate)
        grad_skip = jnp.sum(grad_scan * activated, axis=0)
        grad_pre, grad_act, grad_mats, grad_decay = scan_back(
            step_pre, activated, grad_scan, mats, keep, rates, skip_gain[layer][None], state_in, lam_in, seqs,
            () if last else (out_cols[layer], gate_all_last),
        )
        gate_all_last = gate_all
        grad_step_bias = jnp.sum(grad_pre, axis=0)
        pre_low = grad_pre.astype(bf16)
        grad_step_weight = dot(rank_low, pre_low, (0, 0))
        rank_part = dot(pre_low, step_weight[layer], (1, 1))
        grad_proj = ch_sum(
            jnp.concatenate([rank_part, grad_mats[:, : 2 * STATE]], axis=-1), nch, next(ids)
        ).astype(bf16)
        grad_proj_weight = dot(act_low, grad_proj, (0, 0))
        grad_act = grad_act + dot(grad_proj, proj_weight[layer], (1, 1))
        grad_conv = (grad_act * silu_slope(conv_out)).reshape(seqs, length, channels)
        grad_ext, grad_conv_weight, grad_conv_bias = conv_pull(grad_conv)
        returned = passed_along(grad_ext[:, : KERN - 1], "seq", -1)
        grad_values = grad_ext[:, KERN - 1 :]
        grad_values = jnp.concatenate(
            [grad_values[:, : -(KERN - 1)], grad_values[:, -(KERN - 1) :] + returned], axis=1
        ).reshape(rows, channels).astype(bf16)
        values_all = tokens_of_all(grad_values)
        w_in = lax.optimization_barrier(input_projection_weight)[layer]
        grad_both = jnp.stack([grad_values, grad_gate], axis=1)
        grad_part = lax.dot_general(grad_both, w_in, (((1, 2), (1, 2)), ((), ())), preferred_element_type=f32)
        grad_normed = ch_reduce(grad_part.astype(bf16), nch, next(ids), True)
        scale_now = norm_gain[layer]
        inner = jnp.sum(grad_normed * scale_now * hidden, axis=-1, keepdims=True)
        grad_hidden = inv_rms * scale_now * grad_normed - hidden * (inv_rms * inv_rms * inv_rms) * inner / width
        grad_norm = lax.dynamic_slice_in_dim(jnp.sum(grad_normed * hidden * inv_rms, axis=0), share_start, share, 0)
        grad_rows = grad_rows + grad_hidden
        grad_out_weight = dot(mixed_all, out_cols[layer], (0, 0))
        grad_in_gate = dot(normed_cols, gate_all, (0, 0))
        grad_in_values = dot(normed_cols, values_all, (0, 0))
        small = [grad_norm, grad_conv_weight, grad_conv_bias, grad_proj_weight, grad_step_weight, grad_step_bias, grad_decay, grad_skip]
        small = [v.astype(bf16) for v in small]
        if not last:
            small, _ = lax.optimization_barrier((small, collected[LAYERS - 1]))
        small = [lax.psum(v, "seq").astype(f32) for v in small]
        collected[layer] = (
            small[0],
            jnp.stack([grad_in_values, grad_in_gate], axis=1),
            *small[1:],
            grad_out_weight,
        )
    grad_input = lax.dynamic_slice_in_dim(grad_rows, share_start, share, 1).reshape(seqs, length, share)
    stacked = [jnp.stack([collected[layer][member] for layer in range(LAYERS)], axis=0) for member in range(10)]
    return (result.reshape(seqs, length, share), grad_input, *stacked)


def solution(mesh):
    in_specs = (
        P(None, "seq", None),
        P(None, "seq"),
        P(None, "seq", None),
        P(),
        P(None, None, None, "ch"),
        P(None, None, "ch"),
        P(None, "ch"),
        P(None, "ch", None),
        P(None, None, "ch"),
        P(None, "ch"),
        P(None, None, "ch"),
        P(None, "ch"),
        P(None, "ch", None),
    )
    out_specs = (
        P(None, "seq", "ch"),
        P(None, "seq", "ch"),
        P(None, "ch"),
        P(None, "seq", None, "ch"),
        P(None, None, "ch"),
        P(None, "ch"),
        P(None, "ch", None),
        P(None, None, "ch"),
        P(None, "ch"),
        P(None, None, "ch"),
        P(None, "ch"),
        P(None, "ch", "seq"),
    )
    return jax.shard_map(local, mesh=mesh, in_specs=in_specs, out_specs=out_specs, check_vma=False)
```

time: 1410 us -> 833 us (0.59)
  waiting for transfers between devices: 885 us -> 261 us
  Pallas kernels: 99.5 us -> 278 us
  blocking collectives: 180 us -> 51.5 us
  starting transfers between devices: 19.7 us -> 42.1 us
  other arithmetic: 73.4 us -> 51.8 us
    reduce_scatter x4 -> x0, waiting for transfers between devices: 479 us -> none  [the longest x2 300 us: local(): lax.psum_scatter(grad_in_weight.astype(jnp.bfloat16), 'seq', scatter_dime...]
    psum x10 -> x2, waiting for transfers between devices: 400 us -> 144 us  [local(): small = [lax.psum(v, 'seq').astype(f32) for v in small]]
    all_gather x6 -> x0, blocking collectives: 180 us -> none  [the longest x4 122 us: prefix(): lax.all_gather(part.astype(jnp.bfloat16), axis).astype(part.dtype)]
    pallas_call x8 -> x19, Pallas kernels: 99.5 us -> 278 us  [the longest x3 88.5 us: carry_over(): pl.pallas_call(functools.partial(carry_kernel, n, int(fwd), int(rev)), ou...]
    all_gather x0 -> x6, waiting for transfers between devices: none -> 107 us  [tokens_of_all(): return lax.all_gather(rows, 'seq', tiled=True)]
    psum x0 -> x1, blocking collectives: none -> 51.5 us  [local(): small = [lax.psum(v, 'seq').astype(f32) for v in small]]
    all_to_all x0 -> x4, starting transfers between devices: none -> 24.1 us  [columns_of_all(): return lax.all_to_all(rows, 'seq', split_axis=1, concat_axis=0, tiled=True)]
    select_n x32 -> x0, other arithmetic: 16.7 us -> none  [the longest x16 8.59 us: prefix_hop(): return jax.tree.map(lambda a, b: jnp.where(reached, a, b), new, before)]
  transfers between devices with their start and end apart: 19 -> 17, of which waited for: 17 -> 6; matrix products, arithmetic and copies ran while one was open for 5% -> 15% of each run, Pallas kernels for 1% -> 31%
where the time goes in v2:
time: 833 us; the launch traced here: 821 us
  Pallas kernels  278 us (33%)
  waiting for transfers between devices  261 us (31%)
  matrix products  73.2 us (9%)
  other arithmetic  51.8 us (6%)
  blocking collectives  51.5 us (6%)
  local copies, waits for them, and re-layouts  47 us (6%)
  starting transfers between devices  42.1 us (5%)
  between operations  16.1 us (2%)
    psum x2, waiting for transfers between devices, local(): small = [lax.psum(v, 'seq').astype(f32) for v in small]  144 us
    all_gather x6, waiting for transfers between devices, tokens_of_all(): return lax.all_gather(rows, 'seq', tiled=True)  107 us
    pallas_call x3, Pallas kernels, carry_over(): pl.pallas_call(functools.partial(carry_kernel, n, int(fwd), int(rev)), ou...  88.5 us
    pallas_call x4, Pallas kernels, ch_reduce(): pl.pallas_call(functools.partial(reduce_kernel, n, parts, gather), out_sh...  61.6 us
    dot_general x22, matrix products, dot(): lax.dot_general(a, b, ((contract[:1], contract[1:]), ((), ())), preferred...  54.4 us
    psum x1, blocking collectives, local(): small = [lax.psum(v, 'seq').astype(f32) for v in small]  51.5 us
    pallas_call x2, Pallas kernels, scan_back(): pl.pallas_call(after(functools.partial(back_kernel, seqs), 9, pins), out_...  46.3 us
    pallas_call x4, Pallas kernels, ch_sum(): pl.pallas_call(functools.partial(ch_sum_kernel, n), out_shape=jax.ShapeDt...  28.5 us
  transfers between devices with their start and end apart: 17, of which 6 were waited for; matrix products, arithmetic and copies ran while one was open for 15% of the time, Pallas kernels for 31%

profile of v2, /device:TPU:10, one launch (start us, length us, event | category | flops | bytes accessed | tf_op | source)
XLA Modules:
  0.0 820.8 jit_solution(7528544660641029656)
XLA Ops:
  9.6 14.0 %fusion.100 = (bf16[1,2048,2,1024]{3,2,1,0:T(2,128)(2,1)S(1)}, bf16[1,2048,2,1024]{3,2,1,0:T(2,128)(2,1)}) fusion(bf16[2,2048,2,1024]{3,2,1,0:T(2,128)(2,1)} %param.17), kind=kLoop, calls=%fused_computation.222 | loop fusion | bytes 33554432 | tf_op jit(solution)/shard_map/slice | solution.py:579
  70.8 7.9 scan_local.2
  80.3 25.6 %carry_over.3.refs_5_.refs_7_ = f32[2,16,1024]{2,1,0:T(8,128)S(1)} custom-call(f32[2,1024]{1,0:T(2,128)S(1)} %copy-done.15, f32[16,1024]{1,0:T(8,128)S(1)} %copy-done.4, f32[2,16,1024]{2,1,0:T(8,128)S(1)} %copy-done.8), custom_call_target="tpu_custom_call" | custom-call | flops 19000000512 | tf_op jit(solution)/shard_map/carry_over/pallas_call | solution.py:494
  107.6 11.0 %scan_forward.2 = f32[256,1024]{1,0:T(8,128)} custom-call(f32[256,1024]{1,0:T(8,128)} %convolution_add_fusion.3.refs_0_, f32[256,1024]{1,0:T(8,128)} %bitcast_multiply_fusion.5.refs_1_, f32[256,32]{1,0:T(8,128)} %slice.226.refs_2_.refs_3_, f32[256,1]{1,0:T(8,128)} %copy.60.refs_3_.refs_4_, f32[16,1024]{1,0:T(8,128)} %get-tuple-element.152.refs_4_.refs_1_.refs_5_, ...), custom_call_target="tpu_custom_call" | custom-call | flops 11000000512 | tf_op jit(solution)/shard_map/scan_forward/pallas_call | solution.py:149
  125.4 16.7 %ch_reduce.4 = f32[256,2048]{1,0:T(8,128)S(1)} custom-call(bf16[256,2048]{1,0:T(8,128)(2,1)S(1)} %fusion.18.x_ref), custom_call_target="tpu_custom_call" | custom-call | flops 17999998976 | tf_op jit(solution)/shard_map/ch_reduce/pallas_call | solution.py:434
  158.5 6.9 ch_sum.5
  173.4 7.7 scan_back_local.2.refs_3_
  181.1 7.9 scan_local.3
  190.6 37.3 %carry_over.4 = (f32[2,16,1024]{2,1,0:T(8,128)S(1)}, f32[2,16,1024]{2,1,0:T(8,128)S(1)}) custom-call(f32[2,1024]{1,0:T(2,128)S(1)} %copy-done.17, f32[16,1024]{1,0:T(8,128)S(1)} %copy-done.6, f32[2,16,1024]{2,1,0:T(8,128)S(1)} %copy-done.10, f32[2,16,1024]{2,1,0:T(8,128)S(1)} %copy-done.9), custom_call_target="tpu_custom_call" | custom-call | flops 19000000512 | tf_op jit(solution)/shard_map/carry_over/pallas_call | solution.py:494
  229.3 11.1 %scan_forward.3 = f32[256,1024]{1,0:T(8,128)} custom-call(f32[256,1024]{1,0:T(8,128)} %convolution_add_fusion.2.refs_0_, f32[256,1024]{1,0:T(8,128)} %get-tuple-element.150.refs_1_, f32[256,32]{1,0:T(8,128)} %slice.247.refs_2_.refs_3_, f32[256,1]{1,0:T(8,128)} %copy.60.refs_3_.refs_4_, f32[16,1024]{1,0:T(8,128)} %get-tuple-element.151.refs_4_.refs_1_.refs_5_, ...), custom_call_target="tpu_custom_call" | custom-call | flops 11000000512 | tf_op jit(solution)/shard_map/scan_forward/pallas_call | solution.py:149
  244.8 23.2 %scan_back.2 = (f32[256,1024]{1,0:T(8,128)}, f32[256,1024]{1,0:T(8,128)}, f32[256,128]{1,0:T(8,128)}, f32[16,1024]{1,0:T(8,128)}) custom-call(f32[256,1024]{1,0:T(8,128)} %convolution_add_fusion.2.refs_0_, f32[256,1024]{1,0:T(8,128)} %get-tuple-element.150.refs_1_, f32[256,1024]{1,0:T(8,128)} %get-tuple-element.126.refs_1_.refs_2_, ...), custom_call_target="tpu_custom_call" | custom-call | flops 23000000512 | tf_op jit(solution)/shard_map/scan_back/pallas_call | solution.py:317
  270.5 7.0 ch_sum.6
  296.8 17.3 %ch_reduce.6 = f32[256,2048]{1,0:T(8,128)S(1)} custom-call(bf16[256,2048]{1,0:T(8,128)(2,1)S(1)} %fusion.25.x_ref), custom_call_target="tpu_custom_call" | custom-call | flops 17999998976 | tf_op jit(solution)/shard_map/ch_reduce/pallas_call | solution.py:434
  326.1 51.5 %all-reduce.17 = (bf16[512]{0:T(512)(128)(2,1)S(1)}, bf16[1024]{0:T(1024)(128)(2,1)S(1)}, bf16[1024]{0:T(1024)(128)(2,1)S(1)}, bf16[1024]{0:T(1024)(128)(2,1)S(1)}) all-reduce(bf16[512]{0:T(512)(128)(2,1)S(1)} %dynamic_slice.35, bf16[1024]{0:T(1024)(128)(2,1)S(1)} %get-tuple-element.180, ...), channel_id=1, replica_groups=mesh['seq'=8,'ch'=4] {'seq'}, use_global_device_ids=true, to_apply=%region_13.14 | all-reduce | flops 3584 | bytes 14336 | tf_op jit(solution)/shard_map/psum | solution.py:679
  384.2 7.8 scan_back_local.3.refs_2_
  392.8 25.6 %carry_over.5.refs_8_ = f32[2,16,1024]{2,1,0:T(8,128)S(1)} custom-call(f32[2,1024]{1,0:T(2,128)S(1)} %copy-done.16, f32[16,1024]{1,0:T(8,128)S(1)} %copy-done.5, f32[2,16,1024]{2,1,0:T(8,128)S(1)} %copy-done.7), custom_call_target="tpu_custom_call" | custom-call | flops 19000000512 | tf_op jit(solution)/shard_map/carry_over/pallas_call | solution.py:494
  419.1 23.1 %scan_back.3 = (f32[256,1024]{1,0:T(8,128)}, f32[256,1024]{1,0:T(8,128)}, f32[256,128]{1,0:T(8,128)}, f32[16,1024]{1,0:T(8,128)}) custom-call(f32[256,1024]{1,0:T(8,128)} %convolution_add_fusion.3.refs_0_, f32[256,1024]{1,0:T(8,128)} %bitcast_multiply_fusion.5.refs_1_, f32[256,1024]{1,0:T(8,128)} %get-tuple-element.124.refs_1_.refs_2_, ...), custom_call_target="tpu_custom_call" | custom-call | flops 23000000512 | tf_op jit(solution)/shard_map/scan_back/pallas_call | solution.py:317
  444.8 7.8 ch_sum.7
  479.1 16.9 %ch_reduce.7 = f32[256,2048]{1,0:T(8,128)S(1)} custom-call(bf16[256,2048]{1,0:T(8,128)(2,1)S(1)} %fusion.24.x_ref), custom_call_target="tpu_custom_call" | custom-call | flops 17999998976 | tf_op jit(solution)/shard_map/ch_reduce/pallas_call | solution.py:434
  504.7 10.6 %ch_reduce.5 = f32[256,512]{1,0:T(8,128)S(1)} custom-call(bf16[256,2048]{1,0:T(8,128)(2,1)S(1)} %fusion.21.x_ref), custom_call_target="tpu_custom_call" | custom-call | flops 17999998976 | tf_op jit(solution)/shard_map/ch_reduce/pallas_call | solution.py:434
  530.7 37.8 %all-gather.17.cloned.1.call-done = bf16[2048,1024]{1,0:T(8,128)(2,1)} async-done(((bf16[256,1024]{1,0:T(8,128)(2,1)}), bf16[2048,1024]{1,0:T(8,128)(2,1)}) %all-gather.17.cloned.1.call-update) | async-done | bytes 4194320 | tf_op jit(solution)/shard_map/all_gather | solution.py:534
  575.1 68.1 %all-reduce.22.cloned.1.call-done = (bf16[1,512]{1,0:T(2,128)(2,1)}, bf16[4,1024]{1,0:T(4,128)(2,1)}, bf16[1,4,1024]{2,1,0:T(4,128)(2,1)}, bf16[1,1024]{1,0:T(2,...) async-done(((bf16[1,512]{1,0:T(2,128)(2,1)}, bf16[4,1024]{1,0:T(4,128)(2,1)}, ...) | async-done | bytes 89104 | tf_op jit(solution)/shard_map/psum | solution.py:679
  652.0 76.3 %all-reduce.24.cloned.1.call-done = (bf16[1024,160]{0,1:T(8,128)(2,1)}, bf16[1,1024,160]{1,2,0:T(8,128)(2,1)}, bf16[128,1024]{1,0:T(8,128)(2,1)}, bf16[1,128,1024]{2,1,0:T(8,128)(2,1)}) async-done(((bf16[1024,160]{0,1:T(8,128)(2,1)}, bf16[1,1024,160]{1,2,0:T(8,128)(2,1)}, bf16[128,1024]{1,0:T(8,128)(2,1)}, bf16[1,128,1024]{2,1,0:T(8,128)(2,1)}), (bf16[1024,160]{0,1:T(8,128)(2,1)}, ...) | async-done | bytes 1179664 | tf_op jit(solution)/shard_map/psum | solution.py:679
  733.6 69.1 %all-gather.15.cloned.1.call-done = bf16[2048,1024]{1,0:T(8,128)(2,1)} async-done(((bf16[256,1024]{1,0:T(8,128)(2,1)}), bf16[2048,1024]{1,0:T(8,128)(2,1)}) %all-gather.15.cloned.1.call-update) | async-done | bytes 4194320 | tf_op jit(solution)/shard_map/all_gather | solution.py:534
  (373 shorter events, 216.3 us)
Async XLA Ops:
  28.0 19.9 %collective-permute-start = (f32[2,3,1024]{2,1,0:T(4,128)S(1)}, f32[2,3,1024]{2,1,0:T(4,128)S(1)}, u32[]{:S(2)}, u32[]{:S(2)}) collective-permute-start(f32[2,3,1024]{2,1,0:T(4,128)S(1)} %slice.262), channel_id=1, source_target_pairs={{0,4},{4,8},{8,12},{12,16},{16,20},{20,24},{24,28},{1,5},{5,9},{9,... | collective-permute-start | bytes 73736 | tf_op jit(solution)/shard_map/ppermute | solution.py:506
  31.6 15.4 %collective-permute-start.1 = (f32[2,3]{1,0:T(2,128)S(1)}, f32[2,3]{1,0:T(2,128)S(1)}, u32[]{:S(2)}, u32[]{:S(2)}) collective-permute-start(f32[2,3]{1,0:T(2,128)S(1)} %slice.213), channel_id=1, source_target_pairs={{0,4},{4,8},{8,12},{12,16},{16,20},{20,24},{24,28},{1,5},{5,9},{9,... | collective-permute-start | bytes 80 | tf_op jit(solution)/shard_map/ppermute | solution.py:506
  36.6 28.2 %all-to-all-start = ((bf16[256,8,256]{2,0,1:T(8,128)(2,1)}), bf16[256,8,256]{2,0,1:T(8,128)(2,1)}, u32[]{:S(2)}, u32[]{:S(2)}) async-start(bf16[256,8,256]{2,0,1:T(8,128)(2,1)} %copy.57), calls=%async_computation | async-start | bytes 2097152 | tf_op jit(solution)/shard_map/all_to_all | solution.py:539
  45.2 73.4 %copy-start.89 = (f32[1,1024]{1,0:T(1,128)}, f32[1,1024]{1,0:T(1,128)S(1)}, u32[]{:S(2)}) copy-start(f32[1,1024]{1,0:T(1,128)S(1)} %get-tuple-element.165.refs_6_) | copy-start | bytes 12292
  48.8 69.8 %copy-start.34 = (f32[2,128,1024]{2,1,0:T(8,128)}, f32[2,128,1024]{2,1,0:T(8,128)S(1)}, u32[]{:S(2)}) copy-start(f32[2,128,1024]{2,1,0:T(8,128)S(1)} %get-tuple-element.134) | copy-start | bytes 3145732
  64.8 41.8 %all-to-all-start.1 = ((bf16[256,8,256]{2,0,1:T(8,128)(2,1)}), bf16[256,8,256]{2,0,1:T(8,128)(2,1)S(1)}, u32[]{:S(2)}, u32[]{:S(2)}) async-start(bf16[256,8,256]{2,0,1:T(8,128)(2,1)} %fusion.27), calls=%async_computation.1 | async-start | bytes 2097152 | tf_op jit(solution)/shard_map/all_to_all | solution.py:539
  70.8 158.4 %all-gather.7.cloned.1.call-start = ((), (), s32[]{:S(2)}) async-start(), calls=%async_computation.4 | async-start | bytes 4718592 | tf_op jit(solution)/shard_map/all_gather | solution.py:534
  142.5 172.1 %copy-start.18 = (f32[256,2048]{1,0:T(8,128)}, f32[256,2048]{1,0:T(8,128)S(1)}, u32[]{:S(2)}) copy-start(f32[256,2048]{1,0:T(8,128)S(1)} %get-tuple-element.132) | copy-start | bytes 6291460
  145.9 11.1 %collective-permute-start.2 = (f32[2,3,1024]{2,1,0:T(4,128)S(1)}, f32[2,3,1024]{2,1,0:T(4,128)S(1)}, u32[]{:S(2)}, u32[]{:S(2)}) collective-permute-start(f32[2,3,1024]{2,1,0:T(4,128)S(1)} %slice.275), channel_id=1, source_target_pairs={{0,4},{4,8},{8,12},{12,16},{16,20},{20,24},{24,28},{1,5},{5,9},{9,... | collective-permute-start | bytes 73736 | tf_op jit(solution)/shard_map/ppermute | solution.py:506
  150.7 78.5 %all-to-all-start.2 = ((bf16[256,8,256]{2,0,1:T(8,128)(2,1)}), bf16[256,8,256]{2,0,1:T(8,128)(2,1)}, u32[]{:S(2)}, u32[]{:S(2)}) async-start(bf16[256,8,256]{2,0,1:T(8,128)(2,1)} %bitcast.303), calls=%async_computation.2 | async-start | bytes 2097152 | tf_op jit(solution)/shard_map/all_to_all | solution.py:539
  156.9 227.2 %all-gather.9.cloned.1.call-start = ((), (), s32[]{:S(2)}) async-start(), calls=%async_computation.5 | async-start | bytes 4718592 | tf_op jit(solution)/shard_map/all_gather | solution.py:534
  244.0 175.1 %all-gather.11.cloned.1.call-start = ((), (), s32[]{:S(2)}) async-start(), calls=%async_computation.6 | async-start | bytes 4718592 | tf_op jit(solution)/shard_map/all_gather | solution.py:534
  244.7 272.4 %all-gather.13.cloned.1.call-start = ((), (), s32[]{:S(2)}) async-start(), calls=%async_computation.7 | async-start | bytes 4718592 | tf_op jit(solution)/shard_map/all_gather | solution.py:534
  278.2 6.8 collective-permute-start.3
  318.4 59.3 %copy-start.35 = (f32[2,128,1024]{2,1,0:T(8,128)S(1)}, f32[2,128,1024]{2,1,0:T(8,128)}, u32[]{:S(2)}) copy-start(f32[2,128,1024]{2,1,0:T(8,128)} %copy-done.34) | copy-start | bytes 3145732
  318.4 59.3 %copy-start.90 = (f32[1,1024]{1,0:T(1,128)S(1)}, f32[1,1024]{1,0:T(1,128)}, u32[]{:S(2)}) copy-start(f32[1,1024]{1,0:T(1,128)} %copy-done.89) | copy-start | bytes 12292
  319.4 58.3 %copy-start.50 = (bf16[256,2048]{1,0:T(8,128)(2,1)S(1)}, bf16[256,2048]{1,0:T(8,128)(2,1)}, u32[]{:S(2)}) copy-start(bf16[256,2048]{1,0:T(8,128)(2,1)} %copy-done.49) | copy-start | bytes 3145732
  319.4 99.7 %all-to-all-start.3 = ((bf16[256,8,256]{2,0,1:T(8,128)(2,1)}), bf16[256,8,256]{2,0,1:T(8,128)(2,1)}, u32[]{:S(2)}, u32[]{:S(2)}) async-start(bf16[256,8,256]{2,0,1:T(8,128)(2,1)} %bitcast.286), calls=%async_computation.3 | async-start | bytes 2097152 | tf_op jit(solution)/shard_map/all_to_all | solution.py:539
  326.0 242.4 %all-gather.17.cloned.1.call-start = ((), (), s32[]{:S(2)}) async-start(), calls=%async_computation.9 | async-start | bytes 4718592 | tf_op jit(solution)/shard_map/all_gather | solution.py:534
  384.1 259.2 %all-reduce.22.cloned.1.call-start = ((), (), s32[]{:S(2)}) async-start(), calls=%async_computation.10 | async-start | bytes 192512 | tf_op jit(solution)/shard_map/psum | solution.py:679
  454.5 16.4 %collective-permute-start.4 = (f32[2,3,1024]{2,1,0:T(4,128)S(1)}, f32[2,3,1024]{2,1,0:T(4,128)S(1)}, u32[]{:S(2)}, u32[]{:S(2)}) collective-permute-start(f32[2,3,1024]{2,1,0:T(4,128)S(1)} %pad_add_fusion.2), channel_id=1, source_target_pairs={{4,0},{8,4},{12,8},{16,12},{20,16},{24,20},{28,24},{5,1},{9,5},{13... | collective-permute-start | bytes 73736 | tf_op jit(solution)/shard_map/ppermute | solution.py:506
  499.1 229.2 %all-reduce.24.cloned.1.call-start = ((), (), s32[]{:S(2)}) async-start(), calls=%async_computation.11 | async-start | bytes 2359296 | tf_op jit(solution)/shard_map/psum | solution.py:679
  500.1 302.6 %all-gather.15.cloned.1.call-start = ((), (), s32[]{:S(2)}) async-start(), calls=%async_computation.8 | async-start | bytes 4718592 | tf_op jit(solution)/shard_map/all_gather | solution.py:534
  733.6 72.6 %copy-start.61 = (f32[256,1,1024]{2,0,1:T(8,128)S(1)}, f32[256,1,1024]{2,0,1:T(8,128)}, u32[]{:S(2)}) copy-start(f32[256,1,1024]{2,0,1:T(8,128)} %convolution_bitcast_fusion.1) | copy-start | bytes 3145732
  (97 other events, 628.6 us)
Sparse Core Ops, SparseCore 0:
  121.7 103.3 all-gather.6
  244.1 73.4 all-gather.8
  320.3 96.3 all-gather.10
  418.6 75.4 all-gather.12
  496.1 72.3 all-gather.16
  573.8 69.3 all-reduce.21
  647.6 80.5 all-reduce.23
  730.6 72.1 all-gather.14

commit v3 on v2

--- a/solution.py
+++ b/solution.py
@@ -73,6 +73,7 @@
     length = rows // seqs
     spread_states(bc_ref, wide, pick, rows)
     prep(pre_ref, act_ref, keep_ref, dstep, dx, rows)
+    yield
     for gs in group_sets(channels, 8):
         a2 = [-jnp.exp(dl_ref[:, lanes(g)]) * LOG2E for g in gs]
         for s in range(seqs):
@@ -91,31 +92,90 @@
             st = lax.fori_loop(0, length // 8, blk, tuple(jnp.zeros((STATE, LANES), jnp.float32) for _ in gs))
             for k, g in enumerate(gs):
                 end_ref[s, :, lanes(g)] = st[k]
+            yield
 
 VM = pl.BlockSpec(memory_space=pltpu.VMEM)
 
-def scan_local(pre, act, bc, keep, dl, seqs, pins=()):
+
+def played(kernel, counts, plan, places):
+    n_in, n_out, n_scratch = counts
+
+    def run(*refs):
+        refs = list(refs)
+
+        def take(k):
+            head, refs[:] = refs[:k], refs[k:]
+            return head
+
+        own = take(n_in)
+        sources = take(len(plan))
+        own += take(n_out)
+        targets = take(len(plan))
+        own += take(n_scratch)
+        jobs = []
+        for (kind, when), src, out in zip(plan, sources, targets):
+            jobs.append((kind(*places, src, out, take(kind.semaphores)), when))
+        if plan:
+            seq, ch = lax.axis_index("seq"), lax.axis_index("ch")
+            zs, ys = places
+            z, y = seq // ys, lax.rem(seq, ys)
+            peers = [{"seq": lax.rem(z + d, zs) * ys + y} for d in range(1, zs)]
+            peers += [{"seq": z * ys + lax.rem(y + d, ys)} for d in range(1, ys)]
+            xs = lax.axis_size("ch") // 2
+            peers += [{"ch": lax.rem(ch // 2 + e, xs) * 2 + lax.rem(ch, 2)} for e in range(1, xs)]
+            peers.append({"ch": ch + 1 - 2 * lax.rem(ch, 2)})
+            barrier = pltpu.get_barrier_semaphore()
+            for peer in peers:
+                pl.semaphore_signal(barrier, inc=1, device_id=peer, device_id_type=MESH)
+        for at, _ in enumerate(kernel(*own)):
+            if at == 0 and plan:
+                pl.semaphore_wait(barrier, len(peers))
+                for job, _ in jobs:
+                    job.begin()
+            for job, when in jobs:
+                if at in when:
+                    job.step(when.index(at))
+        for job, when in jobs:
+            job.finish()
+
+    return run
+
+
+def play_call(kernel, counts, plan, places, cid, out_shape, scratch, arrays, us, name, pins=()):
+    arrays = list(arrays) + [v for _, _, v in plan]
+    kinds = [(kind, when) for kind, when, _ in plan]
+    out_shape = list(out_shape) + [kind.result(v, *places) for kind, _, v in plan]
+    sems = [spec for kind, _, v in plan for spec in kind.specs(v, *places)]
+    extra = dict(collective_id=cid, has_side_effects=True) if plan else {}
+    return pl.pallas_call(
+        after(played(kernel, counts, kinds, places), len(arrays), pins),
+        out_shape=out_shape,
+        in_specs=[VM] * len(arrays) + [ANY] * len(pins),
+        out_specs=[VM] * len(out_shape),
+        scratch_shapes=list(scratch) + sems,
+        compiler_params=pltpu.CompilerParams(vmem_limit_bytes=60 * 2**20, **extra),
+        cost_estimate=cost(us),
+        name=name,
+    )(*arrays, *pins)
+
+def scan_local(pre, act, bc, keep, dl, seqs, plan, places, cid):
     rows, channels = pre.shape
     f = jnp.float32
-    return pl.pallas_call(
-        after(functools.partial(local_kernel, seqs), 5, pins),
-        out_shape=[
-            jax.ShapeDtypeStruct((seqs, STATE, channels), f),
-            jax.ShapeDtypeStruct((seqs, channels), f),
-        ],
-        in_specs=[VM] * 5 + [ANY] * len(pins), out_specs=[VM] * 2,
-        scratch_shapes=[pltpu.VMEM((rows * STATE, 2 * LANES), f), pltpu.VMEM((32 * STATE, 2 * STATE), jnp.bfloat16),
-                        pltpu.VMEM((channels // LANES, rows, LANES), f), pltpu.VMEM((channels // LANES, rows, LANES), f)],
-        compiler_params=pltpu.CompilerParams(vmem_limit_bytes=60 * 2**20),
-        cost_estimate=cost(8),
-        name="scan_local",
-    )(pre, act, bc, keep, dl, *pins)
+    big = pltpu.VMEM((channels // LANES, rows, LANES), f)
+    return play_call(
+        functools.partial(local_kernel, seqs), (5, 2, 4), plan, places, cid,
+        [jax.ShapeDtypeStruct((seqs, STATE, channels), f), jax.ShapeDtypeStruct((seqs, channels), f)],
+        [pltpu.VMEM((rows * STATE, 2 * LANES), f), pltpu.VMEM((32 * STATE, 2 * STATE), jnp.bfloat16), big, big],
+        (pre, act, bc, keep, dl), 8, "scan_local",
+    )
+
 
 def forward_kernel(seqs, pre_ref, act_ref, bc_ref, keep_ref, dl_ref, in_ref, y_ref, wide, pick, dstep, dx, part):
     rows, channels = pre_ref.shape
     length = rows // seqs
     spread_states(bc_ref, wide, pick, rows)
     prep(pre_ref, act_ref, keep_ref, dstep, dx, rows)
+    yield
     for gs in group_sets(channels, 4):
         a2 = [-jnp.exp(dl_ref[:, lanes(g)]) * LOG2E for g in gs]
         for s in range(seqs):
@@ -142,21 +202,20 @@
                     y_ref[pl.ds(t0, 8), lanes(g)] = acc
                 return 0
             lax.fori_loop(0, length // 8, red, 0)
-
-def scan_forward(pre, act, bc, keep, dl, state_in, seqs, pins=()):
+            yield
+
+def scan_forward(pre, act, bc, keep, dl, state_in, seqs, plan, places, cid):
     rows, channels = pre.shape
     f = jnp.float32
-    return pl.pallas_call(
-        after(functools.partial(forward_kernel, seqs), 6, pins),
-        out_shape=jax.ShapeDtypeStruct((rows, channels), f),
-        in_specs=[VM] * 6 + [ANY] * len(pins), out_specs=VM,
-        scratch_shapes=[pltpu.VMEM((rows * STATE, 2 * LANES), f), pltpu.VMEM((32 * STATE, 2 * STATE), jnp.bfloat16),
-                        pltpu.VMEM((channels // LANES, rows, LANES), f), pltpu.VMEM((channels // LANES, rows, LANES), f),
-                        pltpu.VMEM((4, rows // seqs * 8, LANES), f)],
-        compiler_params=pltpu.CompilerParams(vmem_limit_bytes=60 * 2**20),
-        cost_estimate=cost(11),
-        name="scan_forward",
-    )(pre, act, bc, keep, dl, state_in, *pins)
+    big = pltpu.VMEM((channels // LANES, rows, LANES), f)
+    return play_call(
+        functools.partial(forward_kernel, seqs), (6, 1, 5), plan, places, cid,
+        [jax.ShapeDtypeStruct((rows, channels), f)],
+        [pltpu.VMEM((rows * STATE, 2 * LANES), f), pltpu.VMEM((32 * STATE, 2 * STATE), jnp.bfloat16), big, big,
+         pltpu.VMEM((4, rows // seqs * 8, LANES), f)],
+        (pre, act, bc, keep, dl, state_in), 11, "scan_forward",
+    )
+
 
 LN2 = 0.6931471805599453
 
@@ -202,9 +261,11 @@
         name="scan_back_local",
     )(pre, gs, bc, keep, dl, *pins)
 
-def back_kernel(seqs, pre_ref, act_ref, gs_ref, bc_ref, keep_ref, dl_ref, skip_ref, in_ref, lam_ref,
-                gpre_ref, gact_ref, gbc_ref, gdl_ref,
-                wide, pick, dstep, dx, stepc, gsc, states, partq, partr, accb, accc, rowsum):
+def back_kernel(seqs, with_y, pre_ref, act_ref, gs_ref, bc_ref, keep_ref, dl_ref, skip_ref, in_ref, lam_ref,
+                gpre_ref, gact_ref, gbc_ref, gdl_ref, *rest):
+    if with_y:
+        y_ref, *rest = rest
+    (wide, pick, dstep, dx, stepc, gsc, states, partq, partr, accb, accc, rowsum) = rest
     rows, channels = pre_ref.shape
     length = rows // seqs
     f = jnp.float32
@@ -219,6 +280,7 @@
             gsc[g, sl, :] = gs_ref[sl, lanes(g)]
         return 0
     lax.fori_loop(0, rows // 32, body, 0)
+    yield
     sets = group_sets(channels, 4)
     for index, gs in enumerate(sets):
         a2 = [-jnp.exp(dl_ref[:, lanes(g)]) * LOG2E for g in gs]
@@ -230,13 +292,30 @@
                 st = list(st)
                 t0 = pl.multiple_of(s * length + i * 8, 8)
                 for j in range(8):
-                    b = wide[pl.ds(pl.multiple_of((t0 + j) * STATE, STATE), STATE), pl.ds(0, LANES)]
+                    at = pl.ds(pl.multiple_of((t0 + j) * STATE, STATE), STATE)
+                    b = wide[at, pl.ds(0, LANES)]
+                    if with_y:
+                        c = wide[at, pl.ds(LANES, LANES)]
                     for k, g in enumerate(gs):
                         d = jnp.exp2(a2[k] * dstep[g, pl.ds(t0 + j, 1), :])
                         st[k] = d * st[k] + b * dx[g, pl.ds(t0 + j, 1), :]
                         states[k, pl.ds(pl.multiple_of((i * 8 + j + 1) * STATE, STATE), STATE), :] = st[k]
+                        if with_y:
+                            v = st[k] * c
+                            partq[k, pl.ds(pl.multiple_of(i * 64 + j * 8, 8), 8), :] = v[:8] + v[8:]
                 return tuple(st)
             lax.fori_loop(0, length // 8, fwd, tuple(in_ref[s, :, lanes(g)] for g in gs))
+            if with_y:
+                def read(i, _):
+                    t0 = pl.multiple_of(s * length + i * 8, 8)
+                    for k, g in enumerate(gs):
+                        acc = partq[k, pl.ds(i * 64, 8, stride=8), :]
+                        for m in range(1, 8):
+                            acc = acc + partq[k, pl.ds(i * 64 + m, 8, stride=8), :]
+                        y_ref[pl.ds(t0, 8), lanes(g)] = acc
+                    return 0
+                lax.fori_loop(0, length // 8, read, 0)
+            yield
             def bwd(i, carry):
                 st = list(carry[:len(gs)])
                 am = list(carry[len(gs):])
@@ -289,6 +368,7 @@
                     gact_ref[here, lanes(g)] = stepc[g, here, :] * q + gsc[g, here, :] * skip_ref[:, lanes(g)]
                 return 0
             lax.fori_loop(0, length // 8, red, 0)
+            yield
         for k, g in enumerate(gs):
             gdl_ref[:, lanes(g)] = gdl[k] * (a2[k] * LN2)
     ones = jnp.ones((LANES, LANES), jnp.bfloat16)
@@ -308,27 +388,24 @@
         return 0
     lax.fori_loop(0, rows // 32, fin, 0)
 
-def scan_back(pre, act, gs, bc, keep, dl, skip, state_in, lam_in, seqs, pins=()):
+def scan_back(pre, act, gs, bc, keep, dl, skip, state_in, lam_in, seqs, with_y, plan, places, cid, pins=()):
     rows, channels = pre.shape
     f = jnp.float32
     groups = channels // LANES
     length = rows // seqs
     big = pltpu.VMEM((groups, rows, LANES), f)
-    return pl.pallas_call(
-        after(functools.partial(back_kernel, seqs), 9, pins),
-        out_shape=[jax.ShapeDtypeStruct((rows, channels), f), jax.ShapeDtypeStruct((rows, channels), f),
-                   jax.ShapeDtypeStruct((rows, LANES), f), jax.ShapeDtypeStruct((STATE, channels), f)],
-        in_specs=[VM] * 9 + [ANY] * len(pins), out_specs=[VM] * 4,
-        scratch_shapes=[pltpu.VMEM((rows * STATE, 2 * LANES), f), pltpu.VMEM((32 * STATE, 2 * STATE), jnp.bfloat16),
-                        big, big, big, big,
-                        pltpu.VMEM((4, (length + 1) * STATE, LANES), f),
-                        pltpu.VMEM((4, length * 8, LANES), f), pltpu.VMEM((4, length * 8, LANES), f),
-                        pltpu.VMEM((rows * STATE, LANES), f), pltpu.VMEM((rows * STATE, LANES), f),
-                        pltpu.VMEM((32 * STATE, LANES), f)],
-        compiler_params=pltpu.CompilerParams(vmem_limit_bytes=60 * 2**20),
-        cost_estimate=cost(23),
-        name="scan_back",
-    )(pre, act, gs, bc, keep, dl, skip, state_in, lam_in, *pins)
+    whole = jax.ShapeDtypeStruct((rows, channels), f)
+    return play_call(
+        functools.partial(back_kernel, seqs, with_y), (9, 4 + with_y, 12), plan, places, cid,
+        [whole, whole, jax.ShapeDtypeStruct((rows, LANES), f), jax.ShapeDtypeStruct((STATE, channels), f)] + [whole] * with_y,
+        [pltpu.VMEM((rows * STATE, 2 * LANES), f), pltpu.VMEM((32 * STATE, 2 * STATE), jnp.bfloat16),
+         big, big, big, big,
+         pltpu.VMEM((4, (length + 1) * STATE, LANES), f),
+         pltpu.VMEM((4, length * 8, LANES), f), pltpu.VMEM((4, length * 8, LANES), f),
+         pltpu.VMEM((rows * STATE, LANES), f), pltpu.VMEM((rows * STATE, LANES), f),
+         pltpu.VMEM((32 * STATE, LANES), f)],
+        (pre, act, gs, bc, keep, dl, skip, state_in, lam_in), 23 + 3 * with_y, "scan_back", pins,
+    )
 
 
 def greet(peers):
@@ -353,21 +430,21 @@
         total = total + slots[d - 1].astype(f32)
     out_ref[...] = total
 
-def ch_sum(x, n, cid):
+def ch_sum(x, n, cid, pins=()):
     return pl.pallas_call(
-        functools.partial(ch_sum_kernel, n),
-        out_shape=jax.ShapeDtypeStruct(x.shape, f32), in_specs=[VM], out_specs=VM,
+        after(functools.partial(ch_sum_kernel, n), 1, pins),
+        out_shape=jax.ShapeDtypeStruct(x.shape, f32), in_specs=[VM] + [ANY] * len(pins), out_specs=VM,
         scratch_shapes=[pltpu.VMEM(x.shape, bf16), pltpu.VMEM((n - 1,) + x.shape, bf16), pltpu.SemaphoreType.DMA((n - 1,)), pltpu.SemaphoreType.DMA((n - 1,))],
         compiler_params=pltpu.CompilerParams(collective_id=cid, has_side_effects=True, vmem_limit_bytes=32 * 2**20), cost_estimate=cost(10), name="ch_sum",
-    )(x)
-
-def reduce_kernel(n, parts, gather, x_ref, out_ref, s1, sum1, s2, mine, got, fin, sem1, rem1, sem2, rem2, sem3, rem3, sem4, rem4):
+    )(x, *pins)
+
+def reduce_steps(n, parts, gather, more, x_ref, out_ref, s1, sum1, s2, mine, got, fin, sem1, rem1, sem2, rem2, sem3, rem3, sem4, rem4):
     xs = n // 2
     me = lax.axis_index("ch")
     x, core = me // 2, lax.rem(me, 2)
     peer = {"ch": x * 2 + 1 - core}
     others = [lax.rem(x + d, xs) for d in range(1, xs)]
-    greet([peer] + [{"ch": o * 2 + core} for o in others])
+    greet([peer] + [{"ch": o * 2 + core} for o in others] + more)
     rows, width = x_ref.shape[0] // parts, x_ref.shape[1] // n
     def cols(block):
         return pl.ds(pl.multiple_of(block * width, width), width)
@@ -382,12 +459,14 @@
     for p in range(parts):
         for k in range(xs):
             stage1(p, k).start()
+    yield
     for p in range(parts):
         for k in range(xs):
             stage1(p, k).wait_recv()
             sum1[p, k] = (x_ref[pl.ds(p * rows, rows), cols(k * 2 + core)].astype(f32) + s1[p, k].astype(f32)).astype(bf16)
         for d in range(xs - 1):
             stage2(p, d).start()
+    yield
     for p in range(parts):
         total = sum1[p, x].astype(f32)
         for d in range(xs - 1):
@@ -399,6 +478,7 @@
                 stage3(p, d).start()
         else:
             out_ref[pl.ds(p * rows, rows), :] = total
+    yield
     if gather:
         def stage4(p, d):
             src = mine.at[p] if d < 0 else got.at[p, d]
@@ -412,6 +492,7 @@
                 stage3(p, d).wait_recv()
                 stage4(p, d).start()
                 out_ref[pl.ds(p * rows, rows), cols(chip(d) * 2 + core)] = got[p, d].astype(out_ref.dtype)
+        yield
         for p in range(parts):
             for d in range(-1, xs - 1):
                 stage4(p, d).wait_recv()
@@ -426,18 +507,117 @@
         if gather:
             for d in range(-1, xs - 1):
                 stage4(p, d).wait_send()
-
-def ch_reduce(x, n, cid, gather, parts=2, out_dtype=f32):
-    rows, width = x.shape
+    yield
+
+
+class ColumnsLine:
+    semaphores = 6
+
+    @staticmethod
+    def result(v, zs, ys):
+        return jax.ShapeDtypeStruct((zs * v.shape[0], v.shape[1] // zs), v.dtype)
+
+    @staticmethod
+    def specs(v, zs, ys):
+        sem = pltpu.SemaphoreType.DMA
+        xs = lax.axis_size("ch") // 2
+        return [sem((zs - 1,))] * 2 + [sem((zs - 1, xs - 1))] * 2 + [sem((zs - 1, xs))] * 2
+
+    def __init__(self, zs, ys, src, out, sems):
+        seq, ch = lax.axis_index("seq"), lax.axis_index("ch")
+        self.nch = lax.axis_size("ch")
+        self.xs = self.nch // 2
+        self.zs, self.ys, self.z, self.y, self.ch = zs, ys, seq // ys, lax.rem(seq, ys), ch
+        self.x, self.core = ch // 2, lax.rem(ch, 2)
+        self.src, self.out, self.sems = src, out, sems
+        self.rows, self.width = src.shape[0], src.shape[1] // zs
+        self.part = self.rows // self.nch
+
+    def cols(self, z):
+        return pl.ds(pl.multiple_of(z * self.width, self.width), self.width)
+
+    def share(self, z, ch):
+        return pl.ds(pl.multiple_of(z * self.rows + ch * self.part, self.part), self.part)
+
+    def remote(self, k, at, src, dst, to):
+        send, recv = self.sems[2 * k : 2 * k + 2]
+        return pltpu.make_async_remote_copy(src_ref=src, dst_ref=dst, send_sem=send.at[at], recv_sem=recv.at[at], device_id=to, device_id_type=MESH)
+
+    def along(self, d):
+        to = lax.rem(self.z + d, self.zs)
+        src = self.src.at[pl.ds(pl.multiple_of(self.ch * self.part, self.part), self.part), self.cols(to)]
+        return self.remote(0, d - 1, src, self.out.at[self.share(self.z, self.ch)], {"seq": to * self.ys + self.y})
+
+    def from_z(self, d):
+        return lax.rem(self.z + self.zs - d, self.zs)
+
+    def over(self, d, e):
+        rows = self.out.at[self.share(self.from_z(d), self.ch)]
+        return self.remote(1, (d - 1, e - 1), rows, rows, {"ch": lax.rem(self.x + e, self.xs) * 2 + self.core})
+
+    def across(self, d, e):
+        rows = self.out.at[self.share(self.from_z(d), lax.rem(self.x + self.xs - e, self.xs) * 2 + self.core)]
+        return self.remote(2, (d - 1, e), rows, rows, {"ch": self.x * 2 + 1 - self.core})
+
+    def lags(self):
+        return range(1, self.zs)
+
+    def begin(self):
+        for d in self.lags():
+            self.along(d).start()
+        here = pl.ds(pl.multiple_of(self.z * self.rows, self.rows), self.rows)
+        self.out[here, :] = self.src[:, self.cols(self.z)]
+
+    def step(self, index):
+        for d in self.lags():
+            if index == 0:
+                self.along(d).wait_recv()
+                for e in range(1, self.xs):
+                    self.over(d, e).start()
+                self.across(d, 0).start()
+            else:
+                for e in range(1, self.xs):
+                    self.over(d, e).wait_recv()
+                    self.across(d, e).start()
+
+    def finish(self):
+        for d in self.lags():
+            for e in range(self.xs):
+                self.across(d, e).wait_recv()
+        for d in self.lags():
+            self.along(d).wait_send()
+            for e in range(1, self.xs):
+                self.over(d, e).wait_send()
+            for e in range(self.xs):
+                self.across(d, e).wait_send()
+
+
+def reduce_kernel(n, parts, gather, *refs):
+    for _ in reduce_steps(n, parts, gather, [], *refs):
+        pass
+
+
+def reduce_scratch_shapes(shape, n, parts):
+    rows, width = shape
     xs, r, w = n // 2, rows // parts, width // n
     sem = pltpu.SemaphoreType.DMA
+    return [
+        pltpu.VMEM((parts, xs, r, w), bf16), pltpu.VMEM((parts, xs, r, w), bf16), pltpu.VMEM((parts, xs - 1, r, w), bf16),
+        pltpu.VMEM((parts, r, w), bf16), pltpu.VMEM((parts, xs - 1, r, w), bf16), pltpu.VMEM((parts, xs, r, w), bf16),
+        sem((parts, xs)), sem((parts, xs)), sem((parts, xs - 1)), sem((parts, xs - 1)),
+        sem((parts, xs - 1)), sem((parts, xs - 1)), sem((parts, xs)), sem((parts, xs)),
+    ]
+
+
+def ch_reduce(x, n, cid, gather, parts=2):
+    rows, width = x.shape
     return pl.pallas_call(
         functools.partial(reduce_kernel, n, parts, gather),
-        out_shape=jax.ShapeDtypeStruct((rows, width if gather else w), out_dtype), in_specs=[VM], out_specs=VM,
-        scratch_shapes=[pltpu.VMEM((parts, xs, r, w), bf16), pltpu.VMEM((parts, xs, r, w), bf16), pltpu.VMEM((parts, xs - 1, r, w), bf16),
-                        pltpu.VMEM((parts, r, w), bf16), pltpu.VMEM((parts, xs - 1, r, w), bf16), pltpu.VMEM((parts, xs, r, w), bf16),
-                        sem((parts, xs)), sem((parts, xs)), sem((parts, xs - 1)), sem((parts, xs - 1)), sem((parts, xs - 1)), sem((parts, xs - 1)), sem((parts, xs)), sem((parts, xs))],
-        compiler_params=pltpu.CompilerParams(collective_id=cid, has_side_effects=True, vmem_limit_bytes=48 * 2**20), cost_estimate=cost(18), name="ch_reduce",
+        out_shape=jax.ShapeDtypeStruct((rows, width if gather else width // n), f32),
+        in_specs=[VM], out_specs=VM,
+        scratch_shapes=reduce_scratch_shapes(x.shape, n, parts),
+        compiler_params=pltpu.CompilerParams(collective_id=cid, has_side_effects=True, vmem_limit_bytes=48 * 2**20),
+        cost_estimate=cost(18), name="ch_reduce",
     )(x)
 
 
@@ -500,6 +680,336 @@
     )(tot, dl, *ends)
 
 
+def seq_at(z, y, ys):
+    return {"seq": z * ys + y}
+
+
+class GatherLine:
+    semaphores = 2
+
+    @staticmethod
+    def result(v, zs, ys):
+        return jax.ShapeDtypeStruct((zs * v.shape[0], v.shape[1]), v.dtype)
+
+    @staticmethod
+    def specs(v, zs, ys):
+        return [pltpu.SemaphoreType.DMA((2, zs - 1))] * 2
+
+
+    def __init__(self, zs, ys, src, out, sems):
+        me = lax.axis_index("seq")
+        self.zs, self.ys, self.z, self.y = zs, ys, me // ys, lax.rem(me, ys)
+        self.src, self.out = src, out
+        self.send, self.recv = sems
+        self.rows = src.shape[0]
+
+    def block(self, z):
+        return self.out.at[pl.ds(pl.multiple_of(z * self.rows, self.rows), self.rows)]
+
+    def copy(self, way, r):
+        z = self.z
+        to, b = (lax.rem(z + 1, self.zs), z - r) if way == 0 else (lax.rem(z + self.zs - 1, self.zs), z + r)
+        b = lax.rem(b + self.zs, self.zs)
+        return pltpu.make_async_remote_copy(
+            src_ref=self.src if r == 0 else self.block(b),
+            dst_ref=self.block(b),
+            send_sem=self.send.at[way, r],
+            recv_sem=self.recv.at[way, r],
+            device_id=seq_at(to, self.y, self.ys),
+            device_id_type=MESH,
+        )
+
+    def sends(self, way, r):
+        z, last = self.z, self.zs - 1
+        return jnp.logical_and(z < last, z >= r) if way == 0 else jnp.logical_and(z > 0, z + r <= last)
+
+    def receives(self, way, r):
+        z, last = self.z, self.zs - 1
+        return z - 1 - r >= 0 if way == 0 else z + 1 + r <= last
+
+    def begin(self):
+        self.start(0)
+        self.block(self.z)[...] = self.src[...]
+
+    def step(self, index):
+        self.start(index + 1)
+
+    def start(self, r):
+        for way in (0, 1):
+            if r > 0:
+                self.arrive(way, r - 1)
+            @pl.when(self.sends(way, r))
+            def _():
+                self.copy(way, r).start()
+
+    def arrive(self, way, r):
+        @pl.when(self.receives(way, r))
+        def _():
+            self.copy(way, r).wait_recv()
+
+    def finish(self):
+        for way in (0, 1):
+            self.arrive(way, self.zs - 2)
+        for way in (0, 1):
+            for r in range(self.zs - 1):
+                @pl.when(self.sends(way, r))
+                def _():
+                    self.copy(way, r).wait_send()
+
+
+class SumAll:
+    def __init__(self, zs, ys, src, out, yslots, ysum, zslots, sems):
+        me = lax.axis_index("seq")
+        self.zs, self.ys, self.z, self.y = zs, ys, me // ys, lax.rem(me, ys)
+        self.src, self.out, self.yslots, self.ysum, self.zslots = src, out, yslots, ysum, zslots
+        self.sems = sems
+        self.part = src.shape[0] // ys
+        self.share = self.part // zs
+
+    def remote(self, k, i, src, dst, to):
+        send, recv = self.sems[2 * k : 2 * k + 2]
+        return pltpu.make_async_remote_copy(src_ref=src, dst_ref=dst, send_sem=send.at[i], recv_sem=recv.at[i], device_id=to, device_id_type=MESH)
+
+    def rows(self, index, size):
+        return pl.ds(pl.multiple_of(index * size, size), size)
+
+    def y1(self, d):
+        to = lax.rem(self.y + d, self.ys)
+        return self.remote(0, d - 1, self.src.at[self.rows(to, self.part)], self.yslots.at[d - 1], seq_at(self.z, to, self.ys))
+
+    def z1(self, d):
+        to = lax.rem(self.z + d, self.zs)
+        return self.remote(1, d - 1, self.ysum.at[self.rows(to, self.share)], self.zslots.at[d - 1], seq_at(to, self.y, self.ys))
+
+    def mine(self, z):
+        return self.out.at[self.rows(self.y * self.zs + z, self.share)]
+
+    def z2(self, d):
+        to = lax.rem(self.z + d, self.zs)
+        return self.remote(2, d - 1, self.mine(self.z), self.mine(self.z), seq_at(to, self.y, self.ys))
+
+    def y2(self, d, e):
+        to = lax.rem(self.y + d, self.ys)
+        share = self.mine(lax.rem(self.z - e + self.zs, self.zs))
+        return self.remote(3, (d - 1) * self.zs + e, share, share, seq_at(self.z, to, self.ys))
+
+    def begin(self):
+        for d in range(1, self.ys):
+            self.y1(d).start()
+
+    def middle(self):
+        total = self.src[self.rows(self.y, self.part), :].astype(f32)
+        for d in range(1, self.ys):
+            self.y1(d).wait_recv()
+            total = total + self.yslots[d - 1].astype(f32)
+        self.ysum[...] = total.astype(bf16)
+        for d in range(1, self.zs):
+            self.z1(d).start()
+
+    def gather(self):
+        total = self.ysum[self.rows(self.z, self.share), :].astype(f32)
+        for d in range(1, self.zs):
+            self.z1(d).wait_recv()
+            total = total + self.zslots[d - 1].astype(f32)
+        self.mine(self.z)[...] = total.astype(bf16)
+        for d in range(1, self.zs):
+            self.z2(d).start()
+        for d in range(1, self.ys):
+            self.y2(d, 0).start()
+
+    def spread(self):
+        for e in range(1, self.zs):
+            self.z2(e).wait_recv()
+            for d in range(1, self.ys):
+                self.y2(d, e).start()
+
+    def finish(self):
+        for d in range(1, self.ys):
+            for e in range(self.zs):
+                self.y2(d, e).wait_recv()
+        for d in range(1, self.ys):
+            self.y1(d).wait_send()
+            for e in range(self.zs):
+                self.y2(d, e).wait_send()
+        for d in range(1, self.zs):
+            self.z1(d).wait_send()
+            self.z2(d).wait_send()
+
+
+class PartSum:
+    semaphores = 3
+
+    @staticmethod
+    def result(v, zs, ys):
+        return jax.ShapeDtypeStruct(v.shape[1:], f32)
+
+    @staticmethod
+    def specs(v, zs, ys):
+        sem = pltpu.SemaphoreType.DMA((ys - 1,))
+        return [sem, sem, pltpu.VMEM((ys - 1,) + v.shape[1:], v.dtype)]
+
+
+    def __init__(self, zs, ys, src, out, scratch):
+        me = lax.axis_index("seq")
+        self.ys, self.z, self.y = ys, me // ys, lax.rem(me, ys)
+        self.src, self.out = src, out
+        self.send, self.recv, self.slots = scratch
+
+    def copy(self, d):
+        to = lax.rem(self.y + d, self.ys)
+        return pltpu.make_async_remote_copy(
+            src_ref=self.src.at[to],
+            dst_ref=self.slots.at[d - 1],
+            send_sem=self.send.at[d - 1],
+            recv_sem=self.recv.at[d - 1],
+            device_id=seq_at(self.z, to, self.ys),
+            device_id_type=MESH,
+        )
+
+    def begin(self):
+        for d in range(1, self.ys):
+            self.copy(d).start()
+
+    def finish(self):
+        mine = self.src[self.y].astype(f32)
+        for d in range(1, self.ys):
+            self.copy(d).wait_recv()
+            mine = mine + self.slots[d - 1].astype(f32)
+        self.out[...] = mine
+        for d in range(1, self.ys):
+            self.copy(d).wait_send()
+
+
+def closing_kernel(n, zs, ys, parts, count, pieces, x_ref, v_ref, *refs):
+    piece_refs, refs = refs[:pieces], refs[pieces:]
+    p_refs, refs = refs[:count], refs[count:]
+    out_ref, all_ref, sum_ref, *refs = refs
+    part_refs, refs = refs[:count], refs[count:]
+    s_ref, *refs = refs
+    reduce_scratch, scratch = refs[:14], refs[14:]
+    yslots, ysum, zslots, gsend, grecv = scratch[:5]
+    seq = lax.axis_index("seq")
+    z, y = seq // ys, lax.rem(seq, ys)
+    line = GatherLine(zs, ys, v_ref, all_ref, (gsend, grecv))
+    total = SumAll(zs, ys, s_ref, sum_ref, yslots, ysum, zslots, scratch[5:13])
+    sums = [PartSum(zs, ys, p_refs[k], part_refs[k], scratch[13 + 3 * k : 16 + 3 * k]) for k in range(count)]
+    peers = [seq_at(z, lax.rem(y + d, ys), ys) for d in range(1, ys)]
+    peers += [seq_at(lax.rem(z + d, zs), y, ys) for d in range(1, zs)]
+    steps = reduce_steps(n, parts, False, peers, x_ref, out_ref, *reduce_scratch)
+    next(steps)
+    offset = 0
+    for piece in piece_refs:
+        s_ref[pl.ds(offset, piece.shape[0]), :] = piece[...].astype(bf16)
+        offset += piece.shape[0]
+    if offset < s_ref.shape[0]:
+        s_ref[pl.ds(offset, s_ref.shape[0] - offset), :] = jnp.zeros((s_ref.shape[0] - offset, s_ref.shape[1]), bf16)
+    line.start(0)
+    total.begin()
+    for part in sums:
+        part.begin()
+    all_ref[pl.ds(pl.multiple_of(z * line.rows, line.rows), line.rows), :] = v_ref[...]
+    next(steps)
+    total.middle()
+    next(steps)
+    line.start(1)
+    for _ in steps:
+        pass
+    total.gather()
+    for r in range(2, zs - 1):
+        line.start(r)
+    for part in sums[:-1]:
+        part.finish()
+    total.spread()
+    for part in sums[-1:]:
+        part.finish()
+    line.finish()
+    total.finish()
+
+
+def closing(x, v, pieces, ps, n, zs, ys, cid, parts=2):
+    rows, width = x.shape
+    sem = pltpu.SemaphoreType.DMA
+    height = sum(piece.shape[0] for piece in pieces)
+    height += -height % (16 * ys * zs)
+    part = height // ys
+    w = v.shape[1]
+    count = len(ps)
+    return pl.pallas_call(
+        functools.partial(closing_kernel, n, zs, ys, parts, count, len(pieces)),
+        out_shape=[
+            jax.ShapeDtypeStruct((rows, width // n), f32),
+            jax.ShapeDtypeStruct((zs * v.shape[0], v.shape[1]), bf16),
+            jax.ShapeDtypeStruct((height, w), bf16),
+        ]
+        + [PartSum.result(p, zs, ys) for p in ps],
+        in_specs=[VM] * (2 + len(pieces) + count),
+        out_specs=[VM] * (3 + count),
+        scratch_shapes=[pltpu.VMEM((height, w), bf16)] + reduce_scratch_shapes(x.shape, n, parts)
+        + [
+            pltpu.VMEM((ys - 1, part, w), bf16),
+            pltpu.VMEM((part, w), bf16),
+            pltpu.VMEM((zs - 1, part // zs, w), bf16),
+        ]
+        + [sem((2, zs - 1))] * 2
+        + [sem((ys - 1,))] * 2
+        + [sem((zs - 1,))] * 4
+        + [sem(((ys - 1) * zs,))] * 2
+        + [spec for p in ps for spec in PartSum.specs(p, zs, ys)],
+        compiler_params=pltpu.CompilerParams(collective_id=cid, has_side_effects=True, vmem_limit_bytes=58 * 2**20),
+        cost_estimate=cost(70),
+        name="closing",
+    )(x, v, *pieces, *ps)
+
+
+def last_kernel(n, zs, ys, p_ref, t_ref, out_ref, sum_ref, pslots, tslots, psend, precv, tsend, trecv):
+    me = lax.axis_index("seq")
+    z, y = me // ys, lax.rem(me, ys)
+    greet([{"seq": lax.rem(me + d, n)} for d in range(1, n)])
+    def part(d):
+        to = lax.rem(y + d, ys)
+        return pltpu.make_async_remote_copy(src_ref=p_ref.at[to], dst_ref=pslots.at[d - 1], send_sem=psend.at[d - 1], recv_sem=precv.at[d - 1], device_id=seq_at(z, to, ys), device_id_type=MESH)
+    def tiny(d):
+        return pltpu.make_async_remote_copy(src_ref=t_ref, dst_ref=tslots.at[lax.rem(me, n)], send_sem=tsend.at[d - 1], recv_sem=trecv.at[d - 1], device_id={"seq": lax.rem(me + d, n)}, device_id_type=MESH)
+    for d in range(1, n):
+        tiny(d).start()
+    for d in range(1, ys):
+        part(d).start()
+    tslots[me] = t_ref[...]
+    for d in range(1, n):
+        tiny(d).wait_recv()
+    total = tslots[0].astype(f32)
+    for k in range(1, n):
+        total = total + tslots[k].astype(f32)
+    sum_ref[...] = total
+    mine = p_ref[y].astype(f32)
+    for d in range(1, ys):
+        part(d).wait_recv()
+        mine = mine + pslots[d - 1].astype(f32)
+    out_ref[...] = mine
+    for d in range(1, n):
+        tiny(d).wait_send()
+    for d in range(1, ys):
+        part(d).wait_send()
+
+
+def last_sums(p, t, n, zs, ys, cid):
+    sem = pltpu.SemaphoreType.DMA
+    return pl.pallas_call(
+        functools.partial(last_kernel, n, zs, ys),
+        out_shape=[jax.ShapeDtypeStruct(p.shape[1:], f32), jax.ShapeDtypeStruct(t.shape, f32)],
+        in_specs=[VM] * 2,
+        out_specs=[VM] * 2,
+        scratch_shapes=[
+            pltpu.VMEM((ys - 1,) + p.shape[1:], bf16),
+            pltpu.VMEM((n,) + t.shape, bf16),
+            sem((ys - 1,)), sem((ys - 1,)), sem((n - 1,)), sem((n - 1,)),
+        ],
+        compiler_params=pltpu.CompilerParams(collective_id=cid, has_side_effects=True, vmem_limit_bytes=48 * 2**20),
+        cost_estimate=cost(25),
+        name="last_sums",
+    )(p, t)
+
+
 def passed_along(block, axis, distance):
     devices = range(lax.axis_size(axis))
     route = [(i - distance, i) for i in devices if i - distance in devices]
@@ -530,13 +1040,12 @@
     return lax.dot_general(a, b, ((contract[:1], contract[1:]), ((), ())), preferred_element_type=f32)
 
 
-def tokens_of_all(rows):
-    return lax.all_gather(rows, "seq", tiled=True)
-
-
-def columns_of_all(rows):
-    n = lax.axis_size("seq")
-    return lax.all_to_all(rows, "seq", split_axis=1, concat_axis=0, tiled=True)
+def lines(zs, ys):
+    return [[z * ys + y for z in range(zs)] for y in range(ys)]
+
+
+def tokens_of_line(rows, zs, ys):
+    return lax.all_gather(rows, "seq", axis_index_groups=lines(zs, ys), tiled=True)
 
 
 def local(
@@ -567,11 +1076,13 @@
     hidden = hidden_in.astype(f32).reshape(rows, width)
     grad_rows = cotangent.astype(f32).reshape(rows, width)
     ids = iter(range(100))
-
-    out_cols = {LAYERS - 1: columns_of_all(grad_rows.astype(bf16))}
+    zs = 4 if nseq % 4 == 0 else nseq
+    ys = nseq // zs
+    fold = width // nseq
+    places = (zs, ys)
+
+    out_cols = {}
     stored = []
-    result = None
-    ready = {(0, "local"): (out_cols[LAYERS - 1],)}
     for layer in range(LAYERS):
         last = layer == LAYERS - 1
         inv_rms = lax.rsqrt(jnp.mean(hidden * hidden, axis=-1, keepdims=True) + epsilon)
@@ -579,7 +1090,6 @@
         w_in = lax.optimization_barrier(input_projection_weight)[layer]
         both = lax.dot_general(normed, w_in, (((1,), (0,)), ((), ())), preferred_element_type=f32)
         values, gate_pre = both[:, 0], both[:, 1]
-        normed_cols = columns_of_all(normed)
         values3 = values.reshape(seqs, length, channels)
         edge = passed_along(values3[:, -(KERN - 1) :], "seq", 1)
         extended = jnp.concatenate([edge, values3], axis=1)
@@ -594,9 +1104,7 @@
         mats = proj_out[:, RANK:]
         step_pre = dot(rank_low, step_weight[layer], (1, 0)) + step_bias[layer]
         rates = decay_log[layer]
-        end_state, total = scan_local(
-            step_pre, activated, mats, keep, rates, seqs, ready.get((layer, "local"), ())
-        )
+        end_state, total = scan_local(step_pre, activated, mats, keep, rates, seqs, [], places, 0)
         gate_act = jax.nn.silu(gate_pre)
         if last:
             out_low = grad_rows.astype(bf16)
@@ -606,43 +1114,57 @@
             state_in, lam_in = carry_over(total, rates, [end_state, start], nseq, next(ids), True, True)
         else:
             (state_in,) = carry_over(total, rates, [end_state], nseq, next(ids), True, False)
-        pins = (normed_cols,) if layer == 0 else (normed_cols, stored[0][-2])
-        y = scan_forward(step_pre, activated, mats, keep, rates, state_in, seqs, pins)
+        keeping = (hidden, inv_rms, normed, gate_pre, gate_act, conv_out, activated, act_low, conv_pull, rank_low,
+                   step_pre, mats, total, state_in)
+        if last:
+            stored.append(keeping)
+            break
+        (y,) = scan_forward(step_pre, activated, mats, keep, rates, state_in, seqs, [], places, 0)
         scanned = y + skip_gain[layer] * activated
         mixed = (scanned * gate_act).astype(bf16)
         out_part = dot(mixed, output_projection_weight[layer], (1, 0)).astype(bf16)
-        mixed_all = tokens_of_all(mixed)
-        stored.append(
-            (hidden, inv_rms, normed, gate_pre, gate_act, conv_out, activated, act_low, conv_pull, rank_low,
-             step_pre, mats, total, state_in, scanned, mixed_all, normed_cols)
-        )
-        if last:
-            branch = ch_reduce(out_part, nch, next(ids), False)
-            result = (lax.dynamic_slice_in_dim(hidden, share_start, share, 1) + branch).astype(bf16)
-        else:
-            hidden = hidden + ch_reduce(out_part, nch, next(ids), True)
-
-    collected = [None] * LAYERS
+        mixed_all = tokens_of_line(mixed, zs, ys)
+        branch = ch_reduce(out_part, nch, next(ids), True)
+        hidden = hidden + branch
+        stored.append(keeping + (scanned, mixed_all))
+
     for layer in reversed(range(LAYERS)):
         last = layer == LAYERS - 1
         (hidden, inv_rms, normed, gate_pre, gate_act, conv_out, activated, act_low, conv_pull, rank_low,
-         step_pre, mats, total, state_in, scanned, mixed_all, normed_cols) = stored[layer]
+         step_pre, mats, total, state_in) = stored[layer][:14]
         rates = decay_log[layer]
         if not last:
+            scanned, mixed_all = stored[layer][14:]
+            normed_cols = early_cols
             out_low = grad_rows.astype(bf16)
             grad_mixed = dot(out_low, output_projection_weight[layer], (1, 1))
             grad_scan = grad_mixed * gate_act
-            start = scan_back_local(step_pre, grad_scan, mats, keep, rates, seqs, (stored[layer + 1][-2],))
+            grad_gate = (grad_mixed * scanned * silu_slope(gate_pre)).astype(bf16)
+            start = scan_back_local(step_pre, grad_scan, mats, keep, rates, seqs)
             (lam_in,) = carry_over(total, rates, [start], nseq, next(ids), False, True)
-            out_cols[layer] = columns_of_all(out_low)
-        grad_gate = (grad_mixed * scanned * silu_slope(gate_pre)).astype(bf16)
-        gate_all = tokens_of_all(grad_gate)
         grad_skip = jnp.sum(grad_scan * activated, axis=0)
-        grad_pre, grad_act, grad_mats, grad_decay = scan_back(
-            step_pre, activated, grad_scan, mats, keep, rates, skip_gain[layer][None], state_in, lam_in, seqs,
-            () if last else (out_cols[layer], gate_all_last),
+        if last:
+            plan = [(ColumnsLine, (4, 6), v) for v in (normed, out_low, stored[0][2])]
+        else:
+            plan = [
+                (ColumnsLine, (2, 4), out_low),
+                (GatherLine, (4, 8), grad_gate),
+                (PartSum, (), out_parts_last),
+                (PartSum, (), gate_parts_last),
+            ]
+        grad_pre, grad_act, grad_mats, grad_decay, *others = scan_back(
+            step_pre, activated, grad_scan, mats, keep, rates, skip_gain[layer][None], state_in, lam_in, seqs, int(last),
+            plan, places, next(ids), (stored[0][15],) if last else (),
         )
-        gate_all_last = gate_all
+        if last:
+            y, normed_cols, out_cols[layer], early_cols = others
+            scanned = y + skip_gain[layer] * activated
+            mixed = (scanned * gate_act).astype(bf16)
+            mixed_all = tokens_of_line(mixed, zs, ys)
+            grad_gate = (grad_mixed * scanned * silu_slope(gate_pre)).astype(bf16)
+            gate_all = tokens_of_line(grad_gate, zs, ys)
+        else:
+            out_cols[layer], gate_all, grad_out_last, grad_gate_last = others
         grad_step_bias = jnp.sum(grad_pre, axis=0)
         pre_low = grad_pre.astype(bf16)
         grad_step_weight = dot(rank_low, pre_low, (0, 0))
@@ -650,7 +1172,7 @@
         grad_proj = ch_sum(
             jnp.concatenate([rank_part, grad_mats[:, : 2 * STATE]], axis=-1), nch, next(ids)
         ).astype(bf16)
-        grad_proj_weight = dot(act_low, grad_proj, (0, 0))
+        grad_proj_weight = dot(grad_proj, act_low, (0, 0))
         grad_act = grad_act + dot(grad_proj, proj_weight[layer], (1, 1))
         grad_conv = (grad_act * silu_slope(conv_out)).reshape(seqs, length, channels)
         grad_ext, grad_conv_weight, grad_conv_bias = conv_pull(grad_conv)
@@ -659,33 +1181,82 @@
         grad_values = jnp.concatenate(
             [grad_values[:, : -(KERN - 1)], grad_values[:, -(KERN - 1) :] + returned], axis=1
         ).reshape(rows, channels).astype(bf16)
-        values_all = tokens_of_all(grad_values)
         w_in = lax.optimization_barrier(input_projection_weight)[layer]
         grad_both = jnp.stack([grad_values, grad_gate], axis=1)
         grad_part = lax.dot_general(grad_both, w_in, (((1, 2), (1, 2)), ((), ())), preferred_element_type=f32)
-        grad_normed = ch_reduce(grad_part.astype(bf16), nch, next(ids), True)
         scale_now = norm_gain[layer]
-        inner = jnp.sum(grad_normed * scale_now * hidden, axis=-1, keepdims=True)
-        grad_hidden = inv_rms * scale_now * grad_normed - hidden * (inv_rms * inv_rms * inv_rms) * inner / width
-        grad_norm = lax.dynamic_slice_in_dim(jnp.sum(grad_normed * hidden * inv_rms, axis=0), share_start, share, 0)
-        grad_rows = grad_rows + grad_hidden
-        grad_out_weight = dot(mixed_all, out_cols[layer], (0, 0))
-        grad_in_gate = dot(normed_cols, gate_all, (0, 0))
-        grad_in_values = dot(normed_cols, values_all, (0, 0))
-        small = [grad_norm, grad_conv_weight, grad_conv_bias, grad_proj_weight, grad_step_weight, grad_step_bias, grad_decay, grad_skip]
-        small = [v.astype(bf16) for v in small]
-        if not last:
-            small, _ = lax.optimization_barrier((small, collected[LAYERS - 1]))
-        small = [lax.psum(v, "seq").astype(f32) for v in small]
-        collected[layer] = (
-            small[0],
-            jnp.stack([grad_in_values, grad_in_gate], axis=1),
-            *small[1:],
-            grad_out_weight,
+        misc = jnp.concatenate([grad_conv_weight, grad_conv_bias[None], grad_step_bias[None], grad_skip[None]], axis=0)
+        small = [grad_proj_weight, grad_step_weight, grad_decay, misc]
+        if last:
+            values_last = tokens_of_line(grad_values, zs, ys)
+            values_parts_last = dot(normed_cols, values_last, (0, 0)).astype(bf16).reshape(ys, fold, channels)
+            grad_normed = ch_reduce(grad_part.astype(bf16), nch, next(ids), True)
+            out_part = dot(mixed, output_projection_weight[layer], (1, 0)).astype(bf16)
+            branch = ch_reduce(out_part, nch, next(ids), False)
+            result = (lax.dynamic_slice_in_dim(hidden, share_start, share, 1) + branch).astype(bf16)
+        columns = [out_cols[layer][:, k * fold : (k + 1) * fold] for k in range(ys)]
+        out_parts = jnp.stack([dot(mixed_all, k, (0, 0)).astype(bf16) for k in columns], axis=0)
+        gate_parts = dot(normed_cols, gate_all, (0, 0)).astype(bf16).reshape(ys, fold, channels)
+        if last:
+            out_parts_last, gate_parts_last = out_parts, gate_parts
+            inner = jnp.sum(grad_normed * scale_now * hidden, axis=-1, keepdims=True)
+            grad_norm = lax.dynamic_slice_in_dim(jnp.sum(grad_normed * hidden * inv_rms, axis=0), share_start, share, 0)
+            grad_rows = grad_rows + inv_rms * scale_now * grad_normed - hidden * (inv_rms * inv_rms * inv_rms) * inner / width
+            norm_row = jnp.pad(grad_norm[None], ((0, 0), (0, channels - share)))
+            small[-1] = jnp.pad(jnp.concatenate([misc, norm_row], axis=0), ((0, 16 - misc.shape[0] - 1), (0, 0)))
+            small_last = small
+            continue
+        inner = jnp.sum(grad_part * scale_now * hidden, axis=-1, keepdims=True)
+        inner_high = inner.astype(bf16)
+        inner_low = (inner - inner_high.astype(f32)).astype(bf16)
+        beside = jnp.pad(jnp.concatenate([inner_high, inner_low], axis=1), ((0, 0), (0, LANES - 2)))
+        beside = jnp.broadcast_to(beside[:, None], (rows, nch, LANES))
+        send = jnp.concatenate([grad_part.astype(bf16).reshape(rows, nch, share), beside], axis=2)
+        small[-1] = jnp.pad(misc, ((0, 16 - misc.shape[0]), (0, 0)))
+        got, values_all, sums, grad_gate_now, grad_out_weight, grad_values_last = closing(
+            send.reshape(rows, nch * (share + LANES)), grad_values, small + small_last, [gate_parts, out_parts, values_parts_last],
+            nch, zs, ys, next(ids),
         )
-    grad_input = lax.dynamic_slice_in_dim(grad_rows, share_start, share, 1).reshape(seqs, length, share)
-    stacked = [jnp.stack([collected[layer][member] for layer in range(LAYERS)], axis=0) for member in range(10)]
-    return (result.reshape(seqs, length, share), grad_input, *stacked)
+        grad_share, inner = got[:, :share], got[:, share : share + 1] + got[:, share + 1 : share + 2]
+        hidden_share = lax.dynamic_slice_in_dim(hidden, share_start, share, 1)
+        scale_share = lax.dynamic_slice_in_dim(scale_now, share_start, share, 0)
+        grad_norm = jnp.sum(grad_share * hidden_share * inv_rms, axis=0)
+        grad_input = (
+            lax.dynamic_slice_in_dim(grad_rows, share_start, share, 1)
+            + inv_rms * scale_share * grad_share
+            - hidden_share * (inv_rms * inv_rms * inv_rms) * inner / width
+        )
+        parts = dot(normed_cols, values_all, (0, 0)).astype(bf16).reshape(ys, fold, channels)
+        tiny = jnp.pad(grad_norm.astype(bf16)[None], ((0, 15), (0, 0)))
+        grad_in_values, tiny = last_sums(parts, tiny, nseq, zs, ys, next(ids))
+        total_small = sums.astype(f32)
+        heights = [v.shape[0] for v in small_last]
+        half = sum(heights)
+        pairs, at = [], 0
+        for height in heights:
+            pairs.append(jnp.stack([total_small[at : at + height], total_small[half + at : half + at + height]], axis=0))
+            at += height
+        misc = pairs[3]
+        norms = jnp.stack([tiny[0], misc[1, KERN + 3, :share]], axis=0)
+        in_weight = jnp.stack(
+            [jnp.stack(pair, axis=1) for pair in ((grad_in_values, grad_gate_now), (grad_values_last, grad_gate_last))], axis=0
+        )
+        out_weight = jnp.stack([grad_out_weight, grad_out_last], axis=0)
+    shape3 = (seqs, length, share)
+    return (
+        result.reshape(shape3),
+        grad_input.reshape(shape3),
+        norms,
+        in_weight,
+        misc[:, :KERN],
+        misc[:, KERN],
+        jnp.swapaxes(pairs[0], 1, 2),
+        pairs[1],
+        misc[:, KERN + 1],
+        pairs[2],
+        misc[:, KERN + 2],
+        out_weight,
+    )
 
 
 def solution(mesh):

time: 833 us -> 601 us (0.72)
  waiting for transfers between devices: 261 us -> 4.96 us
  Pallas kernels: 278 us -> 399 us
  blocking collectives: 51.5 us -> 0 us
  starting transfers between devices: 42.1 us -> 17.4 us
  other arithmetic: 51.8 us -> 39.5 us
    pallas_call x10 -> x11, Pallas kernels: 113 us -> 274 us  [the longest x5 153 us: play_call(): pl.pallas_call(after(played(kernel, counts, kinds, places), len(arrays),...]
    psum x2 -> x0, waiting for transfers between devices: 144 us -> none  [local(): small = [lax.psum(v, 'seq').astype(f32) for v in small]]
    all_gather x6 -> x4, waiting for transfers between devices: 107 us -> 1.33 us  [tokens_of_line(): lax.all_gather(rows, 'seq', axis_index_groups=lines(zs, ys), tiled=True)]
    psum x1 -> x0, blocking collectives: 51.5 us -> none  [local(): small = [lax.psum(v, 'seq').astype(f32) for v in small]]
    all_to_all x4 -> x0, starting transfers between devices: 24.1 us -> none  [columns_of_all(): return lax.all_to_all(rows, 'seq', split_axis=1, concat_axis=0, tiled=True)]
    pallas_call x3, Pallas kernels: 88.5 us -> 65.5 us  [carry_over(): pl.pallas_call(functools.partial(carry_kernel, n, int(fwd), int(rev)), ou...]
    pallas_call x4 -> x3, Pallas kernels: 61.6 us -> 44.1 us  [ch_reduce(): pl.pallas_call(functools.partial(reduce_kernel, n, parts, gather), out_sh...]
    another operation x23 -> x11, other arithmetic: 17.8 us -> 7.41 us  [the longest x4 2.35 us: local(): jnp.stack([total_small[at:at + height], total_small[half + at:half + at +...]
  transfers between devices with their start and end apart: 17 -> 9, of which waited for: 6 -> 2; matrix products, arithmetic and copies ran while one was open for 15% -> 13% of each run, Pallas kernels for 31% -> 34%
where the time goes in v3:
time: 601 us; the launch traced here: 591 us
  Pallas kernels  399 us (66%)
  matrix products  68.4 us (11%)
  local copies, waits for them, and re-layouts  45.9 us (8%)
  other arithmetic  39.5 us (7%)
  starting transfers between devices  17.4 us (3%)
  between operations  15.8 us (3%)
    pallas_call x5, Pallas kernels, play_call(): pl.pallas_call(after(played(kernel, counts, kinds, places), len(arrays),...  153 us
    pallas_call x1, Pallas kernels, closing(): pl.pallas_call(functools.partial(closing_kernel, n, zs, ys, parts, count,...  72.9 us
    pallas_call x3, Pallas kernels, carry_over(): pl.pallas_call(functools.partial(carry_kernel, n, int(fwd), int(rev)), ou...  65.5 us
    dot_general x24, matrix products, dot(): lax.dot_general(a, b, ((contract[:1], contract[1:]), ((), ())), preferred...  49.4 us
    pallas_call x3, Pallas kernels, ch_reduce(): pl.pallas_call(functools.partial(reduce_kernel, n, parts, gather), out_sh...  44.1 us
    pallas_call x4, Pallas kernels, ch_sum(): pl.pallas_call(after(functools.partial(ch_sum_kernel, n), 1, pins), out_s...  28.9 us
    unnamed x245, local copies, waits for them, and re-layouts  23.6 us
    pallas_call x1, Pallas kernels, last_sums(): pl.pallas_call(functools.partial(last_kernel, n, zs, ys), out_shape=[jax....  19.1 us
  transfers between devices with their start and end apart: 9, of which 2 were waited for; matrix products, arithmetic and copies ran while one was open for 13% of the time, Pallas kernels for 34%

profile of v3, /device:TPU:10, one launch (start us, length us, event | category | flops | bytes accessed | tf_op | source)
XLA Modules:
  0.0 591.2 jit_solution(5297165642613813256)
XLA Ops:
  9.6 14.0 %fusion.108 = (bf16[1,2048,2,1024]{3,2,1,0:T(2,128)(2,1)S(1)}, bf16[1,2048,2,1024]{3,2,1,0:T(2,128)(2,1)}) fusion(bf16[2,2048,2,1024]{3,2,1,0:T(2,128)(2,1)} %param.17), kind=kLoop, calls=%fused_computation.244 | loop fusion | bytes 33554432 | tf_op jit(solution)/shard_map/slice | solution.py:1090
  41.8 6.8 %ch_sum.4 = f32[256,160]{1,0:T(8,128)S(1)} custom-call(f32[256,160]{1,0:T(8,128)S(1)} %fusion.68.refs_0_), custom_call_target="tpu_custom_call" | custom-call | flops 10000000000 | tf_op jit(solution)/shard_map/ch_sum/pallas_call | solution.py:434
  51.9 7.9 %scan_local.2 = (f32[2,16,1024]{2,1,0:T(8,128)}, f32[2,1024]{1,0:T(2,128)}) custom-call(f32[256,1024]{1,0:T(8,128)} %convolution_add_fusion.3.refs_0_, f32[256,1024]{1,0:T(8,128)} %bitcast_multiply_fusion.5.refs_1_, f32[256,32]{1,0:T(8,128)} %slice.289.refs_2_.refs_3_, f32[256,1]{1,0:T(8,128)} %copy.35.refs_3_.refs_4_, ...), custom_call_target="tpu_custom_call" | custom-call | flops 8000000000 | tf_op jit(solution)/shard_map/scan_local/pallas_call | solution.py:150
  61.4 15.8 %carry_over.3.refs_5_.refs_7_ = f32[2,16,1024]{2,1,0:T(8,128)S(1)} custom-call(f32[2,1024]{1,0:T(2,128)S(1)} %copy-done.13, f32[16,1024]{1,0:T(8,128)S(1)} %copy-done.2, f32[2,16,1024]{2,1,0:T(8,128)S(1)} %copy-done.8), custom_call_target="tpu_custom_call" | custom-call | flops 19000000512 | tf_op jit(solution)/shard_map/carry_over/pallas_call | solution.py:674
  77.8 11.0 %scan_forward.1 = f32[256,1024]{1,0:T(8,128)} custom-call(f32[256,1024]{1,0:T(8,128)} %convolution_add_fusion.3.refs_0_, f32[256,1024]{1,0:T(8,128)} %bitcast_multiply_fusion.5.refs_1_, f32[256,32]{1,0:T(8,128)} %slice.289.refs_2_.refs_3_, f32[256,1]{1,0:T(8,128)} %copy.35.refs_3_.refs_4_, f32[16,1024]{1,0:T(8,128)} %get-tuple-element.154.refs_4_.refs_1_.refs_5_, ...), custom_call_target="tpu_custom_call" | custom-call | flops 11000000512 | tf_op jit(solution)/shard_map/scan_forward/pallas_call | solution.py:150
  94.7 17.2 %ch_reduce.3 = f32[256,2048]{1,0:T(8,128)S(1)} custom-call(bf16[256,2048]{1,0:T(8,128)(2,1)S(1)} %fusion.18.refs_0_), custom_call_target="tpu_custom_call" | custom-call | flops 17999998976 | tf_op jit(solution)/shard_map/ch_reduce/pallas_call | solution.py:614
  126.7 7.8 %ch_sum.5 = f32[256,160]{1,0:T(8,128)S(1)} custom-call(f32[256,160]{1,0:T(8,128)S(1)} %fusion.65.refs_0_), custom_call_target="tpu_custom_call" | custom-call | flops 10000000000 | tf_op jit(solution)/shard_map/ch_sum/pallas_call | solution.py:434
  136.4 6.5 %multiply_reduce_fusion.5 = (f32[1024]{0:T(1024)}, f32[256,1024]{1,0:T(8,128)}, f32[256,1024]{1,0:T(8,128)}, f32[256,1024]{1,0:T(8,128)}, f32[256,1024]{1,0:T(8,128)}) fusion(f32[2,128,1024]{2,1,0:T(8,128)S(1)} %get-tuple-element.116, f32[256,2,1024]{2,0,1:T(8,128)S(1)} %fusion.3, bf16[256,2048]{1,0:T(8,128)(2,1)S(1)} %bitcast.320, ...), kind=kOutput, calls=%fused_computation.106 | convolution fusion | flops 1077672960 | bytes 11538432 | tf_op jit(solution)/shard_map/dot_general | solution.py:1040
  142.9 7.7 %scan_back_local.2.refs_3_ = f32[2,16,1024]{2,1,0:T(8,128)} custom-call(f32[256,1024]{1,0:T(8,128)} %convolution_add_fusion.2.refs_0_, f32[256,1024]{1,0:T(8,128)} %get-tuple-element.110.refs_1_.refs_2_, f32[256,32]{1,0:T(8,128)} %slice.312.refs_2_.refs_3_, f32[256,1]{1,0:T(8,128)} %copy.35.refs_3_.refs_4_, f32[16,1024]{1,0:T(8,128)} %get-tuple-element.153.refs_4_.refs_1_.refs_5_), custom_call_target="tpu_custom_call" | custom-call | flops 8000000000 | tf_op jit(solution)/shard_map/scan_back_local/pallas_call | solution.py:253
  150.6 7.9 %scan_local.3 = (f32[2,16,1024]{2,1,0:T(8,128)}, f32[2,1024]{1,0:T(2,128)}) custom-call(f32[256,1024]{1,0:T(8,128)} %convolution_add_fusion.2.refs_0_, f32[256,1024]{1,0:T(8,128)} %get-tuple-element.149.refs_1_, f32[256,32]{1,0:T(8,128)} %slice.312.refs_2_.refs_3_, f32[256,1]{1,0:T(8,128)} %copy.35.refs_3_.refs_4_, ...), custom_call_target="tpu_custom_call" | custom-call | flops 8000000000 | tf_op jit(solution)/shard_map/scan_local/pallas_call | solution.py:150
  160.2 20.5 %carry_over.4 = (f32[2,16,1024]{2,1,0:T(8,128)S(1)}, f32[2,16,1024]{2,1,0:T(8,128)S(1)}) custom-call(f32[2,1024]{1,0:T(2,128)S(1)} %copy-done.15, f32[16,1024]{1,0:T(8,128)S(1)} %copy-done.4, f32[2,16,1024]{2,1,0:T(8,128)S(1)} %copy-done.7, f32[2,16,1024]{2,1,0:T(8,128)S(1)} %copy-done.5), custom_call_target="tpu_custom_call" | custom-call | flops 19000000512 | tf_op jit(solution)/shard_map/carry_over/pallas_call | solution.py:674
  182.0 39.0 %scan_back.2 = (f32[256,1024]{1,0:T(8,128)}, f32[256,1024]{1,0:T(8,128)}, f32[256,128]{1,0:T(8,128)}, f32[16,1024]{1,0:T(8,128)}, f32[256,1024]{1,0:T(8,128)}, /...) custom-call(f32[256,1024]{1,0:T(8,128)} %convolution_add_fusion.2.refs_0_, ...), custom_call_target="tpu_custom_call" | custom-call | flops 25999998976 | tf_op jit(solution)/shard_map/scan_back/pallas_call | solution.py:150
  223.4 7.7 %ch_sum.6 = f32[256,160]{1,0:T(8,128)S(1)} custom-call(f32[256,160]{1,0:T(8,128)S(1)} %pad_maximum_fusion.8.refs_0_), custom_call_target="tpu_custom_call" | custom-call | flops 10000000000 | tf_op jit(solution)/shard_map/ch_sum/pallas_call | solution.py:434
  243.9 10.5 %ch_reduce.4 = f32[256,512]{1,0:T(8,128)S(1)} custom-call(bf16[256,2048]{1,0:T(8,128)(2,1)S(1)} %fusion.21.refs_0_), custom_call_target="tpu_custom_call" | custom-call | flops 17999998976 | tf_op jit(solution)/shard_map/ch_reduce/pallas_call | solution.py:614
  258.8 6.5 %fusion.24.refs_0_ = bf16[256,2048]{1,0:T(8,128)(2,1)S(1)} fusion(bf16[1,2048,2,1024]{3,2,1,0:T(2,128)(2,1)} %get-tuple-element.122, bf16[256,1,1024]{2,0,1:T(8,128)(2,1)S(1)} %bitcast.306, bf16[256,1,1024]{2,0,1:T(8,128)(2,1)S(1)} %bitcast.307), kind=kOutput, calls=%fused_computation.23 | convolution fusion | flops 2148532224 | bytes 10485760 | tf_op jit(solution)/shard_map/dot_general | solution.py:1186
  265.4 16.3 %ch_reduce.5 = f32[256,2048]{1,0:T(8,128)S(1)} custom-call(bf16[256,2048]{1,0:T(8,128)(2,1)S(1)} %fusion.24.refs_0_), custom_call_target="tpu_custom_call" | custom-call | flops 17999998976 | tf_op jit(solution)/shard_map/ch_reduce/pallas_call | solution.py:614
  285.9 5.7 multiply_reduce_fusion.9
  291.6 7.8 %scan_back_local.3.refs_2_ = f32[2,16,1024]{2,1,0:T(8,128)} custom-call(f32[256,1024]{1,0:T(8,128)} %convolution_add_fusion.3.refs_0_, f32[256,1024]{1,0:T(8,128)} %get-tuple-element.112.refs_1_.refs_2_, f32[256,32]{1,0:T(8,128)} %slice.289.refs_2_.refs_3_, f32[256,1]{1,0:T(8,128)} %copy.35.refs_3_.refs_4_, f32[16,1024]{1,0:T(8,128)} %get-tuple-element.154.refs_4_.refs_1_.refs_5_), custom_call_target="tpu_custom_call" | custom-call | flops 8000000000 | tf_op jit(solution)/shard_map/scan_back_local/pallas_call | solution.py:253
  300.3 29.2 %carry_over.5.refs_8_ = f32[2,16,1024]{2,1,0:T(8,128)S(1)} custom-call(f32[2,1024]{1,0:T(2,128)S(1)} %copy-done.14, f32[16,1024]{1,0:T(8,128)S(1)} %copy-done.3, f32[2,16,1024]{2,1,0:T(8,128)S(1)} %copy-done.6), custom_call_target="tpu_custom_call" | custom-call | flops 19000000512 | tf_op jit(solution)/shard_map/carry_over/pallas_call | solution.py:674
  339.8 87.4 %scan_back.3 = (f32[256,1024]{1,0:T(8,128)}, f32[256,1024]{1,0:T(8,128)}, f32[256,128]{1,0:T(8,128)}, f32[16,1024]{1,0:T(8,128)}, bf16[1024,512]{1,0:T(8,128)(2,...) custom-call(f32[256,1024]{1,0:T(8,128)} %convolution_add_fusion.3.refs_0_, ...), custom_call_target="tpu_custom_call" | custom-call | flops 23000000512 | tf_op jit(solution)/shard_map/scan_back/pallas_call | solution.py:150
  429.0 6.6 %ch_sum.7 = f32[256,160]{1,0:T(8,128)S(1)} custom-call(f32[256,160]{1,0:T(8,128)S(1)} %pad_maximum_fusion.9.refs_0_), custom_call_target="tpu_custom_call" | custom-call | flops 10000000000 | tf_op jit(solution)/shard_map/ch_sum/pallas_call | solution.py:434
  458.0 6.6 %fusion.109 = (bf16[256,2048]{1,0:T(8,128)(2,1)S(1)}, f32[256]{0:T(256)S(1)}) fusion(bf16[2,128,2048]{2,1,0:T(8,128)(2,1)S(1)} %copy-done.19, f32[2048]{0:T(1024)S(1)} %bitcast.334, bf16[1,2048,2,1024]{3,2,1,0:T(2,128)(2,1)} %copy-done.36, bf16[256,1,1024]{2,0,1:T(8,128)(2,1)S(1)} %bitcast.378, bf16[256,1,1024]{2,0,1:T(8,128)(2,1)S(1)} %bitcast.322), kind=kOutput, calls=%fused_computation.245 | convolution fusion | flops 2150629120 | bytes 11543552 | tf_op jit(solution)/shard_map/dot_general | solution.py:1186
  471.7 72.9 %closing.1 = (f32[256,640]{1,0:T(8,128)}, bf16[1024,1024]{1,0:T(8,128)(2,1)}, bf16[640,1024]{1,0:T(8,128)(2,1)}, f32[256,1024]{1,0:T(8,128)}, f32[1024,256]{1,0:T(8,128)}, /*index=5*/f32[256,1024]{1,0:T(8,128)}) custom-call(bf16[256,2560]{1,0:T(8,128)(2,1)} %bitcast.309, bf16[256,1024]{1,0:T(8,128)(2,1)} %bitcast.323, f32[160,1024]{1,0:T(8,128)} %fusion.60.refs_0_, ...), custom_call_target="tpu_custom_call" | custom-call | flops 70000001024 | tf_op jit(solution)/shard_map/closing/pallas_call | solution.py:937
  552.3 19.1 %last_sums.1 = (f32[256,1024]{1,0:T(8,128)S(1)}, f32[16,512]{1,0:T(8,128)S(1)}) custom-call(bf16[2,256,1024]{2,1,0:T(8,128)(2,1)S(1)} %bitcast.293, bf16[16,512]{1,0:T(8,128)(2,1)S(1)} %pad.88.t_ref), custom_call_target="tpu_custom_call" | custom-call | flops 24999999488 | tf_op jit(solution)/shard_map/last_sums/pallas_call | solution.py:997
  (379 shorter events, 136.7 us)
Async XLA Ops:
  7.2 174.8 %all-gather.5.cloned.1.call-start = ((), (), s32[]{:S(2)}) async-start(), calls=%async_computation | async-start | bytes 2621440 | tf_op jit(solution)/shard_map/all_gather | solution.py:1048
  8.0 106.6 %copy-start.84 = (f32[1,2048]{1,0:T(1,128)}, f32[1,2048]{1,0:T(1,128)S(1)}, u32[]{:S(2)}) copy-start(f32[1,2048]{1,0:T(1,128)S(1)} %get-tuple-element.163) | copy-start | bytes 24580
  8.0 113.1 %copy-start.86 = (f32[1,2048]{1,0:T(1,128)}, f32[1,2048]{1,0:T(1,128)S(1)}, u32[]{:S(2)}) copy-start(f32[1,2048]{1,0:T(1,128)S(1)} %get-tuple-element.164) | copy-start | bytes 24580
  9.6 102.4 %copy-start.102 = (f32[256]{0:T(256)}, f32[256]{0:T(256)S(1)}, u32[]{:S(2)}) copy-start(f32[256]{0:T(256)S(1)} %get-tuple-element.178) | copy-start | bytes 3076
  27.1 12.2 %collective-permute-start = (f32[2,3,1024]{2,1,0:T(4,128)S(1)}, f32[2,3,1024]{2,1,0:T(4,128)S(1)}, u32[]{:S(2)}, u32[]{:S(2)}) collective-permute-start(f32[2,3,1024]{2,1,0:T(4,128)S(1)} %slice.346), channel_id=1, source_target_pairs={{0,4},{4,8},{8,12},{12,16},{16,20},{20,24},{24,28},{1,5},{5,9},{9,... | collective-permute-start | bytes 73736 | tf_op jit(solution)/shard_map/ppermute | solution.py:1016
  30.8 7.6 %collective-permute-start.1 = (f32[2,3]{1,0:T(2,128)S(1)}, f32[2,3]{1,0:T(2,128)S(1)}, u32[]{:S(2)}, u32[]{:S(2)}) collective-permute-start(f32[2,3]{1,0:T(2,128)S(1)} %slice.276), channel_id=1, source_target_pairs={{0,4},{4,8},{8,12},{12,16},{16,20},{20,24},{24,28},{1,5},{5,9},{9,... | collective-permute-start | bytes 80 | tf_op jit(solution)/shard_map/ppermute | solution.py:1016
  38.4 50.4 %copy-start.97 = (f32[1,1024]{1,0:T(1,128)}, f32[1,1024]{1,0:T(1,128)S(1)}, u32[]{:S(2)}) copy-start(f32[1,1024]{1,0:T(1,128)S(1)} %get-tuple-element.166.refs_6_) | copy-start | bytes 12292
  40.2 48.6 %copy-start.34 = (f32[2,128,1024]{2,1,0:T(8,128)}, f32[2,128,1024]{2,1,0:T(8,128)S(1)}, u32[]{:S(2)}) copy-start(f32[2,128,1024]{2,1,0:T(8,128)S(1)} %get-tuple-element.120) | copy-start | bytes 3145732
  91.0 24.5 %slice-start = ((s8[8388608]{0:T(1024)(128)(4,1)}), s8[4194304]{0:T(1024)(128)(4,1)S(1)}, s32[]{:S(2)}) async-start(s8[8388608]{0:T(1024)(128)(4,1)} %bitcast.303), calls=%async_computation.4 | async-start | bytes 8388608
  94.7 20.8 %slice-start.1 = ((s8[8388608]{0:T(1024)(128)(4,1)}), s8[4194304]{0:T(1024)(128)(4,1)S(1)}, s32[]{:S(2)}) async-start(s8[8388608]{0:T(1024)(128)(4,1)} %bitcast.303), calls=%async_computation.5 | async-start | bytes 8388608
  118.5 112.6 %copy-start.40 = (f32[256,2,1024]{2,0,1:T(8,128)}, f32[256,2,1024]{2,0,1:T(8,128)S(1)}, u32[]{:S(2)}) copy-start(f32[256,2,1024]{2,0,1:T(8,128)S(1)} %fusion.3) | copy-start | bytes 6291460
  118.7 6.7 %collective-permute-start.2 = (f32[2,3,1024]{2,1,0:T(4,128)S(1)}, f32[2,3,1024]{2,1,0:T(4,128)S(1)}, u32[]{:S(2)}, u32[]{:S(2)}) collective-permute-start(f32[2,3,1024]{2,1,0:T(4,128)S(1)} %slice.359), channel_id=1, source_target_pairs={{0,4},{4,8},{8,12},{12,16},{16,20},{20,24},{24,28},{1,5},{5,9},{9,... | collective-permute-start | bytes 73736 | tf_op jit(solution)/shard_map/ppermute | solution.py:1016
  121.8 208.5 %all-gather.7.cloned.1.call-start = ((), (), s32[]{:S(2)}) async-start(), calls=%async_computation.1 | async-start | bytes 2621440 | tf_op jit(solution)/shard_map/all_gather | solution.py:1048
  233.0 103.0 %all-gather.9.cloned.1.call-start = ((), (), s32[]{:S(2)}) async-start(), calls=%async_computation.2 | async-start | bytes 2621440 | tf_op jit(solution)/shard_map/all_gather | solution.py:1048
  235.4 19.1 %copy-start.24 = (f32[2,128,1024]{2,1,0:T(8,128)}, f32[2,128,1024]{2,1,0:T(8,128)S(1)}, u32[]{:S(2)}) copy-start(f32[2,128,1024]{2,1,0:T(8,128)S(1)} %get-tuple-element.144) | copy-start | bytes 3145732
  235.4 19.1 %copy-start.25 = (f32[2,128,1024]{2,1,0:T(8,128)}, f32[2,128,1024]{2,1,0:T(8,128)S(1)}, u32[]{:S(2)}) copy-start(f32[2,128,1024]{2,1,0:T(8,128)S(1)} %get-tuple-element.145) | copy-start | bytes 3145732
  235.4 19.1 %copy-start.26 = (f32[2,128,1024]{2,1,0:T(8,128)}, f32[2,128,1024]{2,1,0:T(8,128)S(1)}, u32[]{:S(2)}) copy-start(f32[2,128,1024]{2,1,0:T(8,128)S(1)} %get-tuple-element.146) | copy-start | bytes 3145732
  235.5 22.1 %collective-permute-start.3 = (f32[2,3,1024]{2,1,0:T(4,128)S(1)}, f32[2,3,1024]{2,1,0:T(4,128)S(1)}, u32[]{:S(2)}, u32[]{:S(2)}) collective-permute-start(f32[2,3,1024]{2,1,0:T(4,128)S(1)} %pad_add_fusion.3), channel_id=1, source_target_pairs={{4,0},{8,4},{12,8},{16,12},{20,16},{24,20},{28,24},{5,1},{9,5},{13... | collective-permute-start | bytes 73736 | tf_op jit(solution)/shard_map/ppermute | solution.py:1016
  257.3 210.5 %all-gather.11.cloned.1.call-start = ((), (), s32[]{:S(2)}) async-start(), calls=%async_computation.3 | async-start | bytes 2621440 | tf_op jit(solution)/shard_map/all_gather | solution.py:1048
  265.3 16.4 %copy-start.17 = (f32[256,2048]{1,0:T(8,128)S(1)}, f32[256,2048]{1,0:T(8,128)}, u32[]{:S(2)}) copy-start(f32[256,2048]{1,0:T(8,128)} %copy-done.16) | copy-start | bytes 6291460
  300.3 29.9 %copy-start.116 = (bf16[1024,512]{1,0:T(8,128)(2,1)S(1)}, bf16[1024,512]{1,0:T(8,128)(2,1)}, u32[]{:S(2)}) copy-start(bf16[1024,512]{1,0:T(8,128)(2,1)} %get-tuple-element.52) | copy-start | bytes 3145732
  339.8 87.4 %copy-start.58 = (bf16[2,128,1024]{2,1,0:T(8,128)(2,1)S(1)}, bf16[2,128,1024]{2,1,0:T(8,128)(2,1)}, u32[]{:S(2)}) copy-start(bf16[2,128,1024]{2,1,0:T(8,128)(2,1)} %param.21) | copy-start | bytes 1572868
  441.0 15.6 %collective-permute-start.4 = (f32[2,3,1024]{2,1,0:T(4,128)S(1)}, f32[2,3,1024]{2,1,0:T(4,128)S(1)}, u32[]{:S(2)}, u32[]{:S(2)}) collective-permute-start(f32[2,3,1024]{2,1,0:T(4,128)S(1)} %pad_add_fusion.2), channel_id=1, source_target_pairs={{4,0},{8,4},{12,8},{16,12},{20,16},{24,20},{28,24},{5,1},{9,5},{13... | collective-permute-start | bytes 73736 | tf_op jit(solution)/shard_map/ppermute | solution.py:1016
  552.3 19.1 %copy-start.68 = (f32[256,1024]{1,0:T(8,128)S(1)}, f32[256,1024]{1,0:T(8,128)}, u32[]{:S(2)}) copy-start(f32[256,1024]{1,0:T(8,128)} %get-tuple-element.67) | copy-start | bytes 3145732
  (105 other events, 464.0 us)
Sparse Core Ops, SparseCore 0:
  121.9 51.6 all-gather.4
  233.1 46.3 all-gather.6
  281.6 54.2 all-gather.8
  337.4 64.5 all-gather.10

commit v4 on v3

--- a/solution.py
+++ b/solution.py
@@ -24,7 +24,7 @@
 
 
 def cost(us):
-    return pl.CostEstimate(flops=int(us * 1.0e9), bytes_accessed=0, transcendentals=0)
+    return pl.CostEstimate(flops=int(us * 0.1e9), bytes_accessed=0, transcendentals=0)
 
 
 LANES = 128
@@ -204,7 +204,7 @@
             lax.fori_loop(0, length // 8, red, 0)
             yield
 
-def scan_forward(pre, act, bc, keep, dl, state_in, seqs, plan, places, cid):
+def scan_forward(pre, act, bc, keep, dl, state_in, seqs, plan, places, cid, pins=()):
     rows, channels = pre.shape
     f = jnp.float32
     big = pltpu.VMEM((channels // LANES, rows, LANES), f)
@@ -213,7 +213,7 @@
         [jax.ShapeDtypeStruct((rows, channels), f)],
         [pltpu.VMEM((rows * STATE, 2 * LANES), f), pltpu.VMEM((32 * STATE, 2 * STATE), jnp.bfloat16), big, big,
          pltpu.VMEM((4, rows // seqs * 8, LANES), f)],
-        (pre, act, bc, keep, dl, state_in), 11, "scan_forward",
+        (pre, act, bc, keep, dl, state_in), 11, "scan_forward", pins,
     )
 
 
@@ -444,7 +444,8 @@
     x, core = me // 2, lax.rem(me, 2)
     peer = {"ch": x * 2 + 1 - core}
     others = [lax.rem(x + d, xs) for d in range(1, xs)]
-    greet([peer] + [{"ch": o * 2 + core} for o in others] + more)
+    if more is not None:
+        greet([peer] + [{"ch": o * 2 + core} for o in others] + more)
     rows, width = x_ref.shape[0] // parts, x_ref.shape[1] // n
     def cols(block):
         return pl.ds(pl.multiple_of(block * width, width), width)
@@ -621,13 +622,20 @@
     )(x)
 
 
-def carry_kernel(n, fwd, rev, *refs):
+def carry_kernel(n, fwd, rev, count, places, layer, *refs):
     refs = list(refs)
     tot_ref, dl_ref = refs.pop(0), refs.pop(0)
     k = fwd + rev
     ends = [refs.pop(0) for _ in range(k)]
+    parts = [refs.pop(0) for _ in range(count)]
+    whole = refs.pop(0) if layer is not None else None
     outs = [refs.pop(0) for _ in range(k)]
-    mine, slots, tots, send, recv, tsend, trecv = refs
+    sums = [refs.pop(0) for _ in range(count)]
+    if layer is not None:
+        local = pltpu.make_async_copy(whole.at[layer], refs.pop(0), refs.pop(-1))
+        local.start()
+    mine, slots, tots, send, recv, tsend, trecv = refs[:7]
+    jobs = [PartSum(*places, parts[j], sums[j], refs[7 + 3 * j : 10 + 3 * j]) for j in range(count)]
     me = lax.axis_index("seq")
     seqs = tot_ref.shape[0]
     greet([{"seq": lax.rem(me + d, n)} for d in range(1, n)])
@@ -650,6 +658,8 @@
             def _():
                 for c in copies(i, d):
                     c.start()
+    for job in jobs:
+        job.begin()
     for d in reversed(range(1, n)):
         for i in range(k):
             place = n - 1 - me if directions[i] else me
@@ -667,17 +677,28 @@
             def _():
                 for c in copies(i, d):
                     c.wait_send()
-
-def carry_over(tot, dl, ends, n, cid, fwd, rev):
+    for job in jobs:
+        job.finish()
+    if layer is not None:
+        local.wait()
+
+
+def carry_over(tot, dl, ends, n, cid, fwd, rev, ps=(), places=(), taken=None):
+    whole, layer = (None, None) if taken is None else taken
+    extra = [] if taken is None else [whole]
     k = len(ends)
     sem = pltpu.SemaphoreType.DMA
     return pl.pallas_call(
-        functools.partial(carry_kernel, n, int(fwd), int(rev)),
-        out_shape=[jax.ShapeDtypeStruct(ends[0].shape, f32)] * k, in_specs=[VM] * (k + 2), out_specs=[VM] * k,
+        functools.partial(carry_kernel, n, int(fwd), int(rev), len(ps), places, layer),
+        out_shape=[jax.ShapeDtypeStruct(ends[0].shape, f32)] * k + [PartSum.result(p, *places) for p in ps]
+        + [jax.ShapeDtypeStruct(w.shape[1:], w.dtype) for w in extra],
+        in_specs=[VM] * (k + 2 + len(ps)) + [ANY] * len(extra), out_specs=[VM] * (k + len(ps)) + [ANY] * len(extra),
         scratch_shapes=[pltpu.VMEM((k,) + ends[0].shape, bf16), pltpu.VMEM((k, n - 1) + ends[0].shape, bf16), pltpu.VMEM((k, n - 1) + tot.shape, f32),
-                        sem((k, n - 1)), sem((k, n - 1)), sem((k, n - 1)), sem((k, n - 1))],
+                        sem((k, n - 1)), sem((k, n - 1)), sem((k, n - 1)), sem((k, n - 1))]
+        + [spec for p in ps for spec in PartSum.specs(p, *places)]
+        + [pltpu.SemaphoreType.DMA] * len(extra),
         compiler_params=pltpu.CompilerParams(collective_id=cid, has_side_effects=True, vmem_limit_bytes=32 * 2**20), cost_estimate=cost(19), name="carry_over",
-    )(tot, dl, *ends)
+    )(tot, dl, *ends, *ps, *extra)
 
 
 def seq_at(z, y, ys):
@@ -748,8 +769,14 @@
             self.copy(way, r).wait_recv()
 
     def finish(self):
+        self.arrived()
+        self.sent()
+
+    def arrived(self):
         for way in (0, 1):
             self.arrive(way, self.zs - 2)
+
+    def sent(self):
         for way in (0, 1):
             for r in range(self.zs - 1):
                 @pl.when(self.sends(way, r))
@@ -758,40 +785,50 @@
 
 
 class SumAll:
-    def __init__(self, zs, ys, src, out, yslots, ysum, zslots, sems):
+    def __init__(self, zs, ys, src, out, scratch):
         me = lax.axis_index("seq")
         self.zs, self.ys, self.z, self.y = zs, ys, me // ys, lax.rem(me, ys)
-        self.src, self.out, self.yslots, self.ysum, self.zslots = src, out, yslots, ysum, zslots
-        self.sems = sems
+        self.src, self.out = src, out
+        self.yslots, self.ysum, self.slots, self.running, self.acc = scratch[:5]
+        self.y1sems, self.zsems, self.y2sems, gather = scratch[5:7], scratch[7:9], scratch[9:11], scratch[11:13]
         self.part = src.shape[0] // ys
         self.share = self.part // zs
-
-    def remote(self, k, i, src, dst, to):
-        send, recv = self.sems[2 * k : 2 * k + 2]
-        return pltpu.make_async_remote_copy(src_ref=src, dst_ref=dst, send_sem=send.at[i], recv_sem=recv.at[i], device_id=to, device_id_type=MESH)
+        self.back = GatherLine(zs, ys, self.mine(self.z), out, gather)
+        self.back.block = self.mine
+
+    @staticmethod
+    def specs(height, w, zs, ys):
+        part = height // ys
+        share = part // zs
+        sem = pltpu.SemaphoreType.DMA
+        return [
+            pltpu.VMEM((ys - 1, part, w), bf16),
+            pltpu.VMEM((part, w), bf16),
+            pltpu.VMEM((2, zs, share, w), bf16),
+            pltpu.VMEM((2, zs, share, w), bf16),
+            pltpu.VMEM((share, w), f32),
+            sem((ys - 1,)), sem((ys - 1,)), sem((2, zs)), sem((2, zs)), sem(((ys - 1) * zs,)), sem(((ys - 1) * zs,)),
+            sem((2, zs - 1)), sem((2, zs - 1)),
+        ]
 
     def rows(self, index, size):
         return pl.ds(pl.multiple_of(index * size, size), size)
 
+    def mine(self, z):
+        return self.out.at[self.rows(self.y * self.zs + z, self.share)]
+
     def y1(self, d):
         to = lax.rem(self.y + d, self.ys)
-        return self.remote(0, d - 1, self.src.at[self.rows(to, self.part)], self.yslots.at[d - 1], seq_at(self.z, to, self.ys))
-
-    def z1(self, d):
-        to = lax.rem(self.z + d, self.zs)
-        return self.remote(1, d - 1, self.ysum.at[self.rows(to, self.share)], self.zslots.at[d - 1], seq_at(to, self.y, self.ys))
-
-    def mine(self, z):
-        return self.out.at[self.rows(self.y * self.zs + z, self.share)]
-
-    def z2(self, d):
-        to = lax.rem(self.z + d, self.zs)
-        return self.remote(2, d - 1, self.mine(self.z), self.mine(self.z), seq_at(to, self.y, self.ys))
-
-    def y2(self, d, e):
+        return pltpu.make_async_remote_copy(src_ref=self.src.at[self.rows(to, self.part)], dst_ref=self.yslots.at[d - 1], send_sem=self.y1sems[0].at[d - 1], recv_sem=self.y1sems[1].at[d - 1], device_id=seq_at(self.z, to, self.ys), device_id_type=MESH)
+
+    def run(self, way, k):
+        to = lax.rem(self.z + (1 if way == 0 else self.zs - 1), self.zs)
+        return pltpu.make_async_remote_copy(src_ref=self.running.at[way, k], dst_ref=self.slots.at[way, k], send_sem=self.zsems[0].at[way, k], recv_sem=self.zsems[1].at[way, k], device_id=seq_at(to, self.y, self.ys), device_id_type=MESH)
+
+    def y2(self, d, b):
         to = lax.rem(self.y + d, self.ys)
-        share = self.mine(lax.rem(self.z - e + self.zs, self.zs))
-        return self.remote(3, (d - 1) * self.zs + e, share, share, seq_at(self.z, to, self.ys))
+        at = (d - 1) * self.zs + b
+        return pltpu.make_async_remote_copy(src_ref=self.mine(b), dst_ref=self.mine(b), send_sem=self.y2sems[0].at[at], recv_sem=self.y2sems[1].at[at], device_id=seq_at(self.z, to, self.ys), device_id_type=MESH)
 
     def begin(self):
         for d in range(1, self.ys):
@@ -803,37 +840,65 @@
             self.y1(d).wait_recv()
             total = total + self.yslots[d - 1].astype(f32)
         self.ysum[...] = total.astype(bf16)
-        for d in range(1, self.zs):
-            self.z1(d).start()
-
-    def gather(self):
-        total = self.ysum[self.rows(self.z, self.share), :].astype(f32)
-        for d in range(1, self.zs):
-            self.z1(d).wait_recv()
-            total = total + self.zslots[d - 1].astype(f32)
-        self.mine(self.z)[...] = total.astype(bf16)
-        for d in range(1, self.zs):
-            self.z2(d).start()
+
+    def line_sum(self, r):
+        for way in (0, 1):
+            k = self.zs - 1 - r if way == 0 else r
+            z, first = self.z, 0 if way == 0 else self.zs - 1
+            own = pl.ds(k * self.share, self.share)
+            @pl.when(z == first)
+            def _():
+                self.running[way, k] = self.ysum[own, :]
+                self.run(way, k).start()
+            inside = jnp.logical_and(z > 0, z < k) if way == 0 else jnp.logical_and(z < self.zs - 1, z > k)
+            @pl.when(inside)
+            def _():
+                self.run(way, k).wait_recv()
+                self.running[way, k] = (self.ysum[own, :].astype(f32) + self.slots[way, k].astype(f32)).astype(bf16)
+                self.run(way, k).start()
+
+    def turn(self):
+        self.acc[...] = self.ysum[self.rows(self.z, self.share), :].astype(f32)
+        for way in (0, 1):
+            @pl.when(self.z > 0 if way == 0 else self.z < self.zs - 1)
+            def _():
+                self.run(way, self.z).wait_recv()
+                self.acc[...] = self.acc[...] + self.slots[way, self.z].astype(f32)
+        self.mine(self.z)[...] = self.acc[...].astype(bf16)
+        self.back.start(0)
         for d in range(1, self.ys):
-            self.y2(d, 0).start()
-
-    def spread(self):
-        for e in range(1, self.zs):
-            self.z2(e).wait_recv()
-            for d in range(1, self.ys):
-                self.y2(d, e).start()
+            self.y2(d, self.z).start()
+
+    def spread(self, r):
+        if r < self.zs - 2:
+            self.back.start(r + 1)
+        else:
+            for way in (0, 1):
+                self.back.arrive(way, r)
+        for way in (0, 1):
+            b = self.z - 1 - r if way == 0 else self.z + 1 + r
+            b = lax.rem(b + self.zs, self.zs)
+            @pl.when(self.back.receives(way, r))
+            def _():
+                for d in range(1, self.ys):
+                    self.y2(d, b).start()
 
     def finish(self):
         for d in range(1, self.ys):
-            for e in range(self.zs):
-                self.y2(d, e).wait_recv()
+            for b in range(self.zs):
+                self.y2(d, b).wait_recv()
         for d in range(1, self.ys):
             self.y1(d).wait_send()
-            for e in range(self.zs):
-                self.y2(d, e).wait_send()
-        for d in range(1, self.zs):
-            self.z1(d).wait_send()
-            self.z2(d).wait_send()
+            for b in range(self.zs):
+                self.y2(d, b).wait_send()
+        for k in range(self.zs):
+            @pl.when(self.z < k)
+            def _():
+                self.run(0, k).wait_send()
+            @pl.when(self.z > k)
+            def _():
+                self.run(1, k).wait_send()
+        self.back.sent()
 
 
 class PartSum:
@@ -880,134 +945,129 @@
             self.copy(d).wait_send()
 
 
-def closing_kernel(n, zs, ys, parts, count, pieces, x_ref, v_ref, *refs):
-    piece_refs, refs = refs[:pieces], refs[pieces:]
-    p_refs, refs = refs[:count], refs[count:]
-    out_ref, all_ref, sum_ref, *refs = refs
-    part_refs, refs = refs[:count], refs[count:]
-    s_ref, *refs = refs
-    reduce_scratch, scratch = refs[:14], refs[14:]
-    yslots, ysum, zslots, gsend, grecv = scratch[:5]
+def closing_kernel(n, nseq, zs, ys, parts, count, pieces, x_ref, b_ref, v_ref, cols_ref, h_ref, *refs):
+    refs = list(refs)
+
+    def take(k):
+        head, refs[:] = refs[:k], refs[k:]
+        return head
+
+    piece_refs, p_refs = take(pieces), take(count)
+    out_ref, branch_ref, sum_ref, values_ref, norm_ref = take(5)
+    part_refs = take(count)
+    s_ref, all_ref, mine_ref, mine_slots, t_ref, tslots = take(6)
+    reduce_scratch, more_scratch, gather_sems, sum_scratch = take(14), take(14), take(2), take(13)
+    part_scratch, (msend, mrecv, tsend, trecv) = take(3 * count), take(4)
     seq = lax.axis_index("seq")
-    z, y = seq // ys, lax.rem(seq, ys)
-    line = GatherLine(zs, ys, v_ref, all_ref, (gsend, grecv))
-    total = SumAll(zs, ys, s_ref, sum_ref, yslots, ysum, zslots, scratch[5:13])
-    sums = [PartSum(zs, ys, p_refs[k], part_refs[k], scratch[13 + 3 * k : 16 + 3 * k]) for k in range(count)]
-    peers = [seq_at(z, lax.rem(y + d, ys), ys) for d in range(1, ys)]
-    peers += [seq_at(lax.rem(z + d, zs), y, ys) for d in range(1, zs)]
-    steps = reduce_steps(n, parts, False, peers, x_ref, out_ref, *reduce_scratch)
+    z = seq // ys
+    line = GatherLine(zs, ys, v_ref, all_ref, gather_sems)
+    total = SumAll(zs, ys, s_ref, sum_ref, sum_scratch)
+    sums = [PartSum(zs, ys, p_refs[k], part_refs[k], part_scratch[3 * k : 3 * k + 3]) for k in range(count)]
+    late = PartSum(zs, ys, mine_ref, values_ref, [msend, mrecv, mine_slots])
+    steps = reduce_steps(n, parts, False, [{"seq": lax.rem(seq + d, nseq)} for d in range(1, nseq)], x_ref, out_ref, *reduce_scratch)
+    more_steps = reduce_steps(n, parts, False, None, b_ref, branch_ref, *more_scratch)
+
+    def tiny(d):
+        return pltpu.make_async_remote_copy(src_ref=t_ref, dst_ref=tslots.at[seq], send_sem=tsend.at[d - 1], recv_sem=trecv.at[d - 1], device_id={"seq": lax.rem(seq + d, nseq)}, device_id_type=MESH)
+
     next(steps)
+    next(more_steps)
+    line.begin()
     offset = 0
     for piece in piece_refs:
         s_ref[pl.ds(offset, piece.shape[0]), :] = piece[...].astype(bf16)
         offset += piece.shape[0]
     if offset < s_ref.shape[0]:
         s_ref[pl.ds(offset, s_ref.shape[0] - offset), :] = jnp.zeros((s_ref.shape[0] - offset, s_ref.shape[1]), bf16)
-    line.start(0)
     total.begin()
+    next(steps)
+    next(more_steps)
+    line.start(1)
+    total.middle()
+    total.line_sum(0)
     for part in sums:
         part.begin()
-    all_ref[pl.ds(pl.multiple_of(z * line.rows, line.rows), line.rows), :] = v_ref[...]
-    next(steps)
-    total.middle()
-    next(steps)
-    line.start(1)
     for _ in steps:
         pass
-    total.gather()
+    w = h_ref.shape[1]
+    row = jnp.sum(out_ref[:, pl.ds(0, w)] * h_ref[...], axis=0, keepdims=True)
+    t_ref[...] = jnp.broadcast_to(row, t_ref.shape).astype(bf16)
+    tslots[seq] = t_ref[...]
+    for d in range(1, nseq):
+        tiny(d).start()
+    total.line_sum(1)
     for r in range(2, zs - 1):
         line.start(r)
-    for part in sums[:-1]:
+        total.line_sum(r)
+    total.turn()
+    for _ in more_steps:
+        pass
+    line.arrived()
+    fold = mine_ref.shape[1]
+    for k in range(ys):
+        def chunk(i, _):
+            at = pl.ds(pl.multiple_of(i * 256, 256), 256)
+            got = jnp.dot(cols_ref[pl.ds(k * fold, fold), :], all_ref[:, at], preferred_element_type=f32)
+            mine_ref[k, :, at] = got.astype(bf16)
+            return 0
+        lax.fori_loop(0, all_ref.shape[1] // 256, chunk, 0)
+    late.begin()
+    for r in range(zs - 1):
+        total.spread(r)
+    for part in sums:
         part.finish()
-    total.spread()
-    for part in sums[-1:]:
-        part.finish()
-    line.finish()
+    for d in range(1, nseq):
+        tiny(d).wait_recv()
+    norm = tslots[0].astype(f32)
+    for k in range(1, nseq):
+        norm = norm + tslots[k].astype(f32)
+    norm_ref[...] = norm
+    late.finish()
     total.finish()
-
-
-def closing(x, v, pieces, ps, n, zs, ys, cid, parts=2):
+    line.sent()
+    for d in range(1, nseq):
+        tiny(d).wait_send()
+
+
+def closing(x, branch, v, cols, h, pieces, ps, n, nseq, zs, ys, cid, parts=2):
     rows, width = x.shape
     sem = pltpu.SemaphoreType.DMA
     height = sum(piece.shape[0] for piece in pieces)
     height += -height % (16 * ys * zs)
-    part = height // ys
     w = v.shape[1]
+    fold = cols.shape[0] // ys
     count = len(ps)
+    tiny = (16, h.shape[1])
     return pl.pallas_call(
-        functools.partial(closing_kernel, n, zs, ys, parts, count, len(pieces)),
+        functools.partial(closing_kernel, n, nseq, zs, ys, parts, count, len(pieces)),
         out_shape=[
             jax.ShapeDtypeStruct((rows, width // n), f32),
-            jax.ShapeDtypeStruct((zs * v.shape[0], v.shape[1]), bf16),
+            jax.ShapeDtypeStruct((rows, branch.shape[1] // n), f32),
             jax.ShapeDtypeStruct((height, w), bf16),
+            jax.ShapeDtypeStruct((fold, w), f32),
+            jax.ShapeDtypeStruct(tiny, f32),
         ]
         + [PartSum.result(p, zs, ys) for p in ps],
-        in_specs=[VM] * (2 + len(pieces) + count),
-        out_specs=[VM] * (3 + count),
-        scratch_shapes=[pltpu.VMEM((height, w), bf16)] + reduce_scratch_shapes(x.shape, n, parts)
-        + [
-            pltpu.VMEM((ys - 1, part, w), bf16),
-            pltpu.VMEM((part, w), bf16),
-            pltpu.VMEM((zs - 1, part // zs, w), bf16),
+        in_specs=[VM] * (5 + len(pieces) + count),
+        out_specs=[VM] * (5 + count),
+        scratch_shapes=[
+            pltpu.VMEM((height, w), bf16),
+            pltpu.VMEM((zs * v.shape[0], w), bf16),
+            pltpu.VMEM((ys, fold, w), bf16),
+            pltpu.VMEM((ys - 1, fold, w), bf16),
+            pltpu.VMEM(tiny, bf16),
+            pltpu.VMEM((nseq,) + tiny, bf16),
         ]
-        + [sem((2, zs - 1))] * 2
-        + [sem((ys - 1,))] * 2
-        + [sem((zs - 1,))] * 4
-        + [sem(((ys - 1) * zs,))] * 2
-        + [spec for p in ps for spec in PartSum.specs(p, zs, ys)],
-        compiler_params=pltpu.CompilerParams(collective_id=cid, has_side_effects=True, vmem_limit_bytes=58 * 2**20),
+        + reduce_scratch_shapes(x.shape, n, parts)
+        + reduce_scratch_shapes(branch.shape, n, parts)
+        + GatherLine.specs(v, zs, ys)
+        + SumAll.specs(height, w, zs, ys)
+        + [spec for p in ps for spec in PartSum.specs(p, zs, ys)]
+        + [sem((ys - 1,)), sem((ys - 1,)), sem((nseq - 1,)), sem((nseq - 1,))],
+        compiler_params=pltpu.CompilerParams(collective_id=cid, has_side_effects=True, vmem_limit_bytes=60 * 2**20),
         cost_estimate=cost(70),
         name="closing",
-    )(x, v, *pieces, *ps)
-
-
-def last_kernel(n, zs, ys, p_ref, t_ref, out_ref, sum_ref, pslots, tslots, psend, precv, tsend, trecv):
-    me = lax.axis_index("seq")
-    z, y = me // ys, lax.rem(me, ys)
-    greet([{"seq": lax.rem(me + d, n)} for d in range(1, n)])
-    def part(d):
-        to = lax.rem(y + d, ys)
-        return pltpu.make_async_remote_copy(src_ref=p_ref.at[to], dst_ref=pslots.at[d - 1], send_sem=psend.at[d - 1], recv_sem=precv.at[d - 1], device_id=seq_at(z, to, ys), device_id_type=MESH)
-    def tiny(d):
-        return pltpu.make_async_remote_copy(src_ref=t_ref, dst_ref=tslots.at[lax.rem(me, n)], send_sem=tsend.at[d - 1], recv_sem=trecv.at[d - 1], device_id={"seq": lax.rem(me + d, n)}, device_id_type=MESH)
-    for d in range(1, n):
-        tiny(d).start()
-    for d in range(1, ys):
-        part(d).start()
-    tslots[me] = t_ref[...]
-    for d in range(1, n):
-        tiny(d).wait_recv()
-    total = tslots[0].astype(f32)
-    for k in range(1, n):
-        total = total + tslots[k].astype(f32)
-    sum_ref[...] = total
-    mine = p_ref[y].astype(f32)
-    for d in range(1, ys):
-        part(d).wait_recv()
-        mine = mine + pslots[d - 1].astype(f32)
-    out_ref[...] = mine
-    for d in range(1, n):
-        tiny(d).wait_send()
-    for d in range(1, ys):
-        part(d).wait_send()
-
-
-def last_sums(p, t, n, zs, ys, cid):
-    sem = pltpu.SemaphoreType.DMA
-    return pl.pallas_call(
-        functools.partial(last_kernel, n, zs, ys),
-        out_shape=[jax.ShapeDtypeStruct(p.shape[1:], f32), jax.ShapeDtypeStruct(t.shape, f32)],
-        in_specs=[VM] * 2,
-        out_specs=[VM] * 2,
-        scratch_shapes=[
-            pltpu.VMEM((ys - 1,) + p.shape[1:], bf16),
-            pltpu.VMEM((n,) + t.shape, bf16),
-            sem((ys - 1,)), sem((ys - 1,)), sem((n - 1,)), sem((n - 1,)),
-        ],
-        compiler_params=pltpu.CompilerParams(collective_id=cid, has_side_effects=True, vmem_limit_bytes=48 * 2**20),
-        cost_estimate=cost(25),
-        name="last_sums",
-    )(p, t)
+    )(x, branch, v, cols, h, *pieces, *ps)
 
 
 def passed_along(block, axis, distance):
@@ -1081,13 +1141,16 @@
     fold = width // nseq
     places = (zs, ys)
 
-    out_cols = {}
+    out_cols, w_copy = {}, {}
     stored = []
+    out_low = grad_rows.astype(bf16)
+    grad_mixed = dot(out_low, output_projection_weight[LAYERS - 1], (1, 1))
+    grad_mixed_line = tokens_of_line(grad_mixed.astype(bf16), zs, ys)
     for layer in range(LAYERS):
         last = layer == LAYERS - 1
         inv_rms = lax.rsqrt(jnp.mean(hidden * hidden, axis=-1, keepdims=True) + epsilon)
         normed = (hidden * inv_rms * norm_gain[layer]).astype(bf16)
-        w_in = lax.optimization_barrier(input_projection_weight)[layer]
+        w_in = w_copy[1] if layer > 0 else input_projection_weight[0]
         both = lax.dot_general(normed, w_in, (((1,), (0,)), ((), ())), preferred_element_type=f32)
         values, gate_pre = both[:, 0], both[:, 1]
         values3 = values.reshape(seqs, length, channels)
@@ -1107,19 +1170,24 @@
         end_state, total = scan_local(step_pre, activated, mats, keep, rates, seqs, [], places, 0)
         gate_act = jax.nn.silu(gate_pre)
         if last:
-            out_low = grad_rows.astype(bf16)
-            grad_mixed = dot(out_low, output_projection_weight[layer], (1, 1))
+            gate_line = tokens_of_line(gate_pre.astype(bf16), zs, ys)
             grad_scan = grad_mixed * gate_act
             start = scan_back_local(step_pre, grad_scan, mats, keep, rates, seqs)
-            state_in, lam_in = carry_over(total, rates, [end_state, start], nseq, next(ids), True, True)
+            state_in, lam_in, w_copy[0] = carry_over(
+                total, rates, [end_state, start], nseq, next(ids), True, True, taken=(input_projection_weight, 0)
+            )
         else:
-            (state_in,) = carry_over(total, rates, [end_state], nseq, next(ids), True, False)
+            state_in, w_copy[1] = carry_over(
+                total, rates, [end_state], nseq, next(ids), True, False, taken=(input_projection_weight, 1)
+            )
         keeping = (hidden, inv_rms, normed, gate_pre, gate_act, conv_out, activated, act_low, conv_pull, rank_low,
                    step_pre, mats, total, state_in)
         if last:
             stored.append(keeping)
             break
-        (y,) = scan_forward(step_pre, activated, mats, keep, rates, state_in, seqs, [], places, 0)
+        (y,) = scan_forward(
+            step_pre, activated, mats, keep, rates, state_in, seqs, [], places, 0, (grad_mixed_line,)
+        )
         scanned = y + skip_gain[layer] * activated
         mixed = (scanned * gate_act).astype(bf16)
         out_part = dot(mixed, output_projection_weight[layer], (1, 0)).astype(bf16)
@@ -1141,36 +1209,44 @@
             grad_scan = grad_mixed * gate_act
             grad_gate = (grad_mixed * scanned * silu_slope(gate_pre)).astype(bf16)
             start = scan_back_local(step_pre, grad_scan, mats, keep, rates, seqs)
-            (lam_in,) = carry_over(total, rates, [start], nseq, next(ids), False, True)
+            gate_all = tokens_of_line(grad_gate, zs, ys)
+            lam_in, grad_out_last, grad_gate_last = carry_over(
+                total, rates, [start], nseq, next(ids), False, True, [out_parts_last, gate_parts_last], places
+            )
         grad_skip = jnp.sum(grad_scan * activated, axis=0)
         if last:
-            plan = [(ColumnsLine, (4, 6), v) for v in (normed, out_low, stored[0][2])]
+            plan = [
+                (ColumnsLine, (3, 5), normed),
+                (ColumnsLine, (4, 6), out_low),
+                (ColumnsLine, (6, 8), stored[0][2]),
+            ]
         else:
             plan = [
                 (ColumnsLine, (2, 4), out_low),
-                (GatherLine, (4, 8), grad_gate),
-                (PartSum, (), out_parts_last),
-                (PartSum, (), gate_parts_last),
+                (PartSum, (), values_parts_last),
             ]
         grad_pre, grad_act, grad_mats, grad_decay, *others = scan_back(
             step_pre, activated, grad_scan, mats, keep, rates, skip_gain[layer][None], state_in, lam_in, seqs, int(last),
-            plan, places, next(ids), (stored[0][15],) if last else (),
+            plan, places, next(ids), (),
         )
         if last:
             y, normed_cols, out_cols[layer], early_cols = others
             scanned = y + skip_gain[layer] * activated
             mixed = (scanned * gate_act).astype(bf16)
-            mixed_all = tokens_of_line(mixed, zs, ys)
             grad_gate = (grad_mixed * scanned * silu_slope(gate_pre)).astype(bf16)
-            gate_all = tokens_of_line(grad_gate, zs, ys)
+            scanned_line = tokens_of_line(scanned.astype(bf16), zs, ys).astype(f32)
+            gates = gate_line.astype(f32)
+            mixed_all = (scanned_line * jax.nn.silu(gates)).astype(bf16)
+            gate_all = (grad_mixed_line.astype(f32) * scanned_line * silu_slope(gates)).astype(bf16)
         else:
-            out_cols[layer], gate_all, grad_out_last, grad_gate_last = others
+            out_cols[layer], grad_values_last = others
         grad_step_bias = jnp.sum(grad_pre, axis=0)
         pre_low = grad_pre.astype(bf16)
         grad_step_weight = dot(rank_low, pre_low, (0, 0))
         rank_part = dot(pre_low, step_weight[layer], (1, 1))
         grad_proj = ch_sum(
-            jnp.concatenate([rank_part, grad_mats[:, : 2 * STATE]], axis=-1), nch, next(ids)
+            jnp.concatenate([rank_part, grad_mats[:, : 2 * STATE]], axis=-1), nch, next(ids),
+            (gate_line,) if last else (),
         ).astype(bf16)
         grad_proj_weight = dot(grad_proj, act_low, (0, 0))
         grad_act = grad_act + dot(grad_proj, proj_weight[layer], (1, 1))
@@ -1181,7 +1257,7 @@
         grad_values = jnp.concatenate(
             [grad_values[:, : -(KERN - 1)], grad_values[:, -(KERN - 1) :] + returned], axis=1
         ).reshape(rows, channels).astype(bf16)
-        w_in = lax.optimization_barrier(input_projection_weight)[layer]
+        w_in = w_copy[layer]
         grad_both = jnp.stack([grad_values, grad_gate], axis=1)
         grad_part = lax.dot_general(grad_both, w_in, (((1, 2), (1, 2)), ((), ())), preferred_element_type=f32)
         scale_now = norm_gain[layer]
@@ -1192,8 +1268,7 @@
             values_parts_last = dot(normed_cols, values_last, (0, 0)).astype(bf16).reshape(ys, fold, channels)
             grad_normed = ch_reduce(grad_part.astype(bf16), nch, next(ids), True)
             out_part = dot(mixed, output_projection_weight[layer], (1, 0)).astype(bf16)
-            branch = ch_reduce(out_part, nch, next(ids), False)
-            result = (lax.dynamic_slice_in_dim(hidden, share_start, share, 1) + branch).astype(bf16)
+            hidden_last = lax.dynamic_slice_in_dim(hidden, share_start, share, 1)
         columns = [out_cols[layer][:, k * fold : (k + 1) * fold] for k in range(ys)]
         out_parts = jnp.stack([dot(mixed_all, k, (0, 0)).astype(bf16) for k in columns], axis=0)
         gate_parts = dot(normed_cols, gate_all, (0, 0)).astype(bf16).reshape(ys, fold, channels)
@@ -1213,22 +1288,19 @@
         beside = jnp.broadcast_to(beside[:, None], (rows, nch, LANES))
         send = jnp.concatenate([grad_part.astype(bf16).reshape(rows, nch, share), beside], axis=2)
         small[-1] = jnp.pad(misc, ((0, 16 - misc.shape[0]), (0, 0)))
-        got, values_all, sums, grad_gate_now, grad_out_weight, grad_values_last = closing(
-            send.reshape(rows, nch * (share + LANES)), grad_values, small + small_last, [gate_parts, out_parts, values_parts_last],
-            nch, zs, ys, next(ids),
+        hidden_share = lax.dynamic_slice_in_dim(hidden, share_start, share, 1)
+        scale_share = lax.dynamic_slice_in_dim(scale_now, share_start, share, 0)
+        got, branch, sums, grad_in_values, tiny, grad_gate_now, grad_out_weight = closing(
+            send.reshape(rows, nch * (share + LANES)), out_part, grad_values, jnp.swapaxes(normed_cols, 0, 1), hidden_share * inv_rms,
+            small + small_last, [gate_parts, out_parts], nch, nseq, zs, ys, next(ids),
         )
         grad_share, inner = got[:, :share], got[:, share : share + 1] + got[:, share + 1 : share + 2]
-        hidden_share = lax.dynamic_slice_in_dim(hidden, share_start, share, 1)
-        scale_share = lax.dynamic_slice_in_dim(scale_now, share_start, share, 0)
-        grad_norm = jnp.sum(grad_share * hidden_share * inv_rms, axis=0)
         grad_input = (
             lax.dynamic_slice_in_dim(grad_rows, share_start, share, 1)
             + inv_rms * scale_share * grad_share
             - hidden_share * (inv_rms * inv_rms * inv_rms) * inner / width
         )
-        parts = dot(normed_cols, values_all, (0, 0)).astype(bf16).reshape(ys, fold, channels)
-        tiny = jnp.pad(grad_norm.astype(bf16)[None], ((0, 15), (0, 0)))
-        grad_in_values, tiny = last_sums(parts, tiny, nseq, zs, ys, next(ids))
+        result = (hidden_last + branch).astype(bf16)
         total_small = sums.astype(f32)
         heights = [v.shape[0] for v in small_last]
         half = sum(heights)

time: 601 us -> 567 us (0.943)
  Pallas kernels: 399 us -> 339 us
  other arithmetic: 39.5 us -> 52 us
  waiting for transfers between devices: 4.96 us -> 16.8 us
  local copies, waits for them, and re-layouts: 45.9 us -> 52.8 us
    pallas_call x5, Pallas kernels: 153 us -> 97.9 us  [play_call(): pl.pallas_call(after(played(kernel, counts, kinds, places), len(arrays),...]
    unnamed x245 -> x263, local copies, waits for them, and re-layouts: 23.6 us -> 35.5 us
    slice x2 -> x3, local copies, waits for them, and re-layouts: 14.8 us -> 3.08 us  [the longest x2 3.06 us: local(): w_in = w_copy[1] if layer > 0 else input_projection_weight[0]]
    pallas_call x3 -> x2, Pallas kernels: 44.1 us -> 33.4 us  [ch_reduce(): pl.pallas_call(functools.partial(reduce_kernel, n, parts, gather), out_sh...]
    all_gather x4 -> x6, waiting for transfers between devices: 1.33 us -> 9.81 us  [tokens_of_line(): lax.all_gather(rows, 'seq', axis_index_groups=lines(zs, ys), tiled=True)]
    pallas_call x5 -> x4, Pallas kernels: 158 us -> 163 us  [the longest x1 91.4 us: closing(): pl.pallas_call(functools.partial(closing_kernel, n, nseq, zs, ys, parts,...]
    dot_general x24 -> x23, matrix products: 49.4 us -> 51.1 us  [dot(): lax.dot_general(a, b, ((contract[:1], contract[1:]), ((), ())), preferred...]
  transfers between devices with their start and end apart: 9 -> 11, of which waited for: 2 -> 5; matrix products, arithmetic and copies ran while one was open for 13% -> 17% of each run, Pallas kernels for 34% -> 39%
where the time goes in v4:
time: 567 us; the launch traced here: 560 us
  Pallas kernels  339 us (60%)
  matrix products  67.5 us (12%)
  local copies, waits for them, and re-layouts  52.8 us (9%)
  other arithmetic  52 us (9%)
  waiting for transfers between devices  16.8 us (3%)
  between operations  16.2 us (3%)
  starting transfers between devices  15.6 us (3%)
    pallas_call x5, Pallas kernels, play_call(): pl.pallas_call(after(played(kernel, counts, kinds, places), len(arrays),...  97.9 us
    pallas_call x1, Pallas kernels, closing(): pl.pallas_call(functools.partial(closing_kernel, n, nseq, zs, ys, parts,...  91.4 us
    pallas_call x3, Pallas kernels, carry_over(): pl.pallas_call(functools.partial(carry_kernel, n, int(fwd), int(rev), len...  71.7 us
    dot_general x23, matrix products, dot(): lax.dot_general(a, b, ((contract[:1], contract[1:]), ((), ())), preferred...  51.1 us
    unnamed x263, local copies, waits for them, and re-layouts  35.5 us
    pallas_call x2, Pallas kernels, ch_reduce(): pl.pallas_call(functools.partial(reduce_kernel, n, parts, gather), out_sh...  33.4 us
    pallas_call x4, Pallas kernels, ch_sum(): pl.pallas_call(after(functools.partial(ch_sum_kernel, n), 1, pins), out_s...  29 us
    pallas_call x2, Pallas kernels, scan_back_local(): pl.pallas_call(after(functools.partial(back_local_kernel, seqs), 5, pins)...  15.6 us
  transfers between devices with their start and end apart: 11, of which 5 were waited for; matrix products, arithmetic and copies ran while one was open for 17% of the time, Pallas kernels for 39%

profile of v4, /device:TPU:10, one launch (start us, length us, event | category | flops | bytes accessed | tf_op | source)
XLA Modules:
  0.0 559.8 jit_solution(16571800843618689478)
XLA Ops:
  11.4 5.0 fusion.142
  34.6 6.8 %ch_sum.4 = f32[256,160]{1,0:T(8,128)S(1)} custom-call(f32[256,160]{1,0:T(8,128)S(1)} %fusion.92.refs_0_), custom_call_target="tpu_custom_call" | custom-call | flops 1000000000 | tf_op jit(solution)/shard_map/ch_sum/pallas_call | solution.py:434
  44.6 7.9 %scan_local.2 = (f32[2,16,1024]{2,1,0:T(8,128)}, f32[2,1024]{1,0:T(2,128)}) custom-call(f32[256,1024]{1,0:T(8,128)} %convolution_add_fusion.3.refs_0_, f32[256,1024]{1,0:T(8,128)} %bitcast_multiply_fusion.5.refs_1_, f32[256,32]{1,0:T(8,128)} %slice.284.refs_2_.refs_3_, f32[256,1]{1,0:T(8,128)} %copy.38.refs_3_.refs_4_, ...), custom_call_target="tpu_custom_call" | custom-call | flops 800000000 | tf_op jit(solution)/shard_map/scan_local/pallas_call | solution.py:150
  54.0 17.8 %carry_over.3 = (f32[2,16,1024]{2,1,0:T(8,128)S(1)}, bf16[2048,2,1024]{2,1,0:T(2,128)(2,1)S(1)}) custom-call(f32[2,1024]{1,0:T(2,128)S(1)} %copy-done.9, f32[16,1024]{1,0:T(8,128)S(1)} %copy-done.2, f32[2,16,1024]{2,1,0:T(8,128)S(1)} %copy-done.7, bf16[2,2048,2,1024]{3,2,1,0:T(2,128)(2,1)} %refs_4_.1), custom_call_target="tpu_custom_call" | custom-call | flops 1900000000 | tf_op jit(solution)/shard_map/carry_over/pallas_call | solution.py:691
  75.8 11.2 %scan_forward.1 = f32[256,1024]{1,0:T(8,128)} custom-call(f32[256,1024]{1,0:T(8,128)} %convolution_add_fusion.3.refs_0_, f32[256,1024]{1,0:T(8,128)} %bitcast_multiply_fusion.5.refs_1_, f32[256,32]{1,0:T(8,128)} %slice.284.refs_2_.refs_3_, f32[256,1]{1,0:T(8,128)} %copy.38.refs_3_.refs_4_, f32[16,1024]{1,0:T(8,128)} %get-tuple-element.156.refs_4_.refs_1_.refs_5_, ...), custom_call_target="tpu_custom_call" | custom-call | flops 1100000000 | tf_op jit(solution)/shard_map/scan_forward/pallas_call | solution.py:150
  92.8 16.9 %ch_reduce.2 = f32[256,2048]{1,0:T(8,128)S(1)} custom-call(bf16[256,2048]{1,0:T(8,128)(2,1)S(1)} %fusion.36.refs_0_), custom_call_target="tpu_custom_call" | custom-call | flops 1800000000 | tf_op jit(solution)/shard_map/ch_reduce/pallas_call | solution.py:615
  128.0 7.1 %ch_sum.5 = f32[256,160]{1,0:T(8,128)S(1)} custom-call(f32[256,160]{1,0:T(8,128)S(1)} %fusion.89.refs_0_), custom_call_target="tpu_custom_call" | custom-call | flops 1000000000 | tf_op jit(solution)/shard_map/ch_sum/pallas_call | solution.py:434
  139.8 7.9 %scan_local.3 = (f32[2,16,1024]{2,1,0:T(8,128)}, f32[2,1024]{1,0:T(2,128)}) custom-call(f32[256,1024]{1,0:T(8,128)} %convolution_add_fusion.2.refs_0_, f32[256,1024]{1,0:T(8,128)} %get-tuple-element.151.refs_1_, f32[256,32]{1,0:T(8,128)} %slice.306.refs_2_.refs_3_, f32[256,1]{1,0:T(8,128)} %copy.38.refs_3_.refs_4_, ...), custom_call_target="tpu_custom_call" | custom-call | flops 800000000 | tf_op jit(solution)/shard_map/scan_local/pallas_call | solution.py:150
  147.7 7.8 %scan_back_local.2.refs_3_ = f32[2,16,1024]{2,1,0:T(8,128)} custom-call(f32[256,1024]{1,0:T(8,128)} %convolution_add_fusion.2.refs_0_, f32[256,1024]{1,0:T(8,128)} %get-tuple-element.116.refs_1_.refs_2_, f32[256,32]{1,0:T(8,128)} %slice.306.refs_2_.refs_3_, f32[256,1]{1,0:T(8,128)} %copy.38.refs_3_.refs_4_, f32[16,1024]{1,0:T(8,128)} %get-tuple-element.155.refs_4_.refs_1_.refs_5_), custom_call_target="tpu_custom_call" | custom-call | flops 800000000 | tf_op jit(solution)/shard_map/scan_back_local/pallas_call | solution.py:253
  156.5 21.8 %carry_over.4 = (f32[2,16,1024]{2,1,0:T(8,128)S(1)}, f32[2,16,1024]{2,1,0:T(8,128)S(1)}, bf16[2048,2,1024]{2,1,0:T(2,128)(2,1)S(1)}) custom-call(f32[2,1024]{1,0:T(2,128)S(1)} %copy-done.11, f32[16,1024]{1,0:T(8,128)S(1)} %copy-done.4, f32[2,16,1024]{2,1,0:T(8,128)S(1)} %copy-done.5, f32[2,16,1024]{2,1,0:T(8,128)S(1)} %copy-done.6, ...), custom_call_target="tpu_custom_call" | custom-call | flops 1900000000 | tf_op jit(solution)/shard_map/carry_over/pallas_call | solution.py:691
  183.0 36.6 %scan_back.2 = (f32[256,1024]{1,0:T(8,128)}, f32[256,1024]{1,0:T(8,128)}, f32[256,128]{1,0:T(8,128)}, f32[16,1024]{1,0:T(8,128)}, f32[256,1024]{1,0:T(8,128)}, /...) custom-call(f32[256,1024]{1,0:T(8,128)} %convolution_add_fusion.2.refs_0_, ...), custom_call_target="tpu_custom_call" | custom-call | flops 2600000000 | tf_op jit(solution)/shard_map/scan_back/pallas_call | solution.py:150
  224.7 7.8 %ch_sum.6 = f32[256,160]{1,0:T(8,128)S(1)} custom-call(f32[256,160]{1,0:T(8,128)S(1)} %pad_maximum_fusion.8.refs_0_, bf16[1024,1024]{1,0:T(8,128)(2,1)S(1)} %copy-done), custom_call_target="tpu_custom_call" | custom-call | flops 1000000000 | tf_op jit(solution)/shard_map/ch_sum/pallas_call | solution.py:434
  248.5 4.7 fusion.33.b_ref
  261.1 8.1 %all-gather.11.cloned.1.call-done = bf16[1024,1024]{1,0:T(8,128)(2,1)} async-done(((bf16[256,1024]{1,0:T(8,128)(2,1)}), bf16[1024,1024]{1,0:T(8,128)(2,1)}) %all-gather.11.cloned.1.call-update) | async-done | bytes 2097168 | tf_op jit(solution)/shard_map/all_gather | solution.py:1108
  282.2 16.5 %ch_reduce.3 = f32[256,2048]{1,0:T(8,128)S(1)} custom-call(bf16[256,2048]{1,0:T(8,128)(2,1)S(1)} %fusion.39.refs_0_), custom_call_target="tpu_custom_call" | custom-call | flops 1800000000 | tf_op jit(solution)/shard_map/ch_reduce/pallas_call | solution.py:615
  303.0 6.6 %multiply_reduce_fusion.9 = (f32[1024]{0:T(1024)}, f32[256,1024]{1,0:T(8,128)}, bf16[256,1024]{1,0:T(8,128)(2,1)}, f32[256,1024]{1,0:T(8,128)}) fusion(f32[2,128,1024]{2,1,0:T(8,128)S(1)} %copy-done.44, f32[256,2,1024]{2,0,1:T(8,128)S(1)} %copy-done.48, f32[256,1024]{1,0:T(8,128)S(1)} %copy-done.53, f32[1024]{0:T(1024)S(1)} %bitcast.354, ...), kind=kOutput, calls=%fused_computation.125 | convolution fusion | flops 1080032256 | bytes 11018240 | tf_op jit(solution)/shard_map/dot_general | solution.py:1100
  309.6 7.8 %scan_back_local.3.refs_2_ = f32[2,16,1024]{2,1,0:T(8,128)} custom-call(f32[256,1024]{1,0:T(8,128)} %convolution_add_fusion.3.refs_0_, f32[256,1024]{1,0:T(8,128)} %get-tuple-element.118.refs_1_.refs_2_, f32[256,32]{1,0:T(8,128)} %slice.284.refs_2_.refs_3_, f32[256,1]{1,0:T(8,128)} %copy.38.refs_3_.refs_4_, f32[16,1024]{1,0:T(8,128)} %get-tuple-element.156.refs_4_.refs_1_.refs_5_), custom_call_target="tpu_custom_call" | custom-call | flops 800000000 | tf_op jit(solution)/shard_map/scan_back_local/pallas_call | solution.py:253
  319.5 32.1 %carry_over.5 = (f32[2,16,1024]{2,1,0:T(8,128)S(1)}, f32[1024,256]{1,0:T(8,128)S(1)}, f32[256,1024]{1,0:T(8,128)S(1)}) custom-call(f32[2,1024]{1,0:T(2,128)S(1)} %copy-done.10, f32[16,1024]{1,0:T(8,128)S(1)} %copy-done.3, f32[2,16,1024]{2,1,0:T(8,128)S(1)} %copy-done.17, bf16[2,1024,256]{2,1,0:T(8,128)(2,1)S(1)} %pad_maximum_fusion.5.refs_3_, ...), custom_call_target="tpu_custom_call" | custom-call | flops 1900000000 | tf_op jit(solution)/shard_map/carry_over/pallas_call | solution.py:691
  356.5 34.4 %scan_back.3 = (f32[256,1024]{1,0:T(8,128)}, f32[256,1024]{1,0:T(8,128)}, f32[256,128]{1,0:T(8,128)}, f32[16,1024]{1,0:T(8,128)}, bf16[1024,512]{1,0:T(8,128)(2,1)}, /*index=5*/f32[256,1024]{1,0:T(8,128)}) custom-call(f32[256,1024]{1,0:T(8,128)} %convolution_add_fusion.3.refs_0_, f32[256,1024]{1,0:T(8,128)} %bitcast_multiply_fusion.5.refs_1_, ...), custom_call_target="tpu_custom_call" | custom-call | flops 2300000000 | tf_op jit(solution)/shard_map/scan_back/pallas_call | solution.py:150
  393.3 7.3 %ch_sum.7 = f32[256,160]{1,0:T(8,128)S(1)} custom-call(f32[256,160]{1,0:T(8,128)S(1)} %pad_maximum_fusion.9.refs_0_), custom_call_target="tpu_custom_call" | custom-call | flops 1000000000 | tf_op jit(solution)/shard_map/ch_sum/pallas_call | solution.py:434
  422.7 4.2 convolution_convert_fusion
  430.2 7.5 %fusion.136 = (bf16[256,2048]{1,0:T(8,128)(2,1)}, f32[256]{0:T(256)S(1)}) fusion(bf16[2,128,2048]{2,1,0:T(8,128)(2,1)S(1)} %copy-done.24, f32[2048]{0:T(1024)S(1)} %bitcast.324, bf16[2048,2,1024]{2,1,0:T(2,128)(2,1)} %copy-done.12, bf16[256,1,1024]{2,0,1:T(8,128)(2,1)S(1)} %bitcast.310, bf16[256,1,1024]{2,0,1:T(8,128)(2,1)S(1)} %bitcast.311), kind=kOutput, calls=%fused_computation.264 | convolution fusion | flops 2150629120 | bytes 11543552 | tf_op jit(solution)/shard_map/dot_general | solution.py:1262
  441.7 91.4 %closing.1 = (f32[256,640]{1,0:T(8,128)}, f32[256,512]{1,0:T(8,128)}, bf16[640,1024]{1,0:T(8,128)(2,1)}, f32[256,1024]{1,0:T(8,128)}, f32[16,512]{1,0:T(8,128)},...) custom-call(bf16[256,2560]{1,0:T(8,128)(2,1)} %bitcast.299, bf16[256,2048]{1,0:T(8,128)(2,1)} %fusion.33.b_ref, ...), custom_call_target="tpu_custom_call" | custom-call | flops 7000000000 | tf_op jit(solution)/shard_map/closing/pallas_call | solution.py:1041
  538.7 5.3 copy.52
  (405 shorter events, 163.4 us)
Async XLA Ops:
  7.2 68.6 %all-gather.7.cloned.1.call-start = ((), (), s32[]{:S(2)}) async-start(), calls=%async_computation | async-start | bytes 2621440 | tf_op jit(solution)/shard_map/all_gather | solution.py:1108
  8.0 22.1 %collective-permute-start.1 = (f32[2,3]{1,0:T(2,128)S(1)}, f32[2,3]{1,0:T(2,128)S(1)}, u32[]{:S(2)}, u32[]{:S(2)}) collective-permute-start(f32[2,3]{1,0:T(2,128)S(1)} %slice.271), channel_id=1, source_target_pairs={{0,4},{4,8},{8,12},{12,16},{16,20},{20,24},{24,28},{1,5},{5,9},{9,... | collective-permute-start | bytes 80 | tf_op jit(solution)/shard_map/ppermute | solution.py:1076
  16.5 206.7 %all-gather.9.cloned.1.call-start = ((), (), s32[]{:S(2)}) async-start(), calls=%async_computation.1 | async-start | bytes 2621440 | tf_op jit(solution)/shard_map/all_gather | solution.py:1108
  16.9 226.0 %copy-start.99 = (f32[256]{0:T(256)}, f32[256]{0:T(256)S(1)}, u32[]{:S(2)}) copy-start(f32[256]{0:T(256)S(1)} %get-tuple-element.180) | copy-start | bytes 3076
  24.7 7.4 %collective-permute-start = (f32[2,3,1024]{2,1,0:T(4,128)S(1)}, f32[2,3,1024]{2,1,0:T(4,128)S(1)}, u32[]{:S(2)}, u32[]{:S(2)}) collective-permute-start(f32[2,3,1024]{2,1,0:T(4,128)S(1)} %slice.339), channel_id=1, source_target_pairs={{0,4},{4,8},{8,12},{12,16},{16,20},{20,24},{24,28},{1,5},{5,9},{9,... | collective-permute-start | bytes 73736 | tf_op jit(solution)/shard_map/ppermute | solution.py:1076
  28.7 204.7 %copy-start.97 = (f32[2,128]{1,0:T(2,128)}, f32[2,128]{1,0:T(2,128)S(1)}, u32[]{:S(2)}) copy-start(f32[2,128]{1,0:T(2,128)S(1)} %get-tuple-element.177) | copy-start | bytes 3076
  29.4 57.6 %copy-start.106 = (f32[1,1024]{1,0:T(1,128)}, f32[1,1024]{1,0:T(1,128)S(1)}, u32[]{:S(2)}) copy-start(f32[1,1024]{1,0:T(1,128)S(1)} %get-tuple-element.168.refs_6_) | copy-start | bytes 12292
  30.2 203.3 %copy-start.82 = (f32[2,128]{1,0:T(2,128)}, f32[2,128]{1,0:T(2,128)S(1)}, u32[]{:S(2)}) copy-start(f32[2,128]{1,0:T(2,128)S(1)} %get-tuple-element.175) | copy-start | bytes 3076
  30.2 203.3 %copy-start.84 = (f32[2,128]{1,0:T(2,128)}, f32[2,128]{1,0:T(2,128)S(1)}, u32[]{:S(2)}) copy-start(f32[2,128]{1,0:T(2,128)S(1)} %get-tuple-element.173) | copy-start | bytes 3076
  30.2 203.3 %copy-start.86 = (f32[2,128]{1,0:T(2,128)}, f32[2,128]{1,0:T(2,128)S(1)}, u32[]{:S(2)}) copy-start(f32[2,128]{1,0:T(2,128)S(1)} %get-tuple-element.174) | copy-start | bytes 3076
  75.8 11.2 %copy-start.43 = (f32[2,128,1024]{2,1,0:T(8,128)S(1)}, f32[2,128,1024]{2,1,0:T(8,128)}, u32[]{:S(2)}) copy-start(f32[2,128,1024]{2,1,0:T(8,128)} %copy-done.42) | copy-start | bytes 3145732
  92.8 20.6 %slice-start = ((s8[8388608]{0:T(1024)(128)(4,1)}), s8[4194304]{0:T(1024)(128)(4,1)S(1)}, s32[]{:S(2)}) async-start(s8[8388608]{0:T(1024)(128)(4,1)} %bitcast.283), calls=%async_computation.6 | async-start | bytes 8388608
  118.6 150.6 %all-gather.11.cloned.1.call-start = ((), (), s32[]{:S(2)}) async-start(), calls=%async_computation.2 | async-start | bytes 2621440 | tf_op jit(solution)/shard_map/all_gather | solution.py:1108
  120.0 6.7 %collective-permute-start.2 = (f32[2,3,1024]{2,1,0:T(4,128)S(1)}, f32[2,3,1024]{2,1,0:T(4,128)S(1)}, u32[]{:S(2)}, u32[]{:S(2)}) collective-permute-start(f32[2,3,1024]{2,1,0:T(4,128)S(1)} %slice.351), channel_id=1, source_target_pairs={{0,4},{4,8},{8,12},{12,16},{16,20},{20,24},{24,28},{1,5},{5,9},{9,... | collective-permute-start | bytes 73736 | tf_op jit(solution)/shard_map/ppermute | solution.py:1076
  182.9 36.6 %copy-start.108 = (f32[1,1024]{1,0:T(1,128)S(1)}, f32[1,1024]{1,0:T(1,128)}, u32[]{:S(2)}) copy-start(f32[1,1024]{1,0:T(1,128)} %get-tuple-element.167.refs_6_) | copy-start | bytes 12292
  222.7 129.6 %all-gather.13.cloned.1.call-start = ((), (), s32[]{:S(2)}) async-start(), calls=%async_computation.3 | async-start | bytes 2621440 | tf_op jit(solution)/shard_map/all_gather | solution.py:1108
  234.4 6.0 %collective-permute-start.3 = (f32[2,3,1024]{2,1,0:T(4,128)S(1)}, f32[2,3,1024]{2,1,0:T(4,128)S(1)}, u32[]{:S(2)}, u32[]{:S(2)}) collective-permute-start(f32[2,3,1024]{2,1,0:T(4,128)S(1)} %pad_add_fusion.3), channel_id=1, source_target_pairs={{4,0},{8,4},{12,8},{16,12},{20,16},{24,20},{28,24},{5,1},{9,5},{13... | collective-permute-start | bytes 73736 | tf_op jit(solution)/shard_map/ppermute | solution.py:1076
  241.3 172.4 %all-gather.17.cloned.1.call-start = ((), (), s32[]{:S(2)}) async-start(), calls=%async_computation.5 | async-start | bytes 2621440 | tf_op jit(solution)/shard_map/all_gather | solution.py:1108
  245.1 177.6 %all-gather.15.cloned.1.call-start = ((), (), s32[]{:S(2)}) async-start(), calls=%async_computation.4 | async-start | bytes 2621440 | tf_op jit(solution)/shard_map/all_gather | solution.py:1108
  254.3 14.9 %copy-start.1 = (bf16[1024,1024]{1,0:T(8,128)(2,1)S(1)}, bf16[1024,1024]{1,0:T(8,128)(2,1)}, u32[]{:S(2)}) copy-start(bf16[1024,1024]{1,0:T(8,128)(2,1)} %all-gather.9.cloned.1.call-done.refs_1_) | copy-start | bytes 6291460
  282.2 16.5 %copy-start.20 = (f32[256,2048]{1,0:T(8,128)S(1)}, f32[256,2048]{1,0:T(8,128)}, u32[]{:S(2)}) copy-start(f32[256,2048]{1,0:T(8,128)} %copy-done.19) | copy-start | bytes 6291460
  282.2 16.5 %copy-start.112 = (f32[256]{0:T(256)S(1)}, f32[256]{0:T(256)}, u32[]{:S(2)}) copy-start(f32[256]{0:T(256)} %copy-done.111) | copy-start | bytes 3076
  356.5 34.4 %copy-start.62 = (bf16[2,128,1024]{2,1,0:T(8,128)(2,1)S(1)}, bf16[2,128,1024]{2,1,0:T(8,128)(2,1)}, u32[]{:S(2)}) copy-start(bf16[2,128,1024]{2,1,0:T(8,128)(2,1)} %param.21) | copy-start | bytes 1572868
  405.2 23.4 %collective-permute-start.4 = (f32[2,3,1024]{2,1,0:T(4,128)}, f32[2,3,1024]{2,1,0:T(4,128)S(1)}, u32[]{:S(2)}, u32[]{:S(2)}) collective-permute-start(f32[2,3,1024]{2,1,0:T(4,128)} %pad_add_fusion.2), channel_id=1, source_target_pairs={{4,0},{8,4},{12,8},{16,12},{20,16},{24,20},{28,24},{5,1},{9,5},{13... | collective-permute-start | bytes 73736 | tf_op jit(solution)/shard_map/ppermute | solution.py:1076
  (117 other events, 475.8 us)
Sparse Core Ops, SparseCore 0:
  16.6 48.3 all-gather.6
  118.7 51.6 all-gather.8
  222.8 46.3 all-gather.10
  270.6 43.9 all-gather.12
  316.0 54.2 all-gather.16
  372.3 50.3 all-gather.14

commit v5 on v4

--- a/solution.py
+++ b/solution.py
@@ -1210,8 +1210,8 @@
             grad_gate = (grad_mixed * scanned * silu_slope(gate_pre)).astype(bf16)
             start = scan_back_local(step_pre, grad_scan, mats, keep, rates, seqs)
             gate_all = tokens_of_line(grad_gate, zs, ys)
-            lam_in, grad_out_last, grad_gate_last = carry_over(
-                total, rates, [start], nseq, next(ids), False, True, [out_parts_last, gate_parts_last], places
+            lam_in, grad_out_last = carry_over(
+                total, rates, [start], nseq, next(ids), False, True, [out_parts_last], places
             )
         grad_skip = jnp.sum(grad_scan * activated, axis=0)
         if last:
@@ -1224,6 +1224,7 @@
             plan = [
                 (ColumnsLine, (2, 4), out_low),
                 (PartSum, (), values_parts_last),
+                (PartSum, (), gate_parts_last),
             ]
         grad_pre, grad_act, grad_mats, grad_decay, *others = scan_back(
             step_pre, activated, grad_scan, mats, keep, rates, skip_gain[layer][None], state_in, lam_in, seqs, int(last),
@@ -1235,11 +1236,8 @@
             mixed = (scanned * gate_act).astype(bf16)
             grad_gate = (grad_mixed * scanned * silu_slope(gate_pre)).astype(bf16)
             scanned_line = tokens_of_line(scanned.astype(bf16), zs, ys).astype(f32)
-            gates = gate_line.astype(f32)
-            mixed_all = (scanned_line * jax.nn.silu(gates)).astype(bf16)
-            gate_all = (grad_mixed_line.astype(f32) * scanned_line * silu_slope(gates)).astype(bf16)
         else:
-            out_cols[layer], grad_values_last = others
+            out_cols[layer], grad_values_last, grad_gate_last = others
         grad_step_bias = jnp.sum(grad_pre, axis=0)
         pre_low = grad_pre.astype(bf16)
         grad_step_weight = dot(rank_low, pre_low, (0, 0))
@@ -1267,6 +1265,10 @@
             values_last = tokens_of_line(grad_values, zs, ys)
             values_parts_last = dot(normed_cols, values_last, (0, 0)).astype(bf16).reshape(ys, fold, channels)
             grad_normed = ch_reduce(grad_part.astype(bf16), nch, next(ids), True)
+            scanned_line = scanned_line + 0.0 * grad_normed[0, 0]
+            gates = gate_line.astype(f32)
+            mixed_all = (scanned_line * jax.nn.silu(gates)).astype(bf16)
+            gate_all = (grad_mixed_line.astype(f32) * scanned_line * silu_slope(gates)).astype(bf16)
             out_part = dot(mixed, output_projection_weight[layer], (1, 0)).astype(bf16)
             hidden_last = lax.dynamic_slice_in_dim(hidden, share_start, share, 1)
         columns = [out_cols[layer][:, k * fold : (k + 1) * fold] for k in range(ys)]

time: 567 us -> 562 us (level)
  Pallas kernels: 339 us -> 333 us
  waiting for transfers between devices: 16.8 us -> 22.7 us
    pallas_call x3, Pallas kernels: 71.7 us -> 62.7 us  [carry_over(): pl.pallas_call(functools.partial(carry_kernel, n, int(fwd), int(rev), len...]
    unnamed x263 -> x179, local copies, waits for them, and re-layouts: 35.5 us -> 31.8 us
  transfers between devices with their start and end apart: 11 -> 11, of which waited for: 5 -> 4; matrix products, arithmetic and copies ran while one was open for 17% -> 18% of each run, Pallas kernels for 39% -> 38%
where the time goes in v5:
time: 562 us; the launch traced here: 554 us
  Pallas kernels  333 us (59%)
  matrix products  71.6 us (13%)
  local copies, waits for them, and re-layouts  47.5 us (8%)
  other arithmetic  47.1 us (8%)
  waiting for transfers between devices  22.7 us (4%)
  between operations  16.7 us (3%)
  starting transfers between devices  16 us (3%)
    pallas_call x5, Pallas kernels, play_call(): pl.pallas_call(after(played(kernel, counts, kinds, places), len(arrays),...  101 us
    pallas_call x1, Pallas kernels, closing(): pl.pallas_call(functools.partial(closing_kernel, n, nseq, zs, ys, parts,...  91.6 us
    pallas_call x3, Pallas kernels, carry_over(): pl.pallas_call(functools.partial(carry_kernel, n, int(fwd), int(rev), len...  62.7 us
    dot_general x23, matrix products, dot(): lax.dot_general(a, b, ((contract[:1], contract[1:]), ((), ())), preferred...  52.5 us
    pallas_call x2, Pallas kernels, ch_reduce(): pl.pallas_call(functools.partial(reduce_kernel, n, parts, gather), out_sh...  33.7 us
    unnamed x179, local copies, waits for them, and re-layouts  31.8 us
    pallas_call x4, Pallas kernels, ch_sum(): pl.pallas_call(after(functools.partial(ch_sum_kernel, n), 1, pins), out_s...  28.5 us
    ppermute x5, starting transfers between devices, passed_along(): return lax.ppermute(block, axis, route)  15.7 us
  transfers between devices with their start and end apart: 11, of which 4 were waited for; matrix products, arithmetic and copies ran while one was open for 18% of the time, Pallas kernels for 38%

profile of v5, /device:TPU:10, one launch (start us, length us, event | category | flops | bytes accessed | tf_op | source)
XLA Modules:
  0.0 554.2 jit_solution(4023234966279854450)
XLA Ops:
  11.4 5.0 fusion.143
  33.5 6.8 %ch_sum.4 = f32[256,160]{1,0:T(8,128)S(1)} custom-call(f32[256,160]{1,0:T(8,128)S(1)} %fusion.93.refs_0_), custom_call_target="tpu_custom_call" | custom-call | flops 1000000000 | tf_op jit(solution)/shard_map/ch_sum/pallas_call | solution.py:434
  43.5 7.8 %scan_local.2 = (f32[2,16,1024]{2,1,0:T(8,128)}, f32[2,1024]{1,0:T(2,128)}) custom-call(f32[256,1024]{1,0:T(8,128)} %convolution_add_fusion.3.refs_0_, f32[256,1024]{1,0:T(8,128)} %bitcast_multiply_fusion.5.refs_1_, f32[256,32]{1,0:T(8,128)} %slice.287.refs_2_.refs_3_, f32[256,1]{1,0:T(8,128)} %copy.38.refs_3_.refs_4_, ...), custom_call_target="tpu_custom_call" | custom-call | flops 800000000 | tf_op jit(solution)/shard_map/scan_local/pallas_call | solution.py:150
  52.9 18.9 %carry_over.3 = (f32[2,16,1024]{2,1,0:T(8,128)S(1)}, bf16[2048,2,1024]{2,1,0:T(2,128)(2,1)S(1)}) custom-call(f32[2,1024]{1,0:T(2,128)S(1)} %copy-done.9, f32[16,1024]{1,0:T(8,128)S(1)} %copy-done.2, f32[2,16,1024]{2,1,0:T(8,128)S(1)} %copy-done.7, bf16[2,2048,2,1024]{3,2,1,0:T(2,128)(2,1)} %refs_4_.1), custom_call_target="tpu_custom_call" | custom-call | flops 1900000000 | tf_op jit(solution)/shard_map/carry_over/pallas_call | solution.py:691
  75.8 11.0 %scan_forward.1 = f32[256,1024]{1,0:T(8,128)} custom-call(f32[256,1024]{1,0:T(8,128)} %convolution_add_fusion.3.refs_0_, f32[256,1024]{1,0:T(8,128)} %bitcast_multiply_fusion.5.refs_1_, f32[256,32]{1,0:T(8,128)} %slice.287.refs_2_.refs_3_, f32[256,1]{1,0:T(8,128)} %copy.38.refs_3_.refs_4_, f32[16,1024]{1,0:T(8,128)} %get-tuple-element.156.refs_4_.refs_1_.refs_5_, ...), custom_call_target="tpu_custom_call" | custom-call | flops 1100000000 | tf_op jit(solution)/shard_map/scan_forward/pallas_call | solution.py:150
  92.7 16.9 %ch_reduce.2 = f32[256,2048]{1,0:T(8,128)S(1)} custom-call(bf16[256,2048]{1,0:T(8,128)(2,1)S(1)} %fusion.37.refs_0_), custom_call_target="tpu_custom_call" | custom-call | flops 1800000000 | tf_op jit(solution)/shard_map/ch_reduce/pallas_call | solution.py:615
  126.8 7.1 %ch_sum.5 = f32[256,160]{1,0:T(8,128)S(1)} custom-call(f32[256,160]{1,0:T(8,128)S(1)} %fusion.90.refs_0_), custom_call_target="tpu_custom_call" | custom-call | flops 1000000000 | tf_op jit(solution)/shard_map/ch_sum/pallas_call | solution.py:434
  138.1 7.8 %scan_local.3 = (f32[2,16,1024]{2,1,0:T(8,128)}, f32[2,1024]{1,0:T(2,128)}) custom-call(f32[256,1024]{1,0:T(8,128)} %convolution_add_fusion.2.refs_0_, f32[256,1024]{1,0:T(8,128)} %get-tuple-element.151.refs_1_, f32[256,32]{1,0:T(8,128)} %slice.309.refs_2_.refs_3_, f32[256,1]{1,0:T(8,128)} %copy.38.refs_3_.refs_4_, ...), custom_call_target="tpu_custom_call" | custom-call | flops 800000000 | tf_op jit(solution)/shard_map/scan_local/pallas_call | solution.py:150
  145.9 7.8 %scan_back_local.2.refs_3_ = f32[2,16,1024]{2,1,0:T(8,128)} custom-call(f32[256,1024]{1,0:T(8,128)} %convolution_add_fusion.2.refs_0_, f32[256,1024]{1,0:T(8,128)} %get-tuple-element.116.refs_1_.refs_2_, f32[256,32]{1,0:T(8,128)} %slice.309.refs_2_.refs_3_, f32[256,1]{1,0:T(8,128)} %copy.38.refs_3_.refs_4_, f32[16,1024]{1,0:T(8,128)} %get-tuple-element.155.refs_4_.refs_1_.refs_5_), custom_call_target="tpu_custom_call" | custom-call | flops 800000000 | tf_op jit(solution)/shard_map/scan_back_local/pallas_call | solution.py:253
  154.6 22.4 %carry_over.4 = (f32[2,16,1024]{2,1,0:T(8,128)S(1)}, f32[2,16,1024]{2,1,0:T(8,128)S(1)}, bf16[2048,2,1024]{2,1,0:T(2,128)(2,1)S(1)}) custom-call(f32[2,1024]{1,0:T(2,128)S(1)} %copy-done.11, f32[16,1024]{1,0:T(8,128)S(1)} %copy-done.4, f32[2,16,1024]{2,1,0:T(8,128)S(1)} %copy-done.5, f32[2,16,1024]{2,1,0:T(8,128)S(1)} %copy-done.6, ...), custom_call_target="tpu_custom_call" | custom-call | flops 1900000000 | tf_op jit(solution)/shard_map/carry_over/pallas_call | solution.py:691
  181.6 36.8 %scan_back.2 = (f32[256,1024]{1,0:T(8,128)}, f32[256,1024]{1,0:T(8,128)}, f32[256,128]{1,0:T(8,128)}, f32[16,1024]{1,0:T(8,128)}, f32[256,1024]{1,0:T(8,128)}, /...) custom-call(f32[256,1024]{1,0:T(8,128)} %convolution_add_fusion.2.refs_0_, ...), custom_call_target="tpu_custom_call" | custom-call | flops 2600000000 | tf_op jit(solution)/shard_map/scan_back/pallas_call | solution.py:150
  224.8 7.8 %ch_sum.6 = f32[256,160]{1,0:T(8,128)S(1)} custom-call(f32[256,160]{1,0:T(8,128)S(1)} %pad_maximum_fusion.8.refs_0_, bf16[1024,1024]{1,0:T(8,128)(2,1)S(1)} %copy-done), custom_call_target="tpu_custom_call" | custom-call | flops 1000000000 | tf_op jit(solution)/shard_map/ch_sum/pallas_call | solution.py:434
  259.9 6.6 %fusion.40.refs_0_ = bf16[256,2048]{1,0:T(8,128)(2,1)S(1)} fusion(bf16[2048,2,1024]{2,1,0:T(2,128)(2,1)} %copy-done.13, bf16[256,1,1024]{2,0,1:T(8,128)(2,1)} %fusion.88, bf16[256,1,1024]{2,0,1:T(8,128)(2,1)} %bitcast.295), kind=kOutput, calls=%fused_computation.38 | convolution fusion | flops 2148532224 | bytes 10485760 | tf_op jit(solution)/shard_map/dot_general | solution.py:1260
  266.6 16.8 %ch_reduce.3 = f32[256,2048]{1,0:T(8,128)S(1)} custom-call(bf16[256,2048]{1,0:T(8,128)(2,1)S(1)} %fusion.40.refs_0_), custom_call_target="tpu_custom_call" | custom-call | flops 1800000000 | tf_op jit(solution)/shard_map/ch_reduce/pallas_call | solution.py:615
  288.2 5.8 %multiply_reduce_fusion.9 = (f32[1024]{0:T(1024)S(1)}, f32[256,1024]{1,0:T(8,128)}, bf16[256,1024]{1,0:T(8,128)(2,1)}, f32[256,1024]{1,0:T(8,128)}) fusion(f32[2,128,1024]{2,1,0:T(8,128)S(1)} %copy-done.40, f32[256,2,1024]{2,0,1:T(8,128)S(1)} %copy-done.44, f32[256,1024]{1,0:T(8,128)S(1)} %copy-done.49, f32[1024]{0:T(1024)S(1)} %bitcast.352, ...), kind=kOutput, calls=%fused_computation.125 | convolution fusion | flops 1080032256 | bytes 11018240 | tf_op jit(solution)/shard_map/dot_general | solution.py:1100
  294.0 7.9 %scan_back_local.3.refs_2_ = f32[2,16,1024]{2,1,0:T(8,128)} custom-call(f32[256,1024]{1,0:T(8,128)} %convolution_add_fusion.3.refs_0_, f32[256,1024]{1,0:T(8,128)} %get-tuple-element.118.refs_1_.refs_2_, f32[256,32]{1,0:T(8,128)} %slice.287.refs_2_.refs_3_, f32[256,1]{1,0:T(8,128)} %copy.38.refs_3_.refs_4_, f32[16,1024]{1,0:T(8,128)} %get-tuple-element.156.refs_4_.refs_1_.refs_5_), custom_call_target="tpu_custom_call" | custom-call | flops 800000000 | tf_op jit(solution)/shard_map/scan_back_local/pallas_call | solution.py:253
  307.5 21.3 %carry_over.5 = (f32[2,16,1024]{2,1,0:T(8,128)S(1)}, f32[1024,256]{1,0:T(8,128)S(1)}) custom-call(f32[2,1024]{1,0:T(2,128)S(1)} %copy-done.10, f32[16,1024]{1,0:T(8,128)S(1)} %copy-done.3, f32[2,16,1024]{2,1,0:T(8,128)S(1)} %copy-done.16, bf16[2,1024,256]{2,1,0:T(8,128)(2,1)S(1)} %pad_maximum_fusion.5.refs_3_), custom_call_target="tpu_custom_call" | custom-call | flops 1900000000 | tf_op jit(solution)/shard_map/carry_over/pallas_call | solution.py:691
  329.6 6.2 %fusion.45 = bf16[512,1024]{1,0:T(8,128)(2,1)} fusion(bf16[1024,512]{1,0:T(8,128)(2,1)} %get-tuple-element.59, bf16[1024,1024]{1,0:T(8,128)(2,1)S(1)} %copy-done.1, bf16[1024,1024]{1,0:T(8,128)(2,1)} %all-gather.7.cloned.1.call-done.refs_6_, bf16[1024,1024]{1,0:T(8,128)(2,1)} %all-gather.11.cloned.1.call-done, f32[]{:T(128)} %bitcast.44), kind=kOutput, calls=%fused_computation.56 | convolution fusion | flops 1088946176 | bytes 8388612 | tf_op jit(solution)/shard_map/dot_general | solution.py:1100
  340.0 37.0 %scan_back.3 = (f32[256,1024]{1,0:T(8,128)}, f32[256,1024]{1,0:T(8,128)}, f32[256,128]{1,0:T(8,128)}, f32[16,1024]{1,0:T(8,128)}, bf16[1024,512]{1,0:T(8,128)(2,...) custom-call(f32[256,1024]{1,0:T(8,128)} %convolution_add_fusion.3.refs_0_, f32[256,1024]{1,0:T(8,128)} %bitcast_multiply_fusion.5.refs_1_, ...), custom_call_target="tpu_custom_call" | custom-call | flops 2300000000 | tf_op jit(solution)/shard_map/scan_back/pallas_call | solution.py:150
  379.5 6.8 %ch_sum.7 = f32[256,160]{1,0:T(8,128)S(1)} custom-call(f32[256,160]{1,0:T(8,128)S(1)} %pad_maximum_fusion.9.refs_0_), custom_call_target="tpu_custom_call" | custom-call | flops 1000000000 | tf_op jit(solution)/shard_map/ch_sum/pallas_call | solution.py:434
  403.5 15.1 %all-gather.15.cloned.1.call-done = bf16[1024,1024]{1,0:T(8,128)(2,1)} async-done(((bf16[256,1024]{1,0:T(8,128)(2,1)}), bf16[1024,1024]{1,0:T(8,128)(2,1)}) %all-gather.15.cloned.1.call-update) | async-done | bytes 2097168 | tf_op jit(solution)/shard_map/all_gather | solution.py:1108
  426.0 6.6 %fusion.137 = (bf16[256,2048]{1,0:T(8,128)(2,1)S(1)}, f32[256]{0:T(256)S(1)}) fusion(bf16[2,128,2048]{2,1,0:T(8,128)(2,1)S(1)} %copy-done.23, f32[2048]{0:T(1024)S(1)} %bitcast.322, bf16[2048,2,1024]{2,1,0:T(2,128)(2,1)} %copy-done.12, bf16[256,1,1024]{2,0,1:T(8,128)(2,1)S(1)} %bitcast.308, bf16[256,1,1024]{2,0,1:T(8,128)(2,1)S(1)} %bitcast.309), kind=kOutput, calls=%fused_computation.264 | convolution fusion | flops 2150629120 | bytes 11543552 | tf_op jit(solution)/shard_map/dot_general | solution.py:1260
  435.6 91.6 %closing.1 = (f32[256,640]{1,0:T(8,128)}, f32[256,512]{1,0:T(8,128)}, bf16[640,1024]{1,0:T(8,128)(2,1)}, f32[256,1024]{1,0:T(8,128)}, f32[16,512]{1,0:T(8,128)},...) custom-call(bf16[256,2560]{1,0:T(8,128)(2,1)} %bitcast.296, bf16[256,2048]{1,0:T(8,128)(2,1)} %fusion.34.b_ref, ...), custom_call_target="tpu_custom_call" | custom-call | flops 7000000000 | tf_op jit(solution)/shard_map/closing/pallas_call | solution.py:1041
  533.0 5.3 copy.52
  (321 shorter events, 154.3 us)
Async XLA Ops:
  7.2 68.6 %all-gather.7.cloned.1.call-start = ((), (), s32[]{:S(2)}) async-start(), calls=%async_computation | async-start | bytes 2621440 | tf_op jit(solution)/shard_map/all_gather | solution.py:1108
  8.0 21.7 %collective-permute-start.1 = (f32[2,3]{1,0:T(2,128)S(1)}, f32[2,3]{1,0:T(2,128)S(1)}, u32[]{:S(2)}, u32[]{:S(2)}) collective-permute-start(f32[2,3]{1,0:T(2,128)S(1)} %slice.274), channel_id=1, source_target_pairs={{0,4},{4,8},{8,12},{12,16},{16,20},{20,24},{24,28},{1,5},{5,9},{9,... | collective-permute-start | bytes 80 | tf_op jit(solution)/shard_map/ppermute | solution.py:1076
  16.5 206.8 %all-gather.9.cloned.1.call-start = ((), (), s32[]{:S(2)}) async-start(), calls=%async_computation.1 | async-start | bytes 2621440 | tf_op jit(solution)/shard_map/all_gather | solution.py:1108
  24.6 8.8 %copy-start.31 = (f32[256,1,1024]{2,0,1:T(8,128)}, f32[256,1,1024]{2,0,1:T(8,128)S(1)}, u32[]{:S(2)}) copy-start(f32[256,1,1024]{2,0,1:T(8,128)S(1)} %slice.342) | copy-start | bytes 3145732
  24.7 7.5 %collective-permute-start = (f32[2,3,1024]{2,1,0:T(4,128)S(1)}, f32[2,3,1024]{2,1,0:T(4,128)S(1)}, u32[]{:S(2)}, u32[]{:S(2)}) collective-permute-start(f32[2,3,1024]{2,1,0:T(4,128)S(1)} %slice.343), channel_id=1, source_target_pairs={{0,4},{4,8},{8,12},{12,16},{16,20},{20,24},{24,28},{1,5},{5,9},{9,... | collective-permute-start | bytes 73736 | tf_op jit(solution)/shard_map/ppermute | solution.py:1076
  29.0 258.3 %copy-start.76 = (f32[1,1024]{1,0:T(1,128)}, f32[1,1024]{1,0:T(1,128)S(1)}, u32[]{:S(2)}) copy-start(f32[1,1024]{1,0:T(1,128)S(1)} %get-tuple-element.168.refs_6_) | copy-start | bytes 12292
  33.1 53.7 %copy-start.39 = (f32[2,128,1024]{2,1,0:T(8,128)}, f32[2,128,1024]{2,1,0:T(8,128)S(1)}, u32[]{:S(2)}) copy-start(f32[2,128,1024]{2,1,0:T(8,128)S(1)} %get-tuple-element.128) | copy-start | bytes 3145732
  42.2 9.1 %copy-start.2 = (f32[16,1024]{1,0:T(8,128)S(1)}, f32[16,1024]{1,0:T(8,128)}, u32[]{:S(2)}) copy-start(f32[16,1024]{1,0:T(8,128)} %get-tuple-element.156.refs_4_.refs_1_.refs_5_) | copy-start | bytes 196612
  92.6 16.9 %copy-start.22 = (bf16[2,128,2048]{2,1,0:T(8,128)(2,1)S(1)}, bf16[2,128,2048]{2,1,0:T(8,128)(2,1)}, u32[]{:S(2)}) copy-start(bf16[2,128,2048]{2,1,0:T(8,128)(2,1)} %param.13) | copy-start | bytes 3145732
  92.6 19.2 %slice-start = ((s8[8388608]{0:T(1024)(128)(4,1)}), s8[4194304]{0:T(1024)(128)(4,1)S(1)}, s32[]{:S(2)}) async-start(s8[8388608]{0:T(1024)(128)(4,1)} %bitcast.283), calls=%async_computation.6 | async-start | bytes 8388608
  111.6 173.6 %copy-start.18 = (f32[256,2048]{1,0:T(8,128)}, f32[256,2048]{1,0:T(8,128)S(1)}, u32[]{:S(2)}) copy-start(f32[256,2048]{1,0:T(8,128)S(1)} %get-tuple-element.126) | copy-start | bytes 6291460
  117.3 9.1 %copy-start.66 = (bf16[2,1024,160]{1,2,0:T(8,128)(2,1)S(1)}, bf16[2,1024,160]{1,2,0:T(8,128)(2,1)}, u32[]{:S(2)}) copy-start(bf16[2,1024,160]{1,2,0:T(8,128)(2,1)} %param.20) | copy-start | bytes 1966084
  117.3 184.6 %all-gather.11.cloned.1.call-start = ((), (), s32[]{:S(2)}) async-start(), calls=%async_computation.2 | async-start | bytes 2621440 | tf_op jit(solution)/shard_map/all_gather | solution.py:1108
  118.8 6.7 %collective-permute-start.2 = (f32[2,3,1024]{2,1,0:T(4,128)S(1)}, f32[2,3,1024]{2,1,0:T(4,128)S(1)}, u32[]{:S(2)}, u32[]{:S(2)}) collective-permute-start(f32[2,3,1024]{2,1,0:T(4,128)S(1)} %slice.355), channel_id=1, source_target_pairs={{0,4},{4,8},{8,12},{12,16},{16,20},{20,24},{24,28},{1,5},{5,9},{9,... | collective-permute-start | bytes 73736 | tf_op jit(solution)/shard_map/ppermute | solution.py:1076
  126.4 9.5 %copy-start.41 = (f32[2,128,1024]{2,1,0:T(8,128)}, f32[2,128,1024]{2,1,0:T(8,128)S(1)}, u32[]{:S(2)}) copy-start(f32[2,128,1024]{2,1,0:T(8,128)S(1)} %get-tuple-element.124) | copy-start | bytes 3145732
  126.8 9.1 %copy-start.28 = (f32[256,2,1024]{2,0,1:T(8,128)S(1)}, f32[256,2,1024]{2,0,1:T(8,128)}, u32[]{:S(2)}) copy-start(f32[256,2,1024]{2,0,1:T(8,128)} %copy-done.27) | copy-start | bytes 6291460
  126.8 9.1 %copy-start.46 = (f32[256,1024]{1,0:T(8,128)S(1)}, f32[256,1024]{1,0:T(8,128)}, u32[]{:S(2)}) copy-start(f32[256,1024]{1,0:T(8,128)} %get-tuple-element.183) | copy-start | bytes 3145732
  181.6 36.8 %copy-start.77 = (f32[1,1024]{1,0:T(1,128)S(1)}, f32[1,1024]{1,0:T(1,128)}, u32[]{:S(2)}) copy-start(f32[1,1024]{1,0:T(1,128)} %get-tuple-element.167.refs_6_) | copy-start | bytes 12292
  221.6 114.2 %all-gather.13.cloned.1.call-start = ((), (), s32[]{:S(2)}) async-start(), calls=%async_computation.3 | async-start | bytes 2621440 | tf_op jit(solution)/shard_map/all_gather | solution.py:1108
  233.9 6.0 %collective-permute-start.3 = (f32[2,3,1024]{2,1,0:T(4,128)S(1)}, f32[2,3,1024]{2,1,0:T(4,128)S(1)}, u32[]{:S(2)}, u32[]{:S(2)}) collective-permute-start(f32[2,3,1024]{2,1,0:T(4,128)S(1)} %pad_add_fusion.3), channel_id=1, source_target_pairs={{4,0},{8,4},{12,8},{16,12},{20,16},{24,20},{28,24},{5,1},{9,5},{13... | collective-permute-start | bytes 73736 | tf_op jit(solution)/shard_map/ppermute | solution.py:1076
  240.8 155.5 %all-gather.17.cloned.1.call-start = ((), (), s32[]{:S(2)}) async-start(), calls=%async_computation.5 | async-start | bytes 2621440 | tf_op jit(solution)/shard_map/all_gather | solution.py:1108
  244.6 173.9 %all-gather.15.cloned.1.call-start = ((), (), s32[]{:S(2)}) async-start(), calls=%async_computation.4 | async-start | bytes 2621440 | tf_op jit(solution)/shard_map/all_gather | solution.py:1108
  340.0 37.0 %copy-start.54 = (bf16[2,128,1024]{2,1,0:T(8,128)(2,1)S(1)}, bf16[2,128,1024]{2,1,0:T(8,128)(2,1)}, u32[]{:S(2)}) copy-start(bf16[2,128,1024]{2,1,0:T(8,128)(2,1)} %param.21) | copy-start | bytes 1572868
  388.9 35.5 %collective-permute-start.4 = (f32[2,3,1024]{2,1,0:T(4,128)S(1)}, f32[2,3,1024]{2,1,0:T(4,128)S(1)}, u32[]{:S(2)}, u32[]{:S(2)}) collective-permute-start(f32[2,3,1024]{2,1,0:T(4,128)S(1)} %pad_add_fusion.2), channel_id=1, source_target_pairs={{4,0},{8,4},{12,8},{16,12},{20,16},{24,20},{28,24},{5,1},{9,5},{13... | collective-permute-start | bytes 73736 | tf_op jit(solution)/shard_map/ppermute | solution.py:1076
  (75 other events, 272.5 us)
Sparse Core Ops, SparseCore 0:
  16.6 50.1 all-gather.6
  117.4 52.4 all-gather.8
  221.7 46.2 all-gather.10
  269.5 43.9 all-gather.12
  314.8 55.6 all-gather.16
  371.9 46.6 all-gather.14

commit v6 on v5

--- a/solution.py
+++ b/solution.py
@@ -692,7 +692,7 @@
         functools.partial(carry_kernel, n, int(fwd), int(rev), len(ps), places, layer),
         out_shape=[jax.ShapeDtypeStruct(ends[0].shape, f32)] * k + [PartSum.result(p, *places) for p in ps]
         + [jax.ShapeDtypeStruct(w.shape[1:], w.dtype) for w in extra],
-        in_specs=[VM] * (k + 2 + len(ps)) + [ANY] * len(extra), out_specs=[VM] * (k + len(ps)) + [ANY] * len(extra),
+        in_specs=[VM] * (k + 2 + len(ps)) + [ANY] * len(extra), out_specs=[VM] * (k + len(ps)) + [pl.BlockSpec(memory_space=pltpu.HBM)] * len(extra),
         scratch_shapes=[pltpu.VMEM((k,) + ends[0].shape, bf16), pltpu.VMEM((k, n - 1) + ends[0].shape, bf16), pltpu.VMEM((k, n - 1) + tot.shape, f32),
                         sem((k, n - 1)), sem((k, n - 1)), sem((k, n - 1)), sem((k, n - 1))]
         + [spec for p in ps for spec in PartSum.specs(p, *places)]
@@ -1130,9 +1130,7 @@
     share = width // nch
     share_start = lax.axis_index("ch") * share
     seg_own = segments.astype(f32)
-    seg_edge = passed_along(seg_own[:, -(KERN - 1) :], "seq", 1)
-    seg_ext = jnp.concatenate([seg_edge, seg_own], axis=1)
-    keep = (seg_ext[:, KERN - 2 : -1] == seg_own).astype(f32).reshape(-1, 1)
+    seg_ext = None
     hidden = hidden_in.astype(f32).reshape(rows, width)
     grad_rows = cotangent.astype(f32).reshape(rows, width)
     ids = iter(range(100))
@@ -1154,7 +1152,15 @@
         both = lax.dot_general(normed, w_in, (((1,), (0,)), ((), ())), preferred_element_type=f32)
         values, gate_pre = both[:, 0], both[:, 1]
         values3 = values.reshape(seqs, length, channels)
-        edge = passed_along(values3[:, -(KERN - 1) :], "seq", 1)
+        edge = values3[:, -(KERN - 1) :]
+        if seg_ext is None:
+            ids_edge = jnp.broadcast_to(seg_own[:, -(KERN - 1) :, None], (seqs, KERN - 1, LANES))
+            edge = passed_along(jnp.concatenate([edge, ids_edge], axis=2), "seq", 1)
+            seg_ext = jnp.concatenate([edge[:, :, channels], seg_own], axis=1)
+            keep = (seg_ext[:, KERN - 2 : -1] == seg_own).astype(f32).reshape(-1, 1)
+            edge = edge[:, :, :channels]
+        else:
+            edge = passed_along(edge, "seq", 1)
         extended = jnp.concatenate([edge, values3], axis=1)
         conv_out, conv_pull = jax.vjp(
             functools.partial(conv_local, seg_ext=seg_ext), extended, conv_weight[layer], conv_bias[layer]

time: 562 us -> 558 us (level)
    ppermute x5 -> x4, starting transfers between devices: 15.7 us -> 12.1 us  [passed_along(): return lax.ppermute(block, axis, route)]
    unnamed x179 -> x180, local copies, waits for them, and re-layouts: 31.8 us -> 32.4 us
  transfers between devices with their start and end apart: 11 -> 10, of which waited for: 4 -> 4; matrix products, arithmetic and copies ran while one was open for 18% -> 17% of each run, Pallas kernels for 38% -> 39%
where the time goes in v6:
time: 558 us; the launch traced here: 551 us
  Pallas kernels  333 us (60%)
  matrix products  71.6 us (13%)
  local copies, waits for them, and re-layouts  48.4 us (9%)
  other arithmetic  46.5 us (8%)
  waiting for transfers between devices  22.6 us (4%)
  between operations  16.6 us (3%)
  starting transfers between devices  12.4 us (2%)
    pallas_call x5, Pallas kernels, play_call(): pl.pallas_call(after(played(kernel, counts, kinds, places), len(arrays),...  102 us
    pallas_call x1, Pallas kernels, closing(): pl.pallas_call(functools.partial(closing_kernel, n, nseq, zs, ys, parts,...  91.5 us
    pallas_call x3, Pallas kernels, carry_over(): pl.pallas_call(functools.partial(carry_kernel, n, int(fwd), int(rev), len...  61.5 us
    dot_general x23, matrix products, dot(): lax.dot_general(a, b, ((contract[:1], contract[1:]), ((), ())), preferred...  52.5 us
    pallas_call x2, Pallas kernels, ch_reduce(): pl.pallas_call(functools.partial(reduce_kernel, n, parts, gather), out_sh...  33.8 us
    unnamed x180, local copies, waits for them, and re-layouts  32.4 us
    pallas_call x4, Pallas kernels, ch_sum(): pl.pallas_call(after(functools.partial(ch_sum_kernel, n), 1, pins), out_s...  28.3 us
    pallas_call x2, Pallas kernels, scan_back_local(): pl.pallas_call(after(functools.partial(back_local_kernel, seqs), 5, pins)...  15.7 us
  transfers between devices with their start and end apart: 10, of which 4 were waited for; matrix products, arithmetic and copies ran while one was open for 17% of the time, Pallas kernels for 39%

profile of v6, /device:TPU:10, one launch (start us, length us, event | category | flops | bytes accessed | tf_op | source)
XLA Modules:
  0.0 550.8 jit_solution(15861433814676991354)
XLA Ops:
  7.2 5.0 fusion.143
  30.2 6.8 %ch_sum.4 = f32[256,160]{1,0:T(8,128)S(1)} custom-call(f32[256,160]{1,0:T(8,128)S(1)} %fusion.93.refs_0_), custom_call_target="tpu_custom_call" | custom-call | flops 1000000000 | tf_op jit(solution)/shard_map/ch_sum/pallas_call | solution.py:434
  40.9 7.9 %scan_local.2 = (f32[2,16,1024]{2,1,0:T(8,128)}, f32[2,1024]{1,0:T(2,128)}) custom-call(f32[256,1024]{1,0:T(8,128)} %convolution_add_fusion.3.refs_0_, f32[256,1024]{1,0:T(8,128)} %bitcast_multiply_fusion.5.refs_1_, f32[256,32]{1,0:T(8,128)} %slice.295.refs_2_.refs_3_, f32[256,1]{1,0:T(8,128)} %copy.64.refs_3_.refs_4_, ...), custom_call_target="tpu_custom_call" | custom-call | flops 800000000 | tf_op jit(solution)/shard_map/scan_local/pallas_call | solution.py:150
  50.4 18.1 %carry_over.3 = (f32[2,16,1024]{2,1,0:T(8,128)S(1)}, bf16[2048,2,1024]{2,1,0:T(2,128)(2,1)S(1)}) custom-call(f32[2,1024]{1,0:T(2,128)S(1)} %copy-done.9, f32[16,1024]{1,0:T(8,128)S(1)} %copy-done.2, f32[2,16,1024]{2,1,0:T(8,128)S(1)} %copy-done.7, bf16[2,2048,2,1024]{3,2,1,0:T(2,128)(2,1)} %refs_4_.1), custom_call_target="tpu_custom_call" | custom-call | flops 1900000000 | tf_op jit(solution)/shard_map/carry_over/pallas_call | solution.py:691
  72.6 11.0 %scan_forward.1 = f32[256,1024]{1,0:T(8,128)} custom-call(f32[256,1024]{1,0:T(8,128)} %convolution_add_fusion.3.refs_0_, f32[256,1024]{1,0:T(8,128)} %bitcast_multiply_fusion.5.refs_1_, f32[256,32]{1,0:T(8,128)} %slice.295.refs_2_.refs_3_, f32[256,1]{1,0:T(8,128)} %copy.64.refs_3_.refs_4_, f32[16,1024]{1,0:T(8,128)} %get-tuple-element.168.refs_4_.refs_1_.refs_5_, ...), custom_call_target="tpu_custom_call" | custom-call | flops 1100000000 | tf_op jit(solution)/shard_map/scan_forward/pallas_call | solution.py:150
  89.4 16.9 %ch_reduce.2 = f32[256,2048]{1,0:T(8,128)S(1)} custom-call(bf16[256,2048]{1,0:T(8,128)(2,1)S(1)} %fusion.37.refs_0_), custom_call_target="tpu_custom_call" | custom-call | flops 1800000000 | tf_op jit(solution)/shard_map/ch_reduce/pallas_call | solution.py:615
  123.6 7.1 %ch_sum.5 = f32[256,160]{1,0:T(8,128)S(1)} custom-call(f32[256,160]{1,0:T(8,128)S(1)} %fusion.90.refs_0_), custom_call_target="tpu_custom_call" | custom-call | flops 1000000000 | tf_op jit(solution)/shard_map/ch_sum/pallas_call | solution.py:434
  134.9 7.9 %scan_local.3 = (f32[2,16,1024]{2,1,0:T(8,128)}, f32[2,1024]{1,0:T(2,128)}) custom-call(f32[256,1024]{1,0:T(8,128)} %convolution_add_fusion.2.refs_0_, f32[256,1024]{1,0:T(8,128)} %get-tuple-element.163.refs_1_, f32[256,32]{1,0:T(8,128)} %slice.317.refs_2_.refs_3_, f32[256,1]{1,0:T(8,128)} %copy.64.refs_3_.refs_4_, ...), custom_call_target="tpu_custom_call" | custom-call | flops 800000000 | tf_op jit(solution)/shard_map/scan_local/pallas_call | solution.py:150
  142.8 7.8 %scan_back_local.2.refs_3_ = f32[2,16,1024]{2,1,0:T(8,128)} custom-call(f32[256,1024]{1,0:T(8,128)} %convolution_add_fusion.2.refs_0_, f32[256,1024]{1,0:T(8,128)} %get-tuple-element.128.refs_1_.refs_2_, f32[256,32]{1,0:T(8,128)} %slice.317.refs_2_.refs_3_, f32[256,1]{1,0:T(8,128)} %copy.64.refs_3_.refs_4_, f32[16,1024]{1,0:T(8,128)} %get-tuple-element.167.refs_4_.refs_1_.refs_5_), custom_call_target="tpu_custom_call" | custom-call | flops 800000000 | tf_op jit(solution)/shard_map/scan_back_local/pallas_call | solution.py:253
  151.4 22.2 %carry_over.4 = (f32[2,16,1024]{2,1,0:T(8,128)S(1)}, f32[2,16,1024]{2,1,0:T(8,128)S(1)}, bf16[2048,2,1024]{2,1,0:T(2,128)(2,1)S(1)}) custom-call(f32[2,1024]{1,0:T(2,128)S(1)} %copy-done.11, f32[16,1024]{1,0:T(8,128)S(1)} %copy-done.4, f32[2,16,1024]{2,1,0:T(8,128)S(1)} %copy-done.5, f32[2,16,1024]{2,1,0:T(8,128)S(1)} %copy-done.6, ...), custom_call_target="tpu_custom_call" | custom-call | flops 1900000000 | tf_op jit(solution)/shard_map/carry_over/pallas_call | solution.py:691
  178.3 36.9 %scan_back.2 = (f32[256,1024]{1,0:T(8,128)}, f32[256,1024]{1,0:T(8,128)}, f32[256,128]{1,0:T(8,128)}, f32[16,1024]{1,0:T(8,128)}, f32[256,1024]{1,0:T(8,128)}, /...) custom-call(f32[256,1024]{1,0:T(8,128)} %convolution_add_fusion.2.refs_0_, ...), custom_call_target="tpu_custom_call" | custom-call | flops 2600000000 | tf_op jit(solution)/shard_map/scan_back/pallas_call | solution.py:150
  221.6 7.6 %ch_sum.6 = f32[256,160]{1,0:T(8,128)S(1)} custom-call(f32[256,160]{1,0:T(8,128)S(1)} %pad_maximum_fusion.8.refs_0_, bf16[1024,1024]{1,0:T(8,128)(2,1)S(1)} %copy-done), custom_call_target="tpu_custom_call" | custom-call | flops 1000000000 | tf_op jit(solution)/shard_map/ch_sum/pallas_call | solution.py:434
  256.7 6.6 %fusion.40.refs_0_ = bf16[256,2048]{1,0:T(8,128)(2,1)S(1)} fusion(bf16[2048,2,1024]{2,1,0:T(2,128)(2,1)} %copy-done.13, bf16[256,1,1024]{2,0,1:T(8,128)(2,1)} %fusion.88, bf16[256,1,1024]{2,0,1:T(8,128)(2,1)} %bitcast.296), kind=kOutput, calls=%fused_computation.38 | convolution fusion | flops 2148532224 | bytes 10485760 | tf_op jit(solution)/shard_map/dot_general | solution.py:1266
  263.3 16.9 %ch_reduce.3 = f32[256,2048]{1,0:T(8,128)S(1)} custom-call(bf16[256,2048]{1,0:T(8,128)(2,1)S(1)} %fusion.40.refs_0_), custom_call_target="tpu_custom_call" | custom-call | flops 1800000000 | tf_op jit(solution)/shard_map/ch_reduce/pallas_call | solution.py:615
  285.1 5.8 %multiply_reduce_fusion.9 = (f32[1024]{0:T(1024)S(1)}, f32[256,1024]{1,0:T(8,128)}, bf16[256,1024]{1,0:T(8,128)(2,1)}, f32[256,1024]{1,0:T(8,128)}) fusion(f32[2,128,1024]{2,1,0:T(8,128)S(1)} %copy-done.40, f32[256,2,1024]{2,0,1:T(8,128)S(1)} %copy-done.44, f32[256,1024]{1,0:T(8,128)S(1)} %copy-done.49, f32[1024]{0:T(1024)S(1)} %bitcast.353, ...), kind=kOutput, calls=%fused_computation.125 | convolution fusion | flops 1080032256 | bytes 11018240 | tf_op jit(solution)/shard_map/dot_general | solution.py:1100
  290.9 7.9 %scan_back_local.3.refs_2_ = f32[2,16,1024]{2,1,0:T(8,128)} custom-call(f32[256,1024]{1,0:T(8,128)} %convolution_add_fusion.3.refs_0_, f32[256,1024]{1,0:T(8,128)} %get-tuple-element.130.refs_1_.refs_2_, f32[256,32]{1,0:T(8,128)} %slice.295.refs_2_.refs_3_, f32[256,1]{1,0:T(8,128)} %copy.64.refs_3_.refs_4_, f32[16,1024]{1,0:T(8,128)} %get-tuple-element.168.refs_4_.refs_1_.refs_5_), custom_call_target="tpu_custom_call" | custom-call | flops 800000000 | tf_op jit(solution)/shard_map/scan_back_local/pallas_call | solution.py:253
  304.4 21.2 %carry_over.5 = (f32[2,16,1024]{2,1,0:T(8,128)S(1)}, f32[1024,256]{1,0:T(8,128)S(1)}) custom-call(f32[2,1024]{1,0:T(2,128)S(1)} %copy-done.10, f32[16,1024]{1,0:T(8,128)S(1)} %copy-done.3, f32[2,16,1024]{2,1,0:T(8,128)S(1)} %copy-done.16, bf16[2,1024,256]{2,1,0:T(8,128)(2,1)S(1)} %pad_maximum_fusion.5.refs_3_), custom_call_target="tpu_custom_call" | custom-call | flops 1900000000 | tf_op jit(solution)/shard_map/carry_over/pallas_call | solution.py:691
  326.3 6.2 %fusion.45 = bf16[512,1024]{1,0:T(8,128)(2,1)} fusion(bf16[1024,512]{1,0:T(8,128)(2,1)} %get-tuple-element.59, bf16[1024,1024]{1,0:T(8,128)(2,1)S(1)} %copy-done.1, bf16[1024,1024]{1,0:T(8,128)(2,1)} %all-gather.7.cloned.1.call-done.refs_6_, bf16[1024,1024]{1,0:T(8,128)(2,1)} %all-gather.11.cloned.1.call-done, f32[]{:T(128)} %bitcast.45), kind=kOutput, calls=%fused_computation.56 | convolution fusion | flops 1088946176 | bytes 8388612 | tf_op jit(solution)/shard_map/dot_general | solution.py:1100
  336.7 38.1 %scan_back.3 = (f32[256,1024]{1,0:T(8,128)}, f32[256,1024]{1,0:T(8,128)}, f32[256,128]{1,0:T(8,128)}, f32[16,1024]{1,0:T(8,128)}, bf16[1024,512]{1,0:T(8,128)(2,...) custom-call(f32[256,1024]{1,0:T(8,128)} %convolution_add_fusion.3.refs_0_, f32[256,1024]{1,0:T(8,128)} %bitcast_multiply_fusion.5.refs_1_, ...), custom_call_target="tpu_custom_call" | custom-call | flops 2300000000 | tf_op jit(solution)/shard_map/scan_back/pallas_call | solution.py:150
  377.4 6.8 %ch_sum.7 = f32[256,160]{1,0:T(8,128)S(1)} custom-call(f32[256,160]{1,0:T(8,128)S(1)} %pad_maximum_fusion.9.refs_0_), custom_call_target="tpu_custom_call" | custom-call | flops 1000000000 | tf_op jit(solution)/shard_map/ch_sum/pallas_call | solution.py:434
  401.4 13.9 %all-gather.15.cloned.1.call-done = bf16[1024,1024]{1,0:T(8,128)(2,1)} async-done(((bf16[256,1024]{1,0:T(8,128)(2,1)}), bf16[1024,1024]{1,0:T(8,128)(2,1)}) %all-gather.15.cloned.1.call-update) | async-done | bytes 2097168 | tf_op jit(solution)/shard_map/all_gather | solution.py:1108
  422.6 6.7 %fusion.137 = (bf16[256,2048]{1,0:T(8,128)(2,1)S(1)}, f32[256]{0:T(256)S(1)}) fusion(bf16[2,128,2048]{2,1,0:T(8,128)(2,1)S(1)} %copy-done.23, f32[2048]{0:T(1024)S(1)} %bitcast.323, bf16[2048,2,1024]{2,1,0:T(2,128)(2,1)} %copy-done.12, bf16[256,1,1024]{2,0,1:T(8,128)(2,1)S(1)} %bitcast.309, bf16[256,1,1024]{2,0,1:T(8,128)(2,1)S(1)} %bitcast.310), kind=kOutput, calls=%fused_computation.265 | convolution fusion | flops 2150629120 | bytes 11543552 | tf_op jit(solution)/shard_map/dot_general | solution.py:1266
  432.2 91.5 %closing.1 = (f32[256,640]{1,0:T(8,128)}, f32[256,512]{1,0:T(8,128)}, bf16[640,1024]{1,0:T(8,128)(2,1)}, f32[256,1024]{1,0:T(8,128)}, f32[16,512]{1,0:T(8,128)},...) custom-call(bf16[256,2560]{1,0:T(8,128)(2,1)} %bitcast.297, bf16[256,2048]{1,0:T(8,128)(2,1)} %fusion.34.b_ref, ...), custom_call_target="tpu_custom_call" | custom-call | flops 7000000000 | tf_op jit(solution)/shard_map/closing/pallas_call | solution.py:1041
  529.6 5.3 copy.78
  (327 shorter events, 152.1 us)
Async XLA Ops:
  7.2 65.4 %all-gather.7.cloned.1.call-start = ((), (), s32[]{:S(2)}) async-start(), calls=%async_computation | async-start | bytes 2621440 | tf_op jit(solution)/shard_map/all_gather | solution.py:1108
  12.3 207.7 %all-gather.9.cloned.1.call-start = ((), (), s32[]{:S(2)}) async-start(), calls=%async_computation.1 | async-start | bytes 2621440 | tf_op jit(solution)/shard_map/all_gather | solution.py:1108
  21.0 8.8 %copy-start.31 = (f32[256,1,1024]{2,0,1:T(8,128)}, f32[256,1,1024]{2,0,1:T(8,128)S(1)}, u32[]{:S(2)}) copy-start(f32[256,1,1024]{2,0,1:T(8,128)S(1)} %slice.350) | copy-start | bytes 3145732
  21.0 8.8 %copy-start.65 = (bf16[2,1024,160]{1,2,0:T(8,128)(2,1)S(1)}, bf16[2,1024,160]{1,2,0:T(8,128)(2,1)}, u32[]{:S(2)}) copy-start(bf16[2,1024,160]{1,2,0:T(8,128)(2,1)} %param.20) | copy-start | bytes 1966084
  21.3 7.3 %collective-permute-start = (f32[2,3,1152]{2,0,1:T(2,128)S(1)}, f32[2,3,1152]{2,0,1:T(2,128)S(1)}, u32[]{:S(2)}, u32[]{:S(2)}) collective-permute-start(f32[2,3,1152]{2,0,1:T(2,128)S(1)} %pad_maximum_fusion.11), channel_id=1, source_target_pairs={{0,4},{4,8},{8,12},{12,16},{16,20},{20,24},{24,28},{1,5},{5,9},{9,... | collective-permute-start | bytes 82952 | tf_op jit(solution)/shard_map/ppermute | solution.py:1076
  25.5 258.6 %copy-start.76 = (f32[1,1024]{1,0:T(1,128)}, f32[1,1024]{1,0:T(1,128)S(1)}, u32[]{:S(2)}) copy-start(f32[1,1024]{1,0:T(1,128)S(1)} %get-tuple-element.180.refs_6_) | copy-start | bytes 12292
  29.8 53.8 %copy-start.39 = (f32[2,128,1024]{2,1,0:T(8,128)}, f32[2,128,1024]{2,1,0:T(8,128)S(1)}, u32[]{:S(2)}) copy-start(f32[2,128,1024]{2,1,0:T(8,128)S(1)} %get-tuple-element.140) | copy-start | bytes 3145732
  39.7 9.1 %copy-start.2 = (f32[16,1024]{1,0:T(8,128)S(1)}, f32[16,1024]{1,0:T(8,128)}, u32[]{:S(2)}) copy-start(f32[16,1024]{1,0:T(8,128)} %get-tuple-element.168.refs_4_.refs_1_.refs_5_) | copy-start | bytes 196612
  89.4 16.9 %copy-start.22 = (bf16[2,128,2048]{2,1,0:T(8,128)(2,1)S(1)}, bf16[2,128,2048]{2,1,0:T(8,128)(2,1)}, u32[]{:S(2)}) copy-start(bf16[2,128,2048]{2,1,0:T(8,128)(2,1)} %param.13) | copy-start | bytes 3145732
  89.4 19.2 %slice-start = ((s8[8388608]{0:T(1024)(128)(4,1)}), s8[4194304]{0:T(1024)(128)(4,1)S(1)}, s32[]{:S(2)}) async-start(s8[8388608]{0:T(1024)(128)(4,1)} %bitcast.284), calls=%async_computation.6 | async-start | bytes 8388608
  108.4 173.7 %copy-start.18 = (f32[256,2048]{1,0:T(8,128)}, f32[256,2048]{1,0:T(8,128)S(1)}, u32[]{:S(2)}) copy-start(f32[256,2048]{1,0:T(8,128)S(1)} %get-tuple-element.138) | copy-start | bytes 6291460
  114.1 9.1 %copy-start.66 = (bf16[2,1024,160]{1,2,0:T(8,128)(2,1)S(1)}, bf16[2,1024,160]{1,2,0:T(8,128)(2,1)}, u32[]{:S(2)}) copy-start(bf16[2,1024,160]{1,2,0:T(8,128)(2,1)} %param.20) | copy-start | bytes 1966084
  114.1 184.6 %all-gather.11.cloned.1.call-start = ((), (), s32[]{:S(2)}) async-start(), calls=%async_computation.2 | async-start | bytes 2621440 | tf_op jit(solution)/shard_map/all_gather | solution.py:1108
  115.5 6.7 %collective-permute-start.1 = (f32[2,3,1024]{2,1,0:T(4,128)S(1)}, f32[2,3,1024]{2,1,0:T(4,128)S(1)}, u32[]{:S(2)}, u32[]{:S(2)}) collective-permute-start(f32[2,3,1024]{2,1,0:T(4,128)S(1)} %slice.365), channel_id=1, source_target_pairs={{0,4},{4,8},{8,12},{12,16},{16,20},{20,24},{24,28},{1,5},{5,9},{9,... | collective-permute-start | bytes 73736 | tf_op jit(solution)/shard_map/ppermute | solution.py:1076
  123.2 9.5 %copy-start.41 = (f32[2,128,1024]{2,1,0:T(8,128)}, f32[2,128,1024]{2,1,0:T(8,128)S(1)}, u32[]{:S(2)}) copy-start(f32[2,128,1024]{2,1,0:T(8,128)S(1)} %get-tuple-element.136) | copy-start | bytes 3145732
  123.6 9.1 %copy-start.28 = (f32[256,2,1024]{2,0,1:T(8,128)S(1)}, f32[256,2,1024]{2,0,1:T(8,128)}, u32[]{:S(2)}) copy-start(f32[256,2,1024]{2,0,1:T(8,128)} %copy-done.27) | copy-start | bytes 6291460
  123.6 9.1 %copy-start.46 = (f32[256,1024]{1,0:T(8,128)S(1)}, f32[256,1024]{1,0:T(8,128)}, u32[]{:S(2)}) copy-start(f32[256,1024]{1,0:T(8,128)} %get-tuple-element.195) | copy-start | bytes 3145732
  178.3 36.9 %copy-start.77 = (f32[1,1024]{1,0:T(1,128)S(1)}, f32[1,1024]{1,0:T(1,128)}, u32[]{:S(2)}) copy-start(f32[1,1024]{1,0:T(1,128)} %get-tuple-element.179.refs_6_) | copy-start | bytes 12292
  218.4 114.1 %all-gather.13.cloned.1.call-start = ((), (), s32[]{:S(2)}) async-start(), calls=%async_computation.3 | async-start | bytes 2621440 | tf_op jit(solution)/shard_map/all_gather | solution.py:1108
  230.5 6.1 %collective-permute-start.2 = (f32[2,3,1024]{2,1,0:T(4,128)S(1)}, f32[2,3,1024]{2,1,0:T(4,128)S(1)}, u32[]{:S(2)}, u32[]{:S(2)}) collective-permute-start(f32[2,3,1024]{2,1,0:T(4,128)S(1)} %pad_add_fusion.3), channel_id=1, source_target_pairs={{4,0},{8,4},{12,8},{16,12},{20,16},{24,20},{28,24},{5,1},{9,5},{13... | collective-permute-start | bytes 73736 | tf_op jit(solution)/shard_map/ppermute | solution.py:1076
  237.6 156.6 %all-gather.17.cloned.1.call-start = ((), (), s32[]{:S(2)}) async-start(), calls=%async_computation.5 | async-start | bytes 2621440 | tf_op jit(solution)/shard_map/all_gather | solution.py:1108
  241.4 173.8 %all-gather.15.cloned.1.call-start = ((), (), s32[]{:S(2)}) async-start(), calls=%async_computation.4 | async-start | bytes 2621440 | tf_op jit(solution)/shard_map/all_gather | solution.py:1108
  336.7 38.1 %copy-start.54 = (bf16[2,128,1024]{2,1,0:T(8,128)(2,1)S(1)}, bf16[2,128,1024]{2,1,0:T(8,128)(2,1)}, u32[]{:S(2)}) copy-start(bf16[2,128,1024]{2,1,0:T(8,128)(2,1)} %param.21) | copy-start | bytes 1572868
  386.7 34.3 %collective-permute-start.3 = (f32[2,3,1024]{2,1,0:T(4,128)S(1)}, f32[2,3,1024]{2,1,0:T(4,128)S(1)}, u32[]{:S(2)}, u32[]{:S(2)}) collective-permute-start(f32[2,3,1024]{2,1,0:T(4,128)S(1)} %pad_add_fusion.2), channel_id=1, source_target_pairs={{4,0},{8,4},{12,8},{16,12},{20,16},{24,20},{28,24},{5,1},{9,5},{13... | collective-permute-start | bytes 73736 | tf_op jit(solution)/shard_map/ppermute | solution.py:1076
  (74 other events, 265.0 us)
Sparse Core Ops, SparseCore 0:
  12.4 51.0 all-gather.6
  114.2 52.2 all-gather.8
  218.5 46.1 all-gather.10
  266.1 43.9 all-gather.12
  311.4 55.6 all-gather.16
  368.6 46.6 all-gather.14

commit v7 on v6

--- a/solution.py
+++ b/solution.py
@@ -1222,8 +1222,8 @@
         grad_skip = jnp.sum(grad_scan * activated, axis=0)
         if last:
             plan = [
-                (ColumnsLine, (3, 5), normed),
-                (ColumnsLine, (4, 6), out_low),
+                (ColumnsLine, (4, 6), normed),
+                (ColumnsLine, (5, 7), out_low),
                 (ColumnsLine, (6, 8), stored[0][2]),
             ]
         else:

time: 558 us -> 556 us (level)
  no operation moved by 1% of the time
where the time goes in v7:
time: 556 us; the launch traced here: 548 us
  Pallas kernels  331 us (60%)
  matrix products  71.5 us (13%)
  local copies, waits for them, and re-layouts  48.4 us (9%)
  other arithmetic  46.5 us (8%)
  waiting for transfers between devices  21.4 us (4%)
  between operations  16.6 us (3%)
  starting transfers between devices  12.4 us (2%)
    pallas_call x5, Pallas kernels, play_call(): pl.pallas_call(after(played(kernel, counts, kinds, places), len(arrays),...  100 us
    pallas_call x1, Pallas kernels, closing(): pl.pallas_call(functools.partial(closing_kernel, n, nseq, zs, ys, parts,...  91.5 us
    pallas_call x3, Pallas kernels, carry_over(): pl.pallas_call(functools.partial(carry_kernel, n, int(fwd), int(rev), len...  61.8 us
    dot_general x23, matrix products, dot(): lax.dot_general(a, b, ((contract[:1], contract[1:]), ((), ())), preferred...  52.3 us
    pallas_call x2, Pallas kernels, ch_reduce(): pl.pallas_call(functools.partial(reduce_kernel, n, parts, gather), out_sh...  33.8 us
    unnamed x180, local copies, waits for them, and re-layouts  32.4 us
    pallas_call x4, Pallas kernels, ch_sum(): pl.pallas_call(after(functools.partial(ch_sum_kernel, n), 1, pins), out_s...  28.5 us
    pallas_call x2, Pallas kernels, scan_back_local(): pl.pallas_call(after(functools.partial(back_local_kernel, seqs), 5, pins)...  15.7 us
  transfers between devices with their start and end apart: 10, of which 4 were waited for; matrix products, arithmetic and copies ran while one was open for 17% of the time, Pallas kernels for 39%

profile of v7, /device:TPU:10, one launch (start us, length us, event | category | flops | bytes accessed | tf_op | source)
XLA Modules:
  0.0 548.3 jit_solution(12014734232840590754)
XLA Ops:
  7.2 5.0 fusion.143
  30.2 6.8 %ch_sum.4 = f32[256,160]{1,0:T(8,128)S(1)} custom-call(f32[256,160]{1,0:T(8,128)S(1)} %fusion.93.refs_0_), custom_call_target="tpu_custom_call" | custom-call | flops 1000000000 | tf_op jit(solution)/shard_map/ch_sum/pallas_call | solution.py:434
  40.9 7.9 %scan_local.2 = (f32[2,16,1024]{2,1,0:T(8,128)}, f32[2,1024]{1,0:T(2,128)}) custom-call(f32[256,1024]{1,0:T(8,128)} %convolution_add_fusion.3.refs_0_, f32[256,1024]{1,0:T(8,128)} %bitcast_multiply_fusion.5.refs_1_, f32[256,32]{1,0:T(8,128)} %slice.295.refs_2_.refs_3_, f32[256,1]{1,0:T(8,128)} %copy.64.refs_3_.refs_4_, ...), custom_call_target="tpu_custom_call" | custom-call | flops 800000000 | tf_op jit(solution)/shard_map/scan_local/pallas_call | solution.py:150
  50.4 18.1 %carry_over.3 = (f32[2,16,1024]{2,1,0:T(8,128)S(1)}, bf16[2048,2,1024]{2,1,0:T(2,128)(2,1)S(1)}) custom-call(f32[2,1024]{1,0:T(2,128)S(1)} %copy-done.9, f32[16,1024]{1,0:T(8,128)S(1)} %copy-done.2, f32[2,16,1024]{2,1,0:T(8,128)S(1)} %copy-done.7, bf16[2,2048,2,1024]{3,2,1,0:T(2,128)(2,1)} %refs_4_.1), custom_call_target="tpu_custom_call" | custom-call | flops 1900000000 | tf_op jit(solution)/shard_map/carry_over/pallas_call | solution.py:691
  72.6 11.0 %scan_forward.1 = f32[256,1024]{1,0:T(8,128)} custom-call(f32[256,1024]{1,0:T(8,128)} %convolution_add_fusion.3.refs_0_, f32[256,1024]{1,0:T(8,128)} %bitcast_multiply_fusion.5.refs_1_, f32[256,32]{1,0:T(8,128)} %slice.295.refs_2_.refs_3_, f32[256,1]{1,0:T(8,128)} %copy.64.refs_3_.refs_4_, f32[16,1024]{1,0:T(8,128)} %get-tuple-element.168.refs_4_.refs_1_.refs_5_, ...), custom_call_target="tpu_custom_call" | custom-call | flops 1100000000 | tf_op jit(solution)/shard_map/scan_forward/pallas_call | solution.py:150
  89.4 16.9 %ch_reduce.2 = f32[256,2048]{1,0:T(8,128)S(1)} custom-call(bf16[256,2048]{1,0:T(8,128)(2,1)S(1)} %fusion.37.refs_0_), custom_call_target="tpu_custom_call" | custom-call | flops 1800000000 | tf_op jit(solution)/shard_map/ch_reduce/pallas_call | solution.py:615
  123.6 7.1 %ch_sum.5 = f32[256,160]{1,0:T(8,128)S(1)} custom-call(f32[256,160]{1,0:T(8,128)S(1)} %fusion.90.refs_0_), custom_call_target="tpu_custom_call" | custom-call | flops 1000000000 | tf_op jit(solution)/shard_map/ch_sum/pallas_call | solution.py:434
  134.9 7.9 %scan_local.3 = (f32[2,16,1024]{2,1,0:T(8,128)}, f32[2,1024]{1,0:T(2,128)}) custom-call(f32[256,1024]{1,0:T(8,128)} %convolution_add_fusion.2.refs_0_, f32[256,1024]{1,0:T(8,128)} %get-tuple-element.163.refs_1_, f32[256,32]{1,0:T(8,128)} %slice.317.refs_2_.refs_3_, f32[256,1]{1,0:T(8,128)} %copy.64.refs_3_.refs_4_, ...), custom_call_target="tpu_custom_call" | custom-call | flops 800000000 | tf_op jit(solution)/shard_map/scan_local/pallas_call | solution.py:150
  142.8 7.8 %scan_back_local.2.refs_3_ = f32[2,16,1024]{2,1,0:T(8,128)} custom-call(f32[256,1024]{1,0:T(8,128)} %convolution_add_fusion.2.refs_0_, f32[256,1024]{1,0:T(8,128)} %get-tuple-element.128.refs_1_.refs_2_, f32[256,32]{1,0:T(8,128)} %slice.317.refs_2_.refs_3_, f32[256,1]{1,0:T(8,128)} %copy.64.refs_3_.refs_4_, f32[16,1024]{1,0:T(8,128)} %get-tuple-element.167.refs_4_.refs_1_.refs_5_), custom_call_target="tpu_custom_call" | custom-call | flops 800000000 | tf_op jit(solution)/shard_map/scan_back_local/pallas_call | solution.py:253
  151.4 22.2 %carry_over.4 = (f32[2,16,1024]{2,1,0:T(8,128)S(1)}, f32[2,16,1024]{2,1,0:T(8,128)S(1)}, bf16[2048,2,1024]{2,1,0:T(2,128)(2,1)S(1)}) custom-call(f32[2,1024]{1,0:T(2,128)S(1)} %copy-done.11, f32[16,1024]{1,0:T(8,128)S(1)} %copy-done.4, f32[2,16,1024]{2,1,0:T(8,128)S(1)} %copy-done.5, f32[2,16,1024]{2,1,0:T(8,128)S(1)} %copy-done.6, ...), custom_call_target="tpu_custom_call" | custom-call | flops 1900000000 | tf_op jit(solution)/shard_map/carry_over/pallas_call | solution.py:691
  178.3 35.4 %scan_back.2 = (f32[256,1024]{1,0:T(8,128)}, f32[256,1024]{1,0:T(8,128)}, f32[256,128]{1,0:T(8,128)}, f32[16,1024]{1,0:T(8,128)}, f32[256,1024]{1,0:T(8,128)}, /...) custom-call(f32[256,1024]{1,0:T(8,128)} %convolution_add_fusion.2.refs_0_, ...), custom_call_target="tpu_custom_call" | custom-call | flops 2600000000 | tf_op jit(solution)/shard_map/scan_back/pallas_call | solution.py:150
  220.1 7.6 %ch_sum.6 = f32[256,160]{1,0:T(8,128)S(1)} custom-call(f32[256,160]{1,0:T(8,128)S(1)} %pad_maximum_fusion.8.refs_0_, bf16[1024,1024]{1,0:T(8,128)(2,1)S(1)} %copy-done), custom_call_target="tpu_custom_call" | custom-call | flops 1000000000 | tf_op jit(solution)/shard_map/ch_sum/pallas_call | solution.py:434
  255.2 6.6 %fusion.40.refs_0_ = bf16[256,2048]{1,0:T(8,128)(2,1)S(1)} fusion(bf16[2048,2,1024]{2,1,0:T(2,128)(2,1)} %copy-done.13, bf16[256,1,1024]{2,0,1:T(8,128)(2,1)} %fusion.88, bf16[256,1,1024]{2,0,1:T(8,128)(2,1)} %bitcast.296), kind=kOutput, calls=%fused_computation.38 | convolution fusion | flops 2148532224 | bytes 10485760 | tf_op jit(solution)/shard_map/dot_general | solution.py:1266
  261.8 16.9 %ch_reduce.3 = f32[256,2048]{1,0:T(8,128)S(1)} custom-call(bf16[256,2048]{1,0:T(8,128)(2,1)S(1)} %fusion.40.refs_0_), custom_call_target="tpu_custom_call" | custom-call | flops 1800000000 | tf_op jit(solution)/shard_map/ch_reduce/pallas_call | solution.py:615
  283.6 5.8 %multiply_reduce_fusion.9 = (f32[1024]{0:T(1024)S(1)}, f32[256,1024]{1,0:T(8,128)}, bf16[256,1024]{1,0:T(8,128)(2,1)}, f32[256,1024]{1,0:T(8,128)}) fusion(f32[2,128,1024]{2,1,0:T(8,128)S(1)} %copy-done.40, f32[256,2,1024]{2,0,1:T(8,128)S(1)} %copy-done.44, f32[256,1024]{1,0:T(8,128)S(1)} %copy-done.49, f32[1024]{0:T(1024)S(1)} %bitcast.353, ...), kind=kOutput, calls=%fused_computation.125 | convolution fusion | flops 1080032256 | bytes 11018240 | tf_op jit(solution)/shard_map/dot_general | solution.py:1100
  289.3 7.9 %scan_back_local.3.refs_2_ = f32[2,16,1024]{2,1,0:T(8,128)} custom-call(f32[256,1024]{1,0:T(8,128)} %convolution_add_fusion.3.refs_0_, f32[256,1024]{1,0:T(8,128)} %get-tuple-element.130.refs_1_.refs_2_, f32[256,32]{1,0:T(8,128)} %slice.295.refs_2_.refs_3_, f32[256,1]{1,0:T(8,128)} %copy.64.refs_3_.refs_4_, f32[16,1024]{1,0:T(8,128)} %get-tuple-element.168.refs_4_.refs_1_.refs_5_), custom_call_target="tpu_custom_call" | custom-call | flops 800000000 | tf_op jit(solution)/shard_map/scan_back_local/pallas_call | solution.py:253
  302.9 21.4 %carry_over.5 = (f32[2,16,1024]{2,1,0:T(8,128)S(1)}, f32[1024,256]{1,0:T(8,128)S(1)}) custom-call(f32[2,1024]{1,0:T(2,128)S(1)} %copy-done.10, f32[16,1024]{1,0:T(8,128)S(1)} %copy-done.3, f32[2,16,1024]{2,1,0:T(8,128)S(1)} %copy-done.16, bf16[2,1024,256]{2,1,0:T(8,128)(2,1)S(1)} %pad_maximum_fusion.5.refs_3_), custom_call_target="tpu_custom_call" | custom-call | flops 1900000000 | tf_op jit(solution)/shard_map/carry_over/pallas_call | solution.py:691
  325.0 6.1 %fusion.45 = bf16[512,1024]{1,0:T(8,128)(2,1)} fusion(bf16[1024,512]{1,0:T(8,128)(2,1)} %get-tuple-element.59, bf16[1024,1024]{1,0:T(8,128)(2,1)S(1)} %copy-done.1, bf16[1024,1024]{1,0:T(8,128)(2,1)} %all-gather.7.cloned.1.call-done.refs_6_, bf16[1024,1024]{1,0:T(8,128)(2,1)} %all-gather.11.cloned.1.call-done, f32[]{:T(128)} %bitcast.45), kind=kOutput, calls=%fused_computation.56 | convolution fusion | flops 1088946176 | bytes 8388612 | tf_op jit(solution)/shard_map/dot_general | solution.py:1100
  335.2 38.0 %scan_back.3 = (f32[256,1024]{1,0:T(8,128)}, f32[256,1024]{1,0:T(8,128)}, f32[256,128]{1,0:T(8,128)}, f32[16,1024]{1,0:T(8,128)}, bf16[1024,512]{1,0:T(8,128)(2,...) custom-call(f32[256,1024]{1,0:T(8,128)} %convolution_add_fusion.3.refs_0_, f32[256,1024]{1,0:T(8,128)} %bitcast_multiply_fusion.5.refs_1_, ...), custom_call_target="tpu_custom_call" | custom-call | flops 2300000000 | tf_op jit(solution)/shard_map/scan_back/pallas_call | solution.py:150
  375.9 7.0 %ch_sum.7 = f32[256,160]{1,0:T(8,128)S(1)} custom-call(f32[256,160]{1,0:T(8,128)S(1)} %pad_maximum_fusion.9.refs_0_), custom_call_target="tpu_custom_call" | custom-call | flops 1000000000 | tf_op jit(solution)/shard_map/ch_sum/pallas_call | solution.py:434
  400.0 12.8 %all-gather.15.cloned.1.call-done = bf16[1024,1024]{1,0:T(8,128)(2,1)} async-done(((bf16[256,1024]{1,0:T(8,128)(2,1)}), bf16[1024,1024]{1,0:T(8,128)(2,1)}) %all-gather.15.cloned.1.call-update) | async-done | bytes 2097168 | tf_op jit(solution)/shard_map/all_gather | solution.py:1108
  420.2 6.6 %fusion.137 = (bf16[256,2048]{1,0:T(8,128)(2,1)S(1)}, f32[256]{0:T(256)S(1)}) fusion(bf16[2,128,2048]{2,1,0:T(8,128)(2,1)S(1)} %copy-done.23, f32[2048]{0:T(1024)S(1)} %bitcast.323, bf16[2048,2,1024]{2,1,0:T(2,128)(2,1)} %copy-done.12, bf16[256,1,1024]{2,0,1:T(8,128)(2,1)S(1)} %bitcast.309, bf16[256,1,1024]{2,0,1:T(8,128)(2,1)S(1)} %bitcast.310), kind=kOutput, calls=%fused_computation.265 | convolution fusion | flops 2150629120 | bytes 11543552 | tf_op jit(solution)/shard_map/dot_general | solution.py:1266
  429.8 91.5 %closing.1 = (f32[256,640]{1,0:T(8,128)}, f32[256,512]{1,0:T(8,128)}, bf16[640,1024]{1,0:T(8,128)(2,1)}, f32[256,1024]{1,0:T(8,128)}, f32[16,512]{1,0:T(8,128)},...) custom-call(bf16[256,2560]{1,0:T(8,128)(2,1)} %bitcast.297, bf16[256,2048]{1,0:T(8,128)(2,1)} %fusion.34.b_ref, ...), custom_call_target="tpu_custom_call" | custom-call | flops 7000000000 | tf_op jit(solution)/shard_map/closing/pallas_call | solution.py:1041
  527.2 5.3 copy.78
  (327 shorter events, 152.1 us)
Async XLA Ops:
  7.2 65.4 %all-gather.7.cloned.1.call-start = ((), (), s32[]{:S(2)}) async-start(), calls=%async_computation | async-start | bytes 2621440 | tf_op jit(solution)/shard_map/all_gather | solution.py:1108
  12.3 206.2 %all-gather.9.cloned.1.call-start = ((), (), s32[]{:S(2)}) async-start(), calls=%async_computation.1 | async-start | bytes 2621440 | tf_op jit(solution)/shard_map/all_gather | solution.py:1108
  21.0 8.8 %copy-start.31 = (f32[256,1,1024]{2,0,1:T(8,128)}, f32[256,1,1024]{2,0,1:T(8,128)S(1)}, u32[]{:S(2)}) copy-start(f32[256,1,1024]{2,0,1:T(8,128)S(1)} %slice.350) | copy-start | bytes 3145732
  21.0 8.8 %copy-start.65 = (bf16[2,1024,160]{1,2,0:T(8,128)(2,1)S(1)}, bf16[2,1024,160]{1,2,0:T(8,128)(2,1)}, u32[]{:S(2)}) copy-start(bf16[2,1024,160]{1,2,0:T(8,128)(2,1)} %param.20) | copy-start | bytes 1966084
  21.3 7.3 %collective-permute-start = (f32[2,3,1152]{2,0,1:T(2,128)S(1)}, f32[2,3,1152]{2,0,1:T(2,128)S(1)}, u32[]{:S(2)}, u32[]{:S(2)}) collective-permute-start(f32[2,3,1152]{2,0,1:T(2,128)S(1)} %pad_maximum_fusion.11), channel_id=1, source_target_pairs={{0,4},{4,8},{8,12},{12,16},{16,20},{20,24},{24,28},{1,5},{5,9},{9,... | collective-permute-start | bytes 82952 | tf_op jit(solution)/shard_map/ppermute | solution.py:1076
  25.5 257.1 %copy-start.76 = (f32[1,1024]{1,0:T(1,128)}, f32[1,1024]{1,0:T(1,128)S(1)}, u32[]{:S(2)}) copy-start(f32[1,1024]{1,0:T(1,128)S(1)} %get-tuple-element.180.refs_6_) | copy-start | bytes 12292
  29.8 53.8 %copy-start.39 = (f32[2,128,1024]{2,1,0:T(8,128)}, f32[2,128,1024]{2,1,0:T(8,128)S(1)}, u32[]{:S(2)}) copy-start(f32[2,128,1024]{2,1,0:T(8,128)S(1)} %get-tuple-element.140) | copy-start | bytes 3145732
  39.7 9.1 %copy-start.2 = (f32[16,1024]{1,0:T(8,128)S(1)}, f32[16,1024]{1,0:T(8,128)}, u32[]{:S(2)}) copy-start(f32[16,1024]{1,0:T(8,128)} %get-tuple-element.168.refs_4_.refs_1_.refs_5_) | copy-start | bytes 196612
  89.4 16.9 %copy-start.22 = (bf16[2,128,2048]{2,1,0:T(8,128)(2,1)S(1)}, bf16[2,128,2048]{2,1,0:T(8,128)(2,1)}, u32[]{:S(2)}) copy-start(bf16[2,128,2048]{2,1,0:T(8,128)(2,1)} %param.13) | copy-start | bytes 3145732
  89.4 19.2 %slice-start = ((s8[8388608]{0:T(1024)(128)(4,1)}), s8[4194304]{0:T(1024)(128)(4,1)S(1)}, s32[]{:S(2)}) async-start(s8[8388608]{0:T(1024)(128)(4,1)} %bitcast.284), calls=%async_computation.6 | async-start | bytes 8388608
  108.4 172.2 %copy-start.18 = (f32[256,2048]{1,0:T(8,128)}, f32[256,2048]{1,0:T(8,128)S(1)}, u32[]{:S(2)}) copy-start(f32[256,2048]{1,0:T(8,128)S(1)} %get-tuple-element.138) | copy-start | bytes 6291460
  114.1 9.1 %copy-start.66 = (bf16[2,1024,160]{1,2,0:T(8,128)(2,1)S(1)}, bf16[2,1024,160]{1,2,0:T(8,128)(2,1)}, u32[]{:S(2)}) copy-start(bf16[2,1024,160]{1,2,0:T(8,128)(2,1)} %param.20) | copy-start | bytes 1966084
  114.1 183.1 %all-gather.11.cloned.1.call-start = ((), (), s32[]{:S(2)}) async-start(), calls=%async_computation.2 | async-start | bytes 2621440 | tf_op jit(solution)/shard_map/all_gather | solution.py:1108
  115.5 6.7 %collective-permute-start.1 = (f32[2,3,1024]{2,1,0:T(4,128)S(1)}, f32[2,3,1024]{2,1,0:T(4,128)S(1)}, u32[]{:S(2)}, u32[]{:S(2)}) collective-permute-start(f32[2,3,1024]{2,1,0:T(4,128)S(1)} %slice.365), channel_id=1, source_target_pairs={{0,4},{4,8},{8,12},{12,16},{16,20},{20,24},{24,28},{1,5},{5,9},{9,... | collective-permute-start | bytes 73736 | tf_op jit(solution)/shard_map/ppermute | solution.py:1076
  123.2 9.5 %copy-start.41 = (f32[2,128,1024]{2,1,0:T(8,128)}, f32[2,128,1024]{2,1,0:T(8,128)S(1)}, u32[]{:S(2)}) copy-start(f32[2,128,1024]{2,1,0:T(8,128)S(1)} %get-tuple-element.136) | copy-start | bytes 3145732
  123.6 9.1 %copy-start.28 = (f32[256,2,1024]{2,0,1:T(8,128)S(1)}, f32[256,2,1024]{2,0,1:T(8,128)}, u32[]{:S(2)}) copy-start(f32[256,2,1024]{2,0,1:T(8,128)} %copy-done.27) | copy-start | bytes 6291460
  123.6 9.1 %copy-start.46 = (f32[256,1024]{1,0:T(8,128)S(1)}, f32[256,1024]{1,0:T(8,128)}, u32[]{:S(2)}) copy-start(f32[256,1024]{1,0:T(8,128)} %get-tuple-element.195) | copy-start | bytes 3145732
  178.3 35.4 %copy-start.77 = (f32[1,1024]{1,0:T(1,128)S(1)}, f32[1,1024]{1,0:T(1,128)}, u32[]{:S(2)}) copy-start(f32[1,1024]{1,0:T(1,128)} %get-tuple-element.179.refs_6_) | copy-start | bytes 12292
  216.8 114.2 %all-gather.13.cloned.1.call-start = ((), (), s32[]{:S(2)}) async-start(), calls=%async_computation.3 | async-start | bytes 2621440 | tf_op jit(solution)/shard_map/all_gather | solution.py:1108
  229.0 6.1 %collective-permute-start.2 = (f32[2,3,1024]{2,1,0:T(4,128)S(1)}, f32[2,3,1024]{2,1,0:T(4,128)S(1)}, u32[]{:S(2)}, u32[]{:S(2)}) collective-permute-start(f32[2,3,1024]{2,1,0:T(4,128)S(1)} %pad_add_fusion.3), channel_id=1, source_target_pairs={{4,0},{8,4},{12,8},{16,12},{20,16},{24,20},{28,24},{5,1},{9,5},{13... | collective-permute-start | bytes 73736 | tf_op jit(solution)/shard_map/ppermute | solution.py:1076
  236.0 156.7 %all-gather.17.cloned.1.call-start = ((), (), s32[]{:S(2)}) async-start(), calls=%async_computation.5 | async-start | bytes 2621440 | tf_op jit(solution)/shard_map/all_gather | solution.py:1108
  239.9 173.0 %all-gather.15.cloned.1.call-start = ((), (), s32[]{:S(2)}) async-start(), calls=%async_computation.4 | async-start | bytes 2621440 | tf_op jit(solution)/shard_map/all_gather | solution.py:1108
  335.2 38.0 %copy-start.54 = (bf16[2,128,1024]{2,1,0:T(8,128)(2,1)S(1)}, bf16[2,128,1024]{2,1,0:T(8,128)(2,1)}, u32[]{:S(2)}) copy-start(bf16[2,128,1024]{2,1,0:T(8,128)(2,1)} %param.21) | copy-start | bytes 1572868
  385.3 33.3 %collective-permute-start.3 = (f32[2,3,1024]{2,1,0:T(4,128)S(1)}, f32[2,3,1024]{2,1,0:T(4,128)S(1)}, u32[]{:S(2)}, u32[]{:S(2)}) collective-permute-start(f32[2,3,1024]{2,1,0:T(4,128)S(1)} %pad_add_fusion.2), channel_id=1, source_target_pairs={{4,0},{8,4},{12,8},{16,12},{20,16},{24,20},{28,24},{5,1},{9,5},{13... | collective-permute-start | bytes 73736 | tf_op jit(solution)/shard_map/ppermute | solution.py:1076
  (74 other events, 265.7 us)
Sparse Core Ops, SparseCore 0:
  12.4 51.0 all-gather.6
  114.2 52.2 all-gather.8
  216.9 46.1 all-gather.10
  264.5 43.9 all-gather.12
  309.9 54.8 all-gather.16
  366.2 46.5 all-gather.14
